TPU v7x, 32 devices: a whole 2x2x4 slice. The times are simulated.
32 devices in a mesh: ctx: 8 (over y, x, core), fsdp: 4 (over z).
Axes of the slice: x: 2, y: 2, z: 4, core: 2. Of those that a mesh axis runs over, the one named last changes fastest.
Arguments:
- hidden_in: bfloat16 [4, 2048, 2048], P('fsdp', 'ctx'), may hold values from -6 to 6
- segment_ids: int32 [4, 2048], P('fsdp', 'ctx'), may hold values from 0 to 8, as said below
- positions: int32 [4, 2048], P('fsdp', 'ctx'), may hold values from 0 to 1151, as said below
- attn_gain: float32 [2048], replicated, may hold values from 0.5 to 1.5
- qkv_weight: bfloat16 [2048, 4096], P(('ctx', 'fsdp')), may hold values from -0.125 to 0.125
- query_norm_gain: float32 [128], replicated, may hold values from 1.2 to 1.8
- k_gain: float32 [128], replicated, may hold values from 1.2 to 1.8
- out_weight: bfloat16 [2048, 2048], P(('ctx', 'fsdp')), may hold values from -1 to 1
- mlp_gain: float32 [2048], replicated, may hold values from 0.5 to 1.5
- gate_up: bfloat16 [2048, 12288], P(('ctx', 'fsdp')), may hold values from -0.125 to 0.125
- down_weight: bfloat16 [6144, 2048], P(('ctx', 'fsdp')), may hold values from -0.078125 to 0.078125
- cotangent: bfloat16 [4, 2048, 2048], P('fsdp', 'ctx'), may hold values from -6 to 6
Outputs:
- hidden_out: bfloat16 [4, 2048, 2048], P('fsdp', 'ctx')
- d_hidden_in: float32 [4, 2048, 2048], P('fsdp', 'ctx')
- d_attn_gain: float32 [2048], replicated
- d_qkv_weight: float32 [2048, 4096], P(('ctx', 'fsdp'))
- d_q_gain: float32 [128], replicated
- d_k_gain: float32 [128], replicated
- d_out_weight: float32 [2048, 2048], P(('ctx', 'fsdp'))
- d_mlp_gain: float32 [2048], replicated
- d_gate_up: float32 [2048, 12288], P(('ctx', 'fsdp'))
- d_down_weight: float32 [6144, 2048], P(('ctx', 'fsdp'))
Inputs may be any that keep to these rules, and one draw needn't show every extreme that they name: `segment_ids`: in each group, segment 0 is a prompt of 1024 tokens and segments 1 to 8 are continuations of 128 tokens each; a segment's tokens lie in runs of 32 consecutive positions, the runs in an order where a group's first and last run belong to the prompt. `positions`: A prompt token's position is its place in the prompt; a continuation token's is 1024 plus its place in the continuation.
All inputs are finite; a program needn't handle non-finite values.
Results may differ from a plain program's by a relative error of at most 0.019.
Values may be sent and summed in bfloat16 or wider, within the bound.
A program may use at most 640 MiB of HBM per device.

v0:
```python
import jax
import jax.numpy as jnp
from jax import lax
from jax.sharding import PartitionSpec as P

QUERY_HEADS = 16
KEY_VALUE_HEADS = 8
HEAD_SIZE = 128
FF = 6144


EPS = 1e-06
ROPE_BASE = 1000000.0
MASK_FILL = -1e30


def norm_rows(values, gain):
    return values * lax.rsqrt(jnp.mean(values * values, axis=-1, keepdims=True) + EPS) * gain


def rotate_half(values, cosine, sine_table):
    middle = values.shape[-1] // 2
    first_half = values[..., :middle]
    second_half = values[..., middle:]
    return jnp.concatenate(
        [
            first_half * cosine - second_half * sine_table,
            second_half * cosine + first_half * sine_table,
        ],
        axis=-1,
    )


def rotary_tables(places):
    exponent = jnp.arange(HEAD_SIZE // 2, dtype=jnp.float32) * (2.0 / HEAD_SIZE)
    inverse = jnp.power(ROPE_BASE, -exponent)
    angles = places.astype(jnp.float32)[:, None] * inverse[None, :]
    return (jnp.cos(angles)[:, None, :], jnp.sin(angles)[:, None, :])


def body(
    hidden_in,
    segment_ids,
    positions,
    attn_gain,
    qkv_weight,
    query_norm_gain,
    k_gain,
    out_weight,
    mlp_gain,
    gate_up,
    down_weight,
    cotangent,
):
    hidden = hidden_in[0].astype(jnp.float32)
    count_of_tokens = hidden.shape[0]
    width = hidden.shape[1]
    segments = segment_ids[0]
    places = positions[0]
    query_total_width = QUERY_HEADS * HEAD_SIZE
    key_total_width = KEY_VALUE_HEADS * HEAD_SIZE
    joined_width = query_total_width + 2 * key_total_width
    repeat_factor = QUERY_HEADS // KEY_VALUE_HEADS
    score_scale = HEAD_SIZE ** (-0.5)
    cosine, sine_table = rotary_tables(places)

    def rotary_per_head(raw, gain):
        head_count = raw.shape[1] // HEAD_SIZE
        return rotate_half(
            norm_rows(raw.reshape(count_of_tokens, head_count, HEAD_SIZE), gain), cosine, sine_table
        )

    w_qkv, w_out, w_gu, w_down = (
        lax.all_gather(qkv_weight, ("ctx", "fsdp"), axis=0, tiled=True),
        lax.all_gather(out_weight, ("ctx", "fsdp"), axis=0, tiled=True),
        lax.all_gather(gate_up, ("ctx", "fsdp"), axis=0, tiled=True),
        lax.all_gather(down_weight, ("ctx", "fsdp"), axis=0, tiled=True),
    )
    normed = norm_rows(hidden, attn_gain).astype(jnp.bfloat16)
    merged_rows = jnp.dot(normed, w_qkv, preferred_element_type=jnp.float32)
    query_unnormed = merged_rows[:, :query_total_width]
    key_raw = merged_rows[:, query_total_width : query_total_width + key_total_width]
    value_raw = merged_rows[:, query_total_width + key_total_width :]
    query_tensor = (
        rotary_per_head(query_unnormed, query_norm_gain)
        .astype(jnp.bfloat16)
        .reshape(count_of_tokens, KEY_VALUE_HEADS, repeat_factor, HEAD_SIZE)
    )
    keys_rotated = rotary_per_head(key_raw, k_gain)
    kv_local = jnp.concatenate(
        [keys_rotated.reshape(count_of_tokens, key_total_width), value_raw], axis=1
    ).astype(jnp.bfloat16)
    kv_rows, seg_rows, place_rows = (
        lax.all_gather(kv_local, "ctx", axis=0, tiled=True),
        lax.all_gather(segments, "ctx", axis=0, tiled=True),
        lax.all_gather(places, "ctx", axis=0, tiled=True),
    )
    group_rows = kv_rows.shape[0]
    rows_per_block = min(512, group_rows)
    block_count = group_rows // rows_per_block

    def block_scores(block_index, row_table, row_segs, row_places):
        row_start = block_index * rows_per_block
        key_value_block = lax.dynamic_slice_in_dim(row_table, row_start, rows_per_block, 0)
        block_of_keys = key_value_block[:, :key_total_width].reshape(
            rows_per_block, KEY_VALUE_HEADS, HEAD_SIZE
        )
        block_of_values = key_value_block[:, key_total_width:].reshape(
            rows_per_block, KEY_VALUE_HEADS, HEAD_SIZE
        )
        key_segs = lax.dynamic_slice_in_dim(row_segs, row_start, rows_per_block, 0)
        key_places = lax.dynamic_slice_in_dim(row_places, row_start, rows_per_block, 0)
        scores = (
            jnp.einsum(
                "qgrd,kgd->grqk", query_tensor, block_of_keys, preferred_element_type=jnp.float32
            )
            * score_scale
        )
        visible = ((key_segs[None, :] == segments[:, None]) | (key_segs[None, :] == 0)) & (
            key_places[None, :] <= places[:, None]
        )
        return (jnp.where(visible, scores, MASK_FILL), block_of_keys, block_of_values)

    def running_total(block_index, running):
        row_top, row_sum = running
        scores, block_of_keys, block_of_values = block_scores(
            block_index, kv_rows, seg_rows, place_rows
        )
        new_top = jnp.maximum(row_top, jnp.max(scores, axis=-1))
        row_sum = row_sum * jnp.exp(row_top - new_top) + jnp.sum(
            jnp.exp(scores - new_top[..., None]), axis=-1
        )
        return (new_top, row_sum)

    initial_maximum = jnp.full(
        (KEY_VALUE_HEADS, repeat_factor, count_of_tokens), MASK_FILL, jnp.float32
    )
    initial_sum = jnp.zeros((KEY_VALUE_HEADS, repeat_factor, count_of_tokens), jnp.float32)
    row_top, row_sum = lax.fori_loop(0, block_count, running_total, (initial_maximum, initial_sum))
    log_total = row_top + jnp.log(row_sum)

    def weighted_sum(block_index, running):
        main_sum, extra_sum = running
        scores, block_of_keys, block_of_values = block_scores(
            block_index, kv_rows, seg_rows, place_rows
        )
        probability = jnp.exp(scores - log_total[..., None])
        rounded = probability.astype(jnp.bfloat16)
        leftover = (probability - rounded.astype(jnp.float32)).astype(jnp.bfloat16)
        main_sum = main_sum + jnp.einsum(
            "grqk,kgd->qgrd", rounded, block_of_values, preferred_element_type=jnp.float32
        )
        extra_sum = extra_sum + jnp.einsum(
            "grqk,kgd->qgrd", leftover, block_of_values, preferred_element_type=jnp.float32
        )
        return (main_sum, extra_sum)

    initial_output = jnp.zeros(
        (count_of_tokens, KEY_VALUE_HEADS, repeat_factor, HEAD_SIZE), jnp.float32
    )
    attended, extra_part = lax.fori_loop(
        0, block_count, weighted_sum, (initial_output, initial_output)
    )
    mixed_low = attended.reshape(count_of_tokens, query_total_width).astype(jnp.bfloat16)
    attended_full = attended + extra_part
    middle = hidden + jnp.dot(mixed_low, w_out, preferred_element_type=jnp.float32)
    second = norm_rows(middle, mlp_gain).astype(jnp.bfloat16)
    gate_rows = jnp.dot(second, w_gu, preferred_element_type=jnp.float32)
    gate_part = gate_rows[:, :FF]
    uppers = gate_rows[:, FF:]
    activated = (gate_part * jax.nn.sigmoid(gate_part) * uppers).astype(jnp.bfloat16)
    output = middle + jnp.dot(activated, w_down, preferred_element_type=jnp.float32)
    upstream = cotangent[0].astype(jnp.float32)
    held_inputs = lax.optimization_barrier(
        (qkv_weight, out_weight, gate_up, down_weight, kv_local, segments, places, output)
    )
    w_qkv, w_out, w_gu, w_down = (
        lax.all_gather(held_inputs[0], ("ctx", "fsdp"), axis=0, tiled=True),
        lax.all_gather(held_inputs[1], ("ctx", "fsdp"), axis=0, tiled=True),
        lax.all_gather(held_inputs[2], ("ctx", "fsdp"), axis=0, tiled=True),
        lax.all_gather(held_inputs[3], ("ctx", "fsdp"), axis=0, tiled=True),
    )
    back_rows, back_segs, back_places = (
        lax.all_gather(held_inputs[4], "ctx", axis=0, tiled=True),
        lax.all_gather(held_inputs[5], "ctx", axis=0, tiled=True),
        lax.all_gather(held_inputs[6], "ctx", axis=0, tiled=True),
    )
    upstream_low = upstream.astype(jnp.bfloat16)
    act_grad = (
        jnp.dot(upstream_low, w_down.T, preferred_element_type=jnp.float32)
        .astype(jnp.bfloat16)
        .astype(jnp.float32)
    )
    _, act_pull = jax.vjp(
        lambda gate_in, up_in: gate_in * jax.nn.sigmoid(gate_in) * up_in, gate_part, uppers
    )
    gate_grad, up_grad = act_pull(act_grad)
    joined_up_grad = jnp.concatenate([gate_grad, up_grad], axis=1).astype(jnp.bfloat16)
    second_grad = jnp.dot(joined_up_grad, w_gu.T, preferred_element_type=jnp.float32)
    _, mlp_pull = jax.vjp(norm_rows, middle, mlp_gain)
    middle_norm_grad, mlp_gain_grad = mlp_pull(second_grad)
    middle_grad = upstream + middle_norm_grad
    middle_low = middle_grad.astype(jnp.bfloat16)
    mixed_grad = (
        jnp.dot(middle_low, w_out.T, preferred_element_type=jnp.float32)
        .astype(jnp.bfloat16)
        .reshape(count_of_tokens, KEY_VALUE_HEADS, repeat_factor, HEAD_SIZE)
    )
    row_delta = jnp.transpose(
        jnp.sum(mixed_grad.astype(jnp.float32) * attended_full, axis=-1), (1, 2, 0)
    )

    def block_gradients(query_acc, block_index):
        scores, block_of_keys, block_of_values = block_scores(
            block_index, back_rows, back_segs, back_places
        )
        probability = jnp.exp(scores - log_total[..., None])
        rounded = probability.astype(jnp.bfloat16)
        prob_grad = jnp.einsum(
            "qgrd,kgd->grqk", mixed_grad, block_of_values, preferred_element_type=jnp.float32
        )
        value_grad = jnp.einsum(
            "grqk,qgrd->kgd", rounded, mixed_grad, preferred_element_type=jnp.float32
        )
        score_grad = (probability * (prob_grad - row_delta[..., None])).astype(jnp.bfloat16)
        query_acc = query_acc + jnp.einsum(
            "grqk,kgd->qgrd", score_grad, block_of_keys, preferred_element_type=jnp.float32
        )
        key_grad = (
            jnp.einsum(
                "grqk,qgrd->kgd", score_grad, query_tensor, preferred_element_type=jnp.float32
            )
            * score_scale
        )
        return (
            query_acc,
            jnp.concatenate(
                [
                    key_grad.reshape(rows_per_block, key_total_width),
                    value_grad.reshape(rows_per_block, key_total_width),
                ],
                axis=1,
            ),
        )

    query_sum, kv_terms = lax.scan(
        block_gradients,
        jnp.zeros((count_of_tokens, KEY_VALUE_HEADS, repeat_factor, HEAD_SIZE), jnp.float32),
        jnp.arange(block_count),
    )
    kv_grad = lax.psum_scatter(
        kv_terms.reshape(group_rows, 2 * key_total_width).astype(jnp.bfloat16),
        "ctx",
        scatter_dimension=0,
        tiled=True,
    ).astype(jnp.float32)
    key_grad = (
        kv_grad[:, :key_total_width]
        .astype(jnp.bfloat16)
        .astype(jnp.float32)
        .reshape(count_of_tokens, KEY_VALUE_HEADS, HEAD_SIZE)
    )
    value_grad = kv_grad[:, key_total_width:].astype(jnp.bfloat16).astype(jnp.float32)
    query_grad = (
        (query_sum * score_scale)
        .astype(jnp.bfloat16)
        .astype(jnp.float32)
        .reshape(count_of_tokens, QUERY_HEADS, HEAD_SIZE)
    )
    _, query_pull = jax.vjp(rotary_per_head, query_unnormed, query_norm_gain)
    query_raw_grad, q_gain_grad = query_pull(query_grad)
    _, key_pull = jax.vjp(rotary_per_head, key_raw, k_gain)
    key_raw_grad, k_gain_grad = key_pull(key_grad)
    joined_grad = jnp.concatenate([query_raw_grad, key_raw_grad, value_grad], axis=1).astype(
        jnp.bfloat16
    )
    normed_grad = jnp.dot(joined_grad, w_qkv.T, preferred_element_type=jnp.float32)
    _, attn_pull = jax.vjp(norm_rows, hidden, attn_gain)
    hidden_norm_grad, attn_gain_grad = attn_pull(normed_grad)
    input_grad = middle_grad + hidden_norm_grad
    input_weights = lax.psum_scatter(
        jnp.concatenate(
            [
                jnp.dot(normed.T, joined_grad, preferred_element_type=jnp.float32),
                jnp.dot(second.T, joined_up_grad, preferred_element_type=jnp.float32),
            ],
            axis=1,
        ),
        ("ctx", "fsdp"),
        scatter_dimension=0,
        tiled=True,
    )
    shards = lax.axis_size(("ctx", "fsdp"))
    out_term = jnp.dot(mixed_low.T, middle_low, preferred_element_type=jnp.float32).reshape(
        shards, -1, width
    )
    down_term = jnp.dot(activated.T, upstream_low, preferred_element_type=jnp.float32).reshape(
        shards, -1, width
    )
    output_weights = lax.psum_scatter(
        jnp.concatenate([out_term, down_term], axis=1).reshape(-1, width),
        ("ctx", "fsdp"),
        scatter_dimension=0,
        tiled=True,
    )
    out_rows = out_weight.shape[0]
    gain_grads = lax.psum(
        (attn_gain_grad, q_gain_grad, k_gain_grad, mlp_gain_grad), ("ctx", "fsdp")
    )
    return (
        output.astype(jnp.bfloat16)[None],
        input_grad[None],
        gain_grads[0],
        input_weights[:, :joined_width],
        gain_grads[1],
        gain_grads[2],
        output_weights[:out_rows],
        gain_grads[3],
        input_weights[:, joined_width:],
        output_weights[out_rows:],
    )


def solution(mesh):
    return jax.shard_map(
        body,
        mesh=mesh,
        in_specs=(
            P("fsdp", "ctx", None),
            P("fsdp", "ctx"),
            P("fsdp", "ctx"),
            P(),
            P(("ctx", "fsdp"), None),
            P(),
            P(),
            P(("ctx", "fsdp"), None),
            P(),
            P(("ctx", "fsdp"), None),
            P(("ctx", "fsdp"), None),
            P("fsdp", "ctx", None),
        ),
        out_specs=(
            P("fsdp", "ctx", None),
            P("fsdp", "ctx", None),
            P(),
            P(("ctx", "fsdp"), None),
            P(),
            P(),
            P(("ctx", "fsdp"), None),
            P(),
            P(("ctx", "fsdp"), None),
            P(("ctx", "fsdp"), None),
        ),
        check_vma=False,
    )
```

profile of v0, /device:TPU:0, one launch (start us, length us, event | category | flops | bytes accessed | tf_op | source)
XLA Modules:
  0.0 4892.7 jit_solution(6292613557794859762)
XLA Ops:
  11.3 117.3 %all-gather.15.cloned.1.call-done = bf16[2048,4096]{1,0:T(8,128)(2,1)} async-done(((bf16[64,4096]{1,0:T(8,128)(2,1)}), bf16[2048,4096]{1,0:T(8,128)(2,1)}) %all-gather.15.cloned.1.call-update) | async-done | bytes 16777232 | tf_op jit(solution)/shard_map/all_gather | solution.py:74
  172.0 23.1 all-gather.17.cloned.1.call-done
  207.5 20.8 while.45
  228.4 35.7 while.46
  281.8 270.8 %all-gather.21.cloned.1.call-done = bf16[2048,12288]{1,0:T(8,128)(2,1)} async-done(((bf16[64,12288]{1,0:T(8,128)(2,1)}), bf16[2048,12288]{1,0:T(8,128)(2,1)}) %all-gather.21.cloned.1.call-update) | async-done | bytes 50331664 | tf_op jit(solution)/shard_map/all_gather | solution.py:76
  552.7 25.4 fusion.72
  578.0 130.2 %all-gather.23.cloned.1.call-done = bf16[6144,2048]{1,0:T(8,128)(2,1)} async-done(((bf16[192,2048]{1,0:T(8,128)(2,1)}), bf16[6144,2048]{1,0:T(8,128)(2,1)}) %all-gather.23.cloned.1.call-update) | async-done | bytes 25165840 | tf_op jit(solution)/shard_map/all_gather | solution.py:77
  708.3 18.2 convolution_add_fusion
  745.5 133.9 %all-gather.25.cloned.1.call-done = bf16[6144,2048]{1,0:T(8,128)(2,1)} async-done(((bf16[192,2048]{1,0:T(8,128)(2,1)}), bf16[6144,2048]{1,0:T(8,128)(2,1)}) %all-gather.25.cloned.1.call-update) | async-done | bytes 25165840 | tf_op jit(solution)/shard_map/all_gather | solution.py:181
  879.4 20.7 fusion.37
  900.1 256.0 %all-gather.27.cloned.1.call-done = bf16[2048,12288]{1,0:T(8,128)(2,1)} async-done(((bf16[64,12288]{1,0:T(8,128)(2,1)}), bf16[2048,12288]{1,0:T(8,128)(2,1)}) %all-gather.27.cloned.1.call-update) | async-done | bytes 50331664 | tf_op jit(solution)/shard_map/all_gather | solution.py:180
  1156.1 23.9 multiply_reduce_fusion
  1183.1 51.5 %all-gather.31.cloned.1.call-done = bf16[2048,2048]{1,0:T(8,128)(2,1)} async-done(((bf16[64,2048]{1,0:T(8,128)(2,1)}), bf16[2048,2048]{1,0:T(8,128)(2,1)}) %all-gather.31.cloned.1.call-update) | async-done | bytes 8388624 | tf_op jit(solution)/shard_map/all_gather | solution.py:179
  1246.0 44.1 all-gather.29.cloned.1.call-done
  1290.1 104.3 %while.47 = (s32[]{:T(128)}, f32[256,8,2,128]{0,3,2,1:T(8,128)}, bf16[4,512,2048]{2,1,0:T(8,128)(2,1)}, s32[4]{0:T(128)S(1)}, bf16[2048,2048]{1,0:T(8,128)(2,1)}...) while((s32[]{:T(128)}, f32[256,8,2,128]{0,3,2,1:T(8,128)}, ...), condition=%wide.region_13.14_spmd.clone, body=%wide.region_12.13_spmd.clone.sunk | while | flops 2712142336 | bytes 85392736 | solution.py:246
  1396.0 42.5 fusion.39
  1474.5 13.6 fusion.57
  1488.1 88.3 %pad_maximum_fusion = f32[2048,16384]{1,0:T(8,128)} fusion(f32[2048,12288]{1,0:T(8,128)} %fusion.39, f32[2048,4096]{1,0:T(8,128)} %fusion.57), kind=kLoop, calls=%fused_computation.52 | loop fusion | flops 33554432 | bytes 268435456 | tf_op jit(solution)/shard_map/concatenate | solution.py:282
  1587.4 22.7 fusion.52
  1620.4 46.4 pad_maximum_fusion.1
  1668.1 12.8 fusion.44
  1680.9 40.4 all-reduce.5
  1724.8 1743.8 %all-reduce.8.cloned.1.call-done = f32[2048,16384]{1,0:T(8,128)} async-done(((f32[2048,16384]{1,0:T(8,128)}), f32[2048,16384]{1,0:T(8,128)}) %all-reduce.8.cloned.1.call-update) | async-done | bytes 134217744
  3475.3 1405.8 %reduce-scatter.5.cloned.1.call-done = f32[256,2048]{1,0:T(8,128)} async-done(((f32[8192,2048]{1,0:T(8,128)}), f32[256,2048]{1,0:T(8,128)}) %reduce-scatter.5.cloned.1.call-update) | async-done | bytes 2097168 | tf_op jit(solution)/shard_map/reduce_scatter | solution.py:300
  (378 shorter events, 342.3 us)
Async XLA Ops:
  7.2 121.4 %all-gather.15.cloned.1.call-start = ((), (), s32[]{:S(2)}) async-start(), calls=%async_computation.2 | async-start | bytes 17301504 | tf_op jit(solution)/shard_map/all_gather | solution.py:74
  7.9 187.3 %all-gather.17.cloned.1.call-start = ((), (), s32[]{:S(2)}) async-start(), calls=%async_computation.3 | async-start | bytes 9437184 | tf_op jit(solution)/shard_map/all_gather | solution.py:94
  10.7 126.4 %copy-start.45 = (f32[256]{0:T(256)}, f32[256]{0:T(256)S(1)}, u32[]{:S(2)}) copy-start(f32[256]{0:T(256)S(1)} %fusion.66) | copy-start | bytes 3076
  11.3 155.1 %copy-start.22 = (f32[256,64]{1,0:T(8,128)}, f32[256,64]{1,0:T(8,128)S(1)}, u32[]{:S(2)}) copy-start(f32[256,64]{1,0:T(8,128)S(1)} %get-tuple-element.790) | copy-start | bytes 196612
  11.3 155.1 %copy-start.24 = (f32[256,64]{1,0:T(8,128)}, f32[256,64]{1,0:T(8,128)S(1)}, u32[]{:S(2)}) copy-start(f32[256,64]{1,0:T(8,128)S(1)} %get-tuple-element.791) | copy-start | bytes 196612
  142.5 133.2 %all-gather.19.cloned.1.call-start = ((), (), s32[]{:S(2)}) async-start(), calls=%async_computation.4 | async-start | bytes 8650752 | tf_op jit(solution)/shard_map/all_gather | solution.py:75
  143.2 409.5 %all-gather.21.cloned.1.call-start = ((), (), s32[]{:S(2)}) async-start(), calls=%async_computation.5 | async-start | bytes 51904512 | tf_op jit(solution)/shard_map/all_gather | solution.py:76
  143.8 564.5 %all-gather.23.cloned.1.call-start = ((), (), s32[]{:S(2)}) async-start(), calls=%async_computation.6 | async-start | bytes 25952256 | tf_op jit(solution)/shard_map/all_gather | solution.py:77
  144.4 735.1 %all-gather.25.cloned.1.call-start = ((), (), s32[]{:S(2)}) async-start(), calls=%async_computation.7 | async-start | bytes 25952256 | tf_op jit(solution)/shard_map/all_gather | solution.py:181
  171.4 36.2 copy-start.2
  207.5 20.9 copy-start.16
  275.6 277.0 %copy-start.36 = (f32[2048]{0:T(1024)S(1)}, f32[2048]{0:T(1024)}, u32[]{:S(2)}) copy-start(f32[2048]{0:T(1024)} %param.26) | copy-start | bytes 24580
  281.8 874.3 %copy-start.11 = (f32[256,2048]{1,0:T(8,128)}, f32[256,2048]{1,0:T(8,128)S(1)}, u32[]{:S(2)}) copy-start(f32[256,2048]{1,0:T(8,128)S(1)} %get-tuple-element.793) | copy-start | bytes 6291460
  726.4 153.0 %copy-start.18 = (bf16[1,256,2048]{2,1,0:T(8,128)(2,1)S(1)}, bf16[1,256,2048]{2,1,0:T(8,128)(2,1)}, u32[]{:S(2)}) copy-start(bf16[1,256,2048]{2,1,0:T(8,128)(2,1)} %param.29) | copy-start | bytes 3145732
  726.5 429.6 %all-gather.27.cloned.1.call-start = ((), (), s32[]{:S(2)}) async-start(), calls=%async_computation.8 | async-start | bytes 51904512 | tf_op jit(solution)/shard_map/all_gather | solution.py:180
  727.2 507.4 %all-gather.31.cloned.1.call-start = ((), (), s32[]{:S(2)}) async-start(), calls=%async_computation.10 | async-start | bytes 8650752 | tf_op jit(solution)/shard_map/all_gather | solution.py:179
  728.0 562.1 %all-gather.29.cloned.1.call-start = ((), (), s32[]{:S(2)}) async-start(), calls=%async_computation.9 | async-start | bytes 9437184 | tf_op jit(solution)/shard_map/all_gather | solution.py:184
  728.7 737.1 %reduce-scatter.3.cloned.1.call-start = ((), (), s32[]{:S(2)}) async-start(), calls=%async_computation.11 | async-start | bytes 9437184 | tf_op jit(solution)/shard_map/reduce_scatter | solution.py:251
  1183.1 58.2 %copy-start.9 = (f32[256,2048]{1,0:T(8,128)}, f32[256,2048]{1,0:T(8,128)S(1)}, u32[]{:S(2)}) copy-start(f32[256,2048]{1,0:T(8,128)S(1)} %fusion.45) | copy-start | bytes 6291460
  1394.4 272.6 %all-gather.33.cloned.1.call-start = ((), (), s32[]{:S(2)}) async-start(), calls=%async_computation.12 | async-start | bytes 17301504 | tf_op jit(solution)/shard_map/all_gather | solution.py:178
  1395.1 2073.5 %all-reduce.8.cloned.1.call-start = ((), (), s32[]{:S(2)}) async-start(), calls=%async_computation.14 | async-start | bytes 268435456
  1576.4 3304.7 %reduce-scatter.5.cloned.1.call-start = ((), (), s32[]{:S(2)}) async-start(), calls=%async_computation.13 | async-start | bytes 69206016 | tf_op jit(solution)/shard_map/reduce_scatter | solution.py:300
  1666.9 54.4 %copy-start.49 = (f32[256]{0:T(256)S(1)}, f32[256]{0:T(256)}, u32[]{:S(2)}) copy-start(f32[256]{0:T(256)} %copy-done.48) | copy-start | bytes 3076
  1666.9 54.4 %copy-start.10 = (f32[256,2048]{1,0:T(8,128)S(1)}, f32[256,2048]{1,0:T(8,128)}, u32[]{:S(2)}) copy-start(f32[256,2048]{1,0:T(8,128)} %copy-done.9) | copy-start | bytes 6291460
  (61 other events, 197.3 us)
Sparse Core Ops, SparseCore 0:
  11.0 117.5 all-gather.14
  142.6 52.5 all-gather.16
  198.1 77.4 all-gather.18
  278.4 274.2 all-gather.20
  555.4 152.8 all-gather.22
  726.6 152.8 all-gather.24
  882.3 273.7 all-gather.26
  1159.0 75.5 all-gather.30
  1237.1 52.9 all-gather.28
  1394.5 71.2 reduce-scatter.2
  1469.2 114.8 all-gather.32
  1591.6 1876.9 all-reduce.7
  3471.1 1409.9 reduce-scatter.4
where the time goes:
time: 4900 us; the launch traced here: 4890 us
  waiting for transfers between devices  4200 us (86%)
  matrix products  305 us (6%)
  other arithmetic  197 us (4%)
  local copies, waits for them, and re-layouts  95.9 us (2%)
  blocking collectives  74 us (2%)
    unnamed x14, waiting for transfers between devices  1750 us
    reduce_scatter x1, waiting for transfers between devices, body(): lax.psum_scatter(jnp.concatenate([out_term, down_term], axis=1).reshape(-...  1410 us
    all_gather x1, waiting for transfers between devices, body(): lax.all_gather(gate_up, ('ctx', 'fsdp'), axis=0, tiled=True)  271 us
    all_gather x1, waiting for transfers between devices, body(): lax.all_gather(held_inputs[2], ('ctx', 'fsdp'), axis=0, tiled=True)  256 us
    all_gather x1, waiting for transfers between devices, body(): lax.all_gather(held_inputs[3], ('ctx', 'fsdp'), axis=0, tiled=True)  134 us
    all_gather x1, waiting for transfers between devices, body(): lax.all_gather(down_weight, ('ctx', 'fsdp'), axis=0, tiled=True)  130 us
    all_gather x1, waiting for transfers between devices, body(): lax.all_gather(qkv_weight, ('ctx', 'fsdp'), axis=0, tiled=True)  117 us
  transfers between devices with their start and end apart: 13, of which 12 were waited for; matrix products, arithmetic and copies ran while one was open for 9% of the time, Pallas kernels for 0%

commit v1 on v0

v1 whole, which is shorter than its diff:
```python
import functools
import math

import jax
import jax.numpy as jnp
from jax import lax
from jax.experimental import pallas as pl
from jax.experimental.pallas import tpu as pltpu
from jax.sharding import PartitionSpec as P

QUERY_HEADS = 16
KEY_VALUE_HEADS = 8
HEAD = 128
FF = 6144
PROMPT = 1024
CONT = 128
RUN = 32
EPS = 1e-06
ROPE_BASE = 1000000.0
SCALE = HEAD ** (-0.5)
SCALE2 = SCALE * math.log2(math.e)
MESH = pl.DeviceIdType.MESH
ANY = pl.BlockSpec(memory_space=pl.ANY)
VMEM = pl.BlockSpec(memory_space=pltpu.VMEM)
SMEM = pl.BlockSpec(memory_space=pltpu.SMEM)
BF16 = jnp.bfloat16
F32 = jnp.float32
DMA = pltpu.SemaphoreType.DMA
VMEM_LIMIT = 60 * 2**20


def cost(us, flops=0):
    return pl.CostEstimate(flops=flops, bytes_accessed=int(us * 3.2e6), transcendentals=0)


def flip(me, mask):
    result = me
    bit = 1
    while bit <= mask:
        if mask & bit:
            result = result + bit - 2 * bit * lax.rem(lax.div(me, bit), 2)
        bit *= 2
    return result


def bits_of(count):
    bits = []
    bit = 1
    while bit < count:
        bits.append(bit)
        bit *= 2
    return bits


def greet(peers):
    barrier = pltpu.get_barrier_semaphore()
    for peer in peers:
        pl.semaphore_signal(barrier, inc=1, device_id=peer, device_id_type=MESH)
    pl.semaphore_wait(barrier, len(peers))


def gather_orders(count):
    chip_bits = bits_of(count)[1:]
    return [chip_bits + [1], chip_bits[::-1] + [1]]


def last_bit(order, slot):
    return [bit for bit in order if slot & bit][-1]


def gather_rows(count, me, group, source, target, send, recv):
    rows = source.shape[0]
    half = rows // 2
    orders = gather_orders(count)

    def copy(part, slot, bit):
        start = pl.multiple_of(flip(me, slot) * rows + part * half, half)
        place = target.at[pl.ds(start, half)]
        origin = source.at[pl.ds(part * half, half)] if slot == 0 else place
        number = part * count + (slot ^ bit)
        return pltpu.make_async_remote_copy(
            origin,
            place,
            send.at[number],
            recv.at[number],
            device_id=(flip(me, bit), group),
            device_id_type=MESH,
        )

    own = pltpu.make_async_copy(
        source, target.at[pl.ds(pl.multiple_of(me * rows, rows), rows)], send.at[0]
    )
    own.start()
    copies = []
    for step in range(len(orders[0])):
        for part in (0, 1):
            item = copy(part, 0, orders[part][step])
            item.start()
            copies.append(item)

    def arrived(part, slot):
        start = pl.multiple_of(flip(me, slot) * rows + part * half, half)
        place = target.at[pl.ds(start, half)]
        number = part * count + slot
        pltpu.make_async_remote_copy(
            place,
            place,
            send.at[number],
            recv.at[number],
            device_id=(flip(me, last_bit(orders[part], slot)), group),
            device_id_type=MESH,
        ).wait_recv()

    def finish():
        waits = []
        for part in (0, 1):
            order = orders[part]
            for slot in range(1, count):
                last = order.index(last_bit(order, slot))
                waits.append((last, bin(slot).count("1"), part, slot))
        for last, _, part, slot in sorted(waits):
            arrived(part, slot)
            for bit in orders[part][last + 1 :]:
                item = copy(part, slot, bit)
                item.start()
                copies.append(item)
        own.wait()
        for item in copies:
            item.wait_send()

    return finish


def gather_kernel(count, source, target, send, recv):
    me = lax.axis_index("ctx")
    group = lax.axis_index("fsdp")
    greet([(flip(me, bit), group) for bit in bits_of(count)])
    gather_rows(count, me, group, source, target, send, recv)()


def gather_ctx(count, collective, values):
    rows, width = values.shape
    return pl.pallas_call(
        functools.partial(gather_kernel, count),
        out_shape=jax.ShapeDtypeStruct((count * rows, width), values.dtype),
        in_specs=[ANY],
        out_specs=ANY,
        scratch_shapes=[DMA((2 * count,)), DMA((2 * count,))],
        compiler_params=pltpu.CompilerParams(collective_id=collective, has_side_effects=True),
        cost_estimate=cost(42),
    )(values)


def trade(count, me, group, pieces, source, target, send, recv):
    copies = []
    local = []
    for slot in list(range(1, count)) + [0]:
        peer = flip(me, slot)
        for number, (origin, place) in enumerate(pieces(peer, me)):
            total = len(pieces(peer, me))
            index = slot * total + number
            if slot == 0:
                item = pltpu.make_async_copy(source.at[origin], target.at[place], send.at[index])
                local.append(item)
            else:
                item = pltpu.make_async_remote_copy(
                    source.at[origin],
                    target.at[place],
                    send.at[index],
                    recv.at[index],
                    device_id=(peer, group),
                    device_id_type=MESH,
                )
                copies.append(item)
            item.start()

    def finish():
        for item in local:
            item.wait()
        for slot in range(1, count):
            peer = flip(me, slot)
            listed = pieces(me, peer)
            for number, (origin, place) in enumerate(listed):
                index = slot * len(listed) + number
                pltpu.make_async_remote_copy(
                    source.at[origin],
                    target.at[place],
                    send.at[index],
                    recv.at[index],
                    device_id=(peer, group),
                    device_id_type=MESH,
                ).wait_recv()
        for item in copies:
            item.wait_send()

    return finish


def span(start, width):
    return pl.ds(pl.multiple_of(start, HEAD), width)


def sharing(count):
    if count not in (KEY_VALUE_HEADS, QUERY_HEADS):
        raise ValueError(count)
    return count // KEY_VALUE_HEADS


def qkv_spans(count, device, gradients=False):
    own = QUERY_HEADS // count * HEAD
    repeat = sharing(count)
    queries = QUERY_HEADS * HEAD
    shared = lax.div(device, repeat) * HEAD
    if repeat == 2 and gradients:
        which = lax.rem(device, 2)
        return [
            (device * own, 0, own),
            (queries + which * (KEY_VALUE_HEADS * HEAD) + shared, own + which * HEAD, HEAD),
        ]
    return [
        (device * own, 0, own),
        (queries + shared, own, HEAD),
        (queries + KEY_VALUE_HEADS * HEAD + shared, own + HEAD, HEAD),
    ]


def mlp_spans(count, device, gradients=False):
    own = FF // count
    return [(device * own, 0, own), (FF + device * own, own, own)]


def outgoing(spans, count):
    def pieces(device, owner):
        return [
            ((slice(None), span(whole, width)), (owner, slice(None), pl.ds(part, width)))
            for whole, part, width in spans(count, device)
        ]

    return pieces


def incoming(spans, count):
    def pieces(device, owner):
        return [
            ((device, slice(None), span(part, width)), (slice(None), span(whole, width)))
            for whole, part, width in spans(count, owner, True)
        ]

    return pieces


def everyone(count, me, group):
    return [(flip(me, slot), group) for slot in range(1, count)]


def spread_kernel(count, source, target, send, recv):
    me = lax.axis_index("ctx")
    group = lax.axis_index("fsdp")
    greet(everyone(count, me, group))
    trade(count, me, group, outgoing(qkv_spans, count), source, target, send, recv)()


def spread_qkv(count, collective, weight):
    rows = weight.shape[0]
    width = QUERY_HEADS // count * HEAD + 2 * HEAD
    return pl.pallas_call(
        functools.partial(spread_kernel, count),
        out_shape=jax.ShapeDtypeStruct((count, rows, width), weight.dtype),
        in_specs=[ANY],
        out_specs=ANY,
        scratch_shapes=[DMA((3 * count,)), DMA((3 * count,))],
        compiler_params=pltpu.CompilerParams(collective_id=collective, has_side_effects=True),
        cost_estimate=cost(12),
    )(weight)


def opening_kernel(
    count, normed, runs, weight, rows, all_runs, parts, send, recv, run_send, run_recv, part_send, part_recv
):
    me = lax.axis_index("ctx")
    group = lax.axis_index("fsdp")
    greet(everyone(count, me, group))
    finish_runs = trade(
        count, me, group, lambda device, owner: [((0,), (owner,))], runs, all_runs, run_send, run_recv
    )
    finish_rows = gather_rows(count, me, group, normed, rows, send, recv)
    finish_parts = trade(
        count, me, group, outgoing(mlp_spans, count), weight, parts, part_send, part_recv
    )
    finish_rows()
    finish_parts()
    finish_runs()


def opening(count, collective, normed, runs, weight):
    tokens, width = normed.shape
    return pl.pallas_call(
        functools.partial(opening_kernel, count),
        out_shape=[
            jax.ShapeDtypeStruct((count * tokens, width), BF16),
            jax.ShapeDtypeStruct((count, 8, 128), jnp.int32),
            jax.ShapeDtypeStruct((count, weight.shape[0], 2 * FF // count), BF16),
        ],
        in_specs=[ANY, ANY, ANY],
        out_specs=[ANY, ANY, ANY],
        scratch_shapes=[
            DMA((2 * count,)),
            DMA((2 * count,)),
            DMA((count,)),
            DMA((count,)),
            DMA((2 * count,)),
            DMA((2 * count,)),
        ],
        compiler_params=pltpu.CompilerParams(collective_id=collective, has_side_effects=True),
        cost_estimate=cost(60),
    )(normed, runs, weight)


def return_kernel(count, spans, source, target, send, recv):
    me = lax.axis_index("ctx")
    group = lax.axis_index("fsdp")
    greet(everyone(count, me, group))
    trade(count, me, group, incoming(spans, count), source, target, send, recv)()


def return_columns(count, collective, spans, width, parts):
    rows = parts.shape[1]
    pieces = len(spans(count, 0, True))
    return pl.pallas_call(
        functools.partial(return_kernel, count, spans),
        out_shape=jax.ShapeDtypeStruct((rows, width), parts.dtype),
        in_specs=[ANY],
        out_specs=ANY,
        scratch_shapes=[DMA((pieces * count,)), DMA((pieces * count,))],
        compiler_params=pltpu.CompilerParams(collective_id=collective, has_side_effects=True),
        cost_estimate=cost(12),
    )(parts)


def total_kernel(count, groups, values, result, near, far, send, recv, far_send, far_recv):
    me = lax.axis_index("ctx")
    group = lax.axis_index("fsdp")
    others = [lax.rem(group + step, groups) for step in range(1, groups)]
    greet(everyone(count, me, group) + [(me, other) for other in others])
    copies = []
    for slot in range(1, count):
        item = pltpu.make_async_remote_copy(
            values,
            near.at[me],
            send.at[slot],
            recv.at[slot],
            device_id=(flip(me, slot), group),
            device_id_type=MESH,
        )
        item.start()
        copies.append(item)
    near[me] = values[...]
    for item in copies:
        item.wait()
    summed = near[0]
    for index in range(1, count):
        summed = summed + near[index]
    far[group] = summed
    copies = []
    for step, other in enumerate(others):
        item = pltpu.make_async_remote_copy(
            far.at[group],
            far.at[group],
            far_send.at[step],
            far_recv.at[step],
            device_id=(me, other),
            device_id_type=MESH,
        )
        item.start()
        copies.append(item)
    for item in copies:
        item.wait()
    summed = far[0]
    for index in range(1, groups):
        summed = summed + far[index]
    result[...] = summed


def total(count, groups, collective, values):
    shape = values.shape
    return pl.pallas_call(
        functools.partial(total_kernel, count, groups),
        out_shape=jax.ShapeDtypeStruct(shape, F32),
        in_specs=[VMEM],
        out_specs=VMEM,
        scratch_shapes=[
            pltpu.VMEM((count,) + shape, F32),
            pltpu.VMEM((groups,) + shape, F32),
            DMA((count,)),
            DMA((count,)),
            DMA((groups,)),
            DMA((groups,)),
        ],
        compiler_params=pltpu.CompilerParams(collective_id=collective, has_side_effects=True),
        cost_estimate=cost(12),
    )(values)


def product_scatter_kernel(
    count, flipped, left, right, result, kept, near_out, near_in, far_out, far_in, ns, nr, fs, fr
):
    me = lax.axis_index("ctx")
    group = lax.axis_index("fsdp")
    rows, width = result.shape
    half = rows // 2
    bits = bits_of(count)
    orders = [bits[1:][::-1], bits[1:]]
    greet([(flip(me, bit), group) for bit in bits])
    tile = min(512, width)

    def product(slot, store):
        start = pl.multiple_of(flip(me, slot) * rows, rows)
        block = left[pl.ds(start, rows), :]

        def step(index, carry):
            columns = pl.ds(pl.multiple_of(index * tile, tile), tile)
            if flipped:
                value = lax.dot_general(
                    block, right[columns, :], (((1,), (1,)), ((), ())), preferred_element_type=F32
                )
            else:
                value = jnp.dot(block, right[:, columns], preferred_element_type=F32)
            store(columns, value)
            return carry

        lax.fori_loop(0, width // tile, step, 0)

    def first(part, slot):
        return [bit for bit in orders[part] if slot & bit][0]

    def near(pair):
        return pltpu.make_async_remote_copy(
            near_out.at[pair],
            near_in.at[pair],
            ns.at[pair],
            nr.at[pair],
            device_id=(flip(me, 1), group),
            device_id_type=MESH,
        )

    def far(part, pair):
        number = part * (count // 2) + pair
        return pltpu.make_async_remote_copy(
            far_out.at[number],
            far_in.at[number],
            fs.at[number],
            fr.at[number],
            device_id=(flip(me, first(part, 2 * pair)), group),
            device_id_type=MESH,
        )

    def needs(part, pair):
        found = []
        for bit in orders[part]:
            if 2 * pair & bit:
                break
            found.append((2 * pair ^ bit) // 2)
        return found

    def settle(part, pair):
        span_rows = pl.ds(part * half, half)
        value = kept[pair, span_rows, :]
        for other in needs(part, pair):
            far(part, other).wait_recv()
            value = value + far_in[part * (count // 2) + other].astype(F32)
        if pair == 0:
            result[span_rows, :] = value
        else:
            far_out[part * (count // 2) + pair] = value.astype(BF16)
            far(part, pair).start()

    pairs = list(range(count // 2))[::-1]
    for pair in pairs:

        def store_near(columns, value):
            near_out[pair, :, columns] = value.astype(BF16)

        def store_kept(columns, value):
            kept[pair, :, columns] = value

        product(2 * pair + 1, store_near)
        near(pair).start()
        product(2 * pair, store_kept)
        near(pair).wait_recv()
        kept[pair] = kept[pair] + near_in[pair].astype(F32)
        for part in (0, 1):
            if pair and not needs(part, pair):
                settle(part, pair)
    for pair in pairs:
        for part in (0, 1):
            if not pair or needs(part, pair):
                settle(part, pair)
    for pair in pairs:
        near(pair).wait_send()
        for part in (0, 1):
            if pair:
                far(part, pair).wait_send()


def product_scatter(count, collective, left, right, flipped):
    tokens, depth = left.shape
    width = right.shape[0] if flipped else right.shape[1]
    rows = tokens // count
    pairs = count // 2
    return pl.pallas_call(
        functools.partial(product_scatter_kernel, count, flipped),
        out_shape=jax.ShapeDtypeStruct((rows, width), F32),
        in_specs=[VMEM, VMEM],
        out_specs=VMEM,
        scratch_shapes=[
            pltpu.VMEM((pairs, rows, width), F32),
            pltpu.VMEM((pairs, rows, width), BF16),
            pltpu.VMEM((pairs, rows, width), BF16),
            pltpu.VMEM((2 * pairs, rows // 2, width), BF16),
            pltpu.VMEM((2 * pairs, rows // 2, width), BF16),
            DMA((pairs,)),
            DMA((pairs,)),
            DMA((2 * pairs,)),
            DMA((2 * pairs,)),
        ],
        compiler_params=pltpu.CompilerParams(
            collective_id=collective, has_side_effects=True, vmem_limit_bytes=VMEM_LIMIT
        ),
        cost_estimate=cost(45, 2 * tokens * depth * width),
    )(left, right)


def swap_halves(value):
    return jnp.concatenate([value[:, HEAD // 2 :], value[:, : HEAD // 2]], axis=1)


def nt(left, right):
    return lax.dot_general(left, right, (((1,), (1,)), ((), ())), preferred_element_type=F32)


def causal(keys, queries):
    key = lax.broadcasted_iota(jnp.int32, (keys, queries), 0)
    query = lax.rem(lax.broadcasted_iota(jnp.int32, (keys, queries), 1), CONT)
    return key <= query


def attention_kernel(
    heads, runs, joined, cosine, sine, q_gain, k_gain, attended, raw, queries, keys, values, mixed, lse, turned, placed
):
    tokens = joined.shape[0]
    blocks = tokens // CONT
    wide = heads * CONT

    def sort(run, carry):
        origin = pl.multiple_of(run * RUN, RUN)
        place = pl.multiple_of(runs[run] * RUN, RUN)
        raw[pl.ds(place, RUN), :] = joined[pl.ds(origin, RUN), :]
        return carry

    lax.fori_loop(0, tokens // RUN, sort, 0)

    def prepare(block, carry):
        span_rows = pl.ds(pl.multiple_of(block * CONT, CONT), CONT)
        cos_rows = cosine[span_rows, :]
        sin_rows = sine[span_rows, :]

        def turn(value, gain):
            value = value * lax.rsqrt(jnp.mean(value * value, axis=-1, keepdims=True) + EPS) * gain
            return (value * cos_rows + swap_halves(value) * sin_rows).astype(BF16)

        for head in range(heads):
            piece = raw[span_rows, head * HEAD : (head + 1) * HEAD]
            queries[block, head * CONT : (head + 1) * CONT, :] = turn(piece, q_gain[...])
        keys[span_rows, :] = turn(raw[span_rows, wide : wide + HEAD], k_gain[...])
        piece = raw[span_rows, wide + HEAD : wide + 2 * HEAD]
        values[span_rows, :] = piece.astype(BF16)
        turned[:, span_rows] = piece.T.astype(BF16)
        return carry

    lax.fori_loop(0, blocks, prepare, 0)

    def attend(block, own, before):
        query = queries[block]
        own_rows = pl.ds(own, CONT)
        weight = jnp.exp2(nt(keys[own_rows, :], query) * SCALE2)
        weight = jnp.where(causal(CONT, wide), weight, 0.0)
        sums = jnp.sum(weight, axis=0, keepdims=True)
        out = jnp.dot(turned[:, own_rows], weight.astype(BF16), preferred_element_type=F32)
        if before:
            weight = jnp.exp2(nt(keys[:before, :], query) * SCALE2)
            sums = sums + jnp.sum(weight, axis=0, keepdims=True)
            out = out + jnp.dot(turned[:, :before], weight.astype(BF16), preferred_element_type=F32)
        out = out / sums
        mixed[block] = out
        lse[block] = jnp.broadcast_to(jnp.log2(sums), (8, wide))
        for head in range(heads):
            placed[own_rows, head * HEAD : (head + 1) * HEAD] = out[
                :, head * CONT : (head + 1) * CONT
            ].T.astype(BF16)

    for block in range(PROMPT // CONT):
        attend(block, block * CONT, block * CONT)

    def continuation(block, carry):
        attend(block, pl.multiple_of(block * CONT, CONT), PROMPT)
        return carry

    lax.fori_loop(PROMPT // CONT, blocks, continuation, 0)

    def unsort(run, carry):
        origin = pl.multiple_of(run * RUN, RUN)
        place = pl.multiple_of(runs[run] * RUN, RUN)
        attended[pl.ds(origin, RUN), :] = placed[pl.ds(place, RUN), :]
        return carry

    lax.fori_loop(0, tokens // RUN, unsort, 0)


def attention(heads, runs, joined, cosine, sine, q_gain, k_gain):
    tokens = joined.shape[0]
    blocks = tokens // CONT
    wide = heads * CONT
    shape = jax.ShapeDtypeStruct
    return pl.pallas_call(
        functools.partial(attention_kernel, heads),
        out_shape=[
            shape((tokens, wide), BF16),
            shape(joined.shape, F32),
            shape((blocks, wide, HEAD), BF16),
            shape((tokens, HEAD), BF16),
            shape((tokens, HEAD), BF16),
            shape((blocks, HEAD, wide), F32),
            shape((blocks, 8, wide), F32),
        ],
        in_specs=[SMEM, VMEM, VMEM, VMEM, VMEM, VMEM],
        out_specs=[VMEM] * 7,
        scratch_shapes=[pltpu.VMEM((HEAD, tokens), BF16), pltpu.VMEM((tokens, wide), BF16)],
        compiler_params=pltpu.CompilerParams(vmem_limit_bytes=VMEM_LIMIT),
        cost_estimate=cost(15),
    )(runs, joined, cosine, sine, q_gain, k_gain)


def attention_back_kernel(
    heads, runs, d_attended, queries, keys, values, mixed, lse, d_queries, d_keys, d_values, arrived, keys_turned
):
    tokens = keys.shape[0]
    blocks = tokens // CONT
    wide = heads * CONT

    def sort(run, carry):
        origin = pl.multiple_of(run * RUN, RUN)
        place = pl.multiple_of(runs[run] * RUN, RUN)
        arrived[pl.ds(place, RUN), :] = d_attended[pl.ds(origin, RUN), :]
        return carry

    lax.fori_loop(0, tokens // RUN, sort, 0)
    d_keys[...] = jnp.zeros_like(d_keys)
    d_values[...] = jnp.zeros_like(d_values)

    def turn(block, carry):
        span_rows = pl.ds(pl.multiple_of(block * CONT, CONT), CONT)
        keys_turned[:, span_rows] = keys[span_rows, :].astype(F32).T.astype(BF16)
        return carry

    lax.fori_loop(0, blocks, turn, 0)

    def back(block, own, before):
        query = queries[block]
        own_rows = pl.ds(own, CONT)
        grad = jnp.concatenate(
            [arrived[own_rows, head * HEAD : (head + 1) * HEAD] for head in range(heads)], axis=0
        )
        grad_turned = grad.astype(F32).T
        delta = jnp.sum(grad_turned * mixed[block], axis=0, keepdims=True)
        total_row = lse[block][:1, :]

        def part(rows, count, masked):
            prob = jnp.exp2(nt(keys[rows, :], query) * SCALE2 - total_row)
            if masked:
                prob = jnp.where(causal(count, wide), prob, 0.0)
            score = (prob * (nt(values[rows, :], grad) - delta)).astype(BF16)
            d_values[rows, :] += jnp.dot(prob.astype(BF16), grad, preferred_element_type=F32)
            d_keys[rows, :] += jnp.dot(score, query, preferred_element_type=F32)
            return jnp.dot(keys_turned[:, rows], score, preferred_element_type=F32)

        result = part(own_rows, CONT, True)
        if before:
            result = result + part(slice(0, before), before, False)
        result = result * SCALE
        for head in range(heads):
            d_queries[own_rows, head * HEAD : (head + 1) * HEAD] = result[
                :, head * CONT : (head + 1) * CONT
            ].T.astype(BF16)

    for block in range(PROMPT // CONT):
        back(block, block * CONT, block * CONT)

    def continuation(block, carry):
        back(block, pl.multiple_of(block * CONT, CONT), PROMPT)
        return carry

    lax.fori_loop(PROMPT // CONT, blocks, continuation, 0)


def attention_back(heads, runs, d_attended, queries, keys, values, mixed, lse):
    tokens = keys.shape[0]
    wide = heads * CONT
    shape = jax.ShapeDtypeStruct
    return pl.pallas_call(
        functools.partial(attention_back_kernel, heads),
        out_shape=[shape((tokens, wide), BF16), shape((tokens, HEAD), F32), shape((tokens, HEAD), F32)],
        in_specs=[SMEM] + [VMEM] * 6,
        out_specs=[VMEM] * 3,
        scratch_shapes=[pltpu.VMEM((tokens, wide), BF16), pltpu.VMEM((HEAD, tokens), BF16)],
        compiler_params=pltpu.CompilerParams(vmem_limit_bytes=VMEM_LIMIT),
        cost_estimate=cost(25),
    )(runs, d_attended, queries, keys, values, mixed, lse)


def joined_back_kernel(
    heads, runs, raw, d_queries, d_keys, d_values, cosine, sine, q_gain, k_gain, share, d_joined, d_q_gain, d_k_gain, placed
):
    tokens = raw.shape[0]
    blocks = tokens // CONT
    wide = heads * CONT
    d_q_gain[...] = jnp.zeros_like(d_q_gain)
    d_k_gain[...] = jnp.zeros_like(d_k_gain)

    def step(block, carry):
        span_rows = pl.ds(pl.multiple_of(block * CONT, CONT), CONT)
        cos_rows = cosine[span_rows, :]
        sin_rows = sine[span_rows, :]

        def pull(value, grad, gain):
            grad = grad * cos_rows - swap_halves(grad) * sin_rows
            scale = lax.rsqrt(jnp.mean(value * value, axis=-1, keepdims=True) + EPS)
            scaled = value * scale
            gain_grad = jnp.sum(grad * scaled, axis=0, keepdims=True)
            grad = grad * gain
            return scale * (grad - scaled * jnp.mean(grad * scaled, axis=-1, keepdims=True)), gain_grad

        for head in range(heads):
            columns = slice(head * HEAD, (head + 1) * HEAD)
            grad, gain_grad = pull(
                raw[span_rows, columns], d_queries[span_rows, columns].astype(F32), q_gain[...]
            )
            placed[span_rows, columns] = grad.astype(BF16)
            d_q_gain[...] += gain_grad
        key_part, value_part = share[:1, :], share[1:, :]
        grad, gain_grad = pull(
            raw[span_rows, wide : wide + HEAD],
            (d_keys[span_rows, :] * SCALE).astype(BF16).astype(F32),
            k_gain[...],
        )
        placed[span_rows, wide : wide + HEAD] = (grad * key_part).astype(BF16)
        d_k_gain[...] += gain_grad * key_part
        placed[span_rows, wide + HEAD : wide + 2 * HEAD] = (d_values[span_rows, :] * value_part).astype(BF16)
        return carry

    lax.fori_loop(0, blocks, step, 0)

    def unsort(run, carry):
        origin = pl.multiple_of(run * RUN, RUN)
        place = pl.multiple_of(runs[run] * RUN, RUN)
        d_joined[pl.ds(origin, RUN), :] = placed[pl.ds(place, RUN), :]
        return carry

    lax.fori_loop(0, tokens // RUN, unsort, 0)


def joined_back(heads, runs, raw, d_queries, d_keys, d_values, cosine, sine, q_gain, k_gain, share):
    shape = jax.ShapeDtypeStruct
    return pl.pallas_call(
        functools.partial(joined_back_kernel, heads),
        out_shape=[shape(raw.shape, BF16), shape((1, HEAD), F32), shape((1, HEAD), F32)],
        in_specs=[SMEM] + [VMEM] * 9,
        out_specs=[VMEM] * 3,
        scratch_shapes=[pltpu.VMEM(raw.shape, BF16)],
        compiler_params=pltpu.CompilerParams(vmem_limit_bytes=VMEM_LIMIT),
        cost_estimate=cost(8),
    )(runs, raw, d_queries, d_keys, d_values, cosine, sine, q_gain, k_gain, share)


def norm_back(values, gain, grad):
    scale = lax.rsqrt(jnp.mean(values * values, axis=-1, keepdims=True) + EPS)
    scaled = values * scale
    pushed = grad * gain
    back = scale * (pushed - scaled * jnp.mean(pushed * scaled, axis=-1, keepdims=True))
    return back, jnp.sum(grad * scaled, axis=0)


def norm_rows(values, gain):
    return values * lax.rsqrt(jnp.mean(values * values, axis=-1, keepdims=True) + EPS) * gain


def rotary(tokens):
    index = jnp.arange(tokens, dtype=jnp.int32)
    place = jnp.where(index < PROMPT, index, PROMPT + (index - PROMPT) % CONT).astype(F32)
    exponent = jnp.arange(HEAD // 2, dtype=F32) * (2.0 / HEAD)
    angles = place[:, None] * jnp.power(ROPE_BASE, -exponent)[None, :]
    cosine, sine = jnp.cos(angles), jnp.sin(angles)
    return jnp.concatenate([cosine, cosine], axis=1), jnp.concatenate([-sine, sine], axis=1)


def body(
    count,
    groups,
    hidden_in,
    segment_ids,
    positions,
    attn_gain,
    qkv_weight,
    query_norm_gain,
    k_gain,
    out_weight,
    mlp_gain,
    gate_up,
    down_weight,
    cotangent,
):
    hidden = hidden_in[0].astype(F32)
    rows, width = hidden.shape
    tokens = rows * count
    heads = QUERY_HEADS // count
    repeat = sharing(count)
    me = lax.axis_index("ctx")

    first = segment_ids[0, ::RUN]
    place = positions[0, ::RUN]
    order = jnp.where(first == 0, place, place + (first - 1) * CONT) // RUN
    runs = jnp.zeros((1, 8, 128), jnp.int32).at[0, 0, : rows // RUN].set(order)

    def gather_groups(values, axis):
        return lax.all_gather(values, "fsdp", axis=axis, tiled=True)

    def scatter_groups(values):
        return lax.psum_scatter(values, "fsdp", scatter_dimension=0, tiled=True)

    w_out = gather_groups(out_weight, 0)
    w_down = gather_groups(down_weight, 0)
    qkv_parts = spread_qkv(count, 1, qkv_weight)
    normed_local = norm_rows(hidden, attn_gain).astype(BF16)
    normed, all_runs, mlp_parts = opening(count, 2, normed_local, runs, gate_up)
    w_qkv = gather_groups(qkv_parts, 1).reshape(width, -1)
    w_gu = gather_groups(mlp_parts, 1).reshape(width, -1)
    run_order = all_runs[:, 0, : rows // RUN].reshape(-1)
    cosine, sine = rotary(tokens)
    q_gain_row = query_norm_gain[None, :]
    k_gain_row = k_gain[None, :]

    joined = jnp.dot(normed, w_qkv, preferred_element_type=F32)
    attended, raw, queries, keys, values, mixed, lse = attention(
        heads, run_order, joined, cosine, sine, q_gain_row, k_gain_row
    )
    middle = hidden + product_scatter(count, 3, attended, w_out, False)
    second = gather_ctx(count, 4, norm_rows(middle, mlp_gain).astype(BF16))
    both = jnp.dot(second, w_gu, preferred_element_type=F32)
    own = both.shape[1] // 2
    gate, up = both[:, :own], both[:, own:]
    sigmoid = jax.nn.sigmoid(gate)
    activated = (gate * sigmoid * up).astype(BF16)

    upstream = gather_ctx(count, 5, cotangent[0])
    d_down = jnp.dot(activated.T, upstream, preferred_element_type=F32).astype(BF16)
    d_down = scatter_groups(d_down)
    d_activated = lax.dot_general(
        upstream, w_down, (((1,), (1,)), ((), ())), preferred_element_type=F32
    ).astype(BF16).astype(F32)
    d_gate = d_activated * up * sigmoid * (1.0 + gate * (1.0 - sigmoid))
    d_up = d_activated * gate * sigmoid
    d_both = jnp.concatenate([d_gate, d_up], axis=1).astype(BF16)

    def weight_grad(left, right):
        grad = lax.dot_general(left, right, (((0,), (0,)), ((), ())), preferred_element_type=F32)
        grad = grad.astype(BF16).reshape(count, groups, -1, right.shape[1])
        return scatter_groups(grad.transpose(1, 0, 2, 3).reshape(groups * count, -1, right.shape[1]))

    gu_parts = weight_grad(second, d_both)
    d_second = product_scatter(count, 6, d_both, w_gu, True)
    middle_back, mlp_gain_grad = norm_back(middle, mlp_gain, d_second)
    d_middle = cotangent[0].astype(F32) + middle_back
    middle_low = gather_ctx(count, 7, d_middle.astype(BF16))
    d_out = lax.dot_general(
        attended, middle_low, (((0,), (0,)), ((), ())), preferred_element_type=F32
    ).astype(BF16)
    d_out = scatter_groups(d_out)
    d_attended = lax.dot_general(
        middle_low, w_out, (((1,), (1,)), ((), ())), preferred_element_type=F32
    ).astype(BF16)
    d_queries, d_keys, d_values = attention_back(
        heads, run_order, d_attended, queries, keys, values, mixed, lse
    )
    share = jnp.ones((2, HEAD), F32)
    if repeat > 1:
        swap = [(index, index ^ 1) for index in range(count)]
        d_keys = d_keys + lax.ppermute(d_keys, "ctx", swap)
        d_values = d_values + lax.ppermute(d_values, "ctx", swap)
        mine = lax.rem(me, 2) == jnp.arange(2)
        share = share * mine[:, None].astype(F32)
    d_joined, q_gain_grad, k_gain_grad = joined_back(
        heads, run_order, raw, d_queries, d_keys, d_values, cosine, sine, q_gain_row, k_gain_row, share
    )
    qkv_grad_parts = weight_grad(normed, d_joined)
    d_normed = product_scatter(count, 8, d_joined, w_qkv, True)
    output = middle + product_scatter(count, 9, activated, w_down, False)
    hidden_back, attn_gain_grad = norm_back(hidden, attn_gain, d_normed)
    d_hidden = d_middle + hidden_back

    d_gate_up = return_columns(count, 10, mlp_spans, 2 * FF, gu_parts)
    qkv_width = qkv_weight.shape[1]
    d_qkv = return_columns(count, 11, qkv_spans, qkv_width, qkv_grad_parts)
    small = jnp.concatenate([attn_gain_grad, mlp_gain_grad, q_gain_grad[0], k_gain_grad[0]])
    padded = -(-small.shape[0] // 1024) * 1024
    small = jnp.pad(small, (0, padded - small.shape[0])).reshape(-1, 128)
    summed = total(count, groups, 12, small).reshape(-1)
    return (
        output.astype(BF16)[None],
        d_hidden[None],
        summed[:width],
        d_qkv.astype(F32),
        summed[2 * width : 2 * width + HEAD],
        summed[2 * width + HEAD : 2 * width + 2 * HEAD],
        d_out.astype(F32),
        summed[width : 2 * width],
        d_gate_up.astype(F32),
        d_down.astype(F32),
    )


def solution(mesh):
    return jax.shard_map(
        functools.partial(body, mesh.shape["ctx"], mesh.shape["fsdp"]),
        mesh=mesh,
        in_specs=(
            P("fsdp", "ctx", None),
            P("fsdp", "ctx"),
            P("fsdp", "ctx"),
            P(),
            P(("ctx", "fsdp"), None),
            P(),
            P(),
            P(("ctx", "fsdp"), None),
            P(),
            P(("ctx", "fsdp"), None),
            P(("ctx", "fsdp"), None),
            P("fsdp", "ctx", None),
        ),
        out_specs=(
            P("fsdp", "ctx", None),
            P("fsdp", "ctx", None),
            P(),
            P(("ctx", "fsdp"), None),
            P(),
            P(),
            P(("ctx", "fsdp"), None),
            P(),
            P(("ctx", "fsdp"), None),
            P(("ctx", "fsdp"), None),
        ),
        check_vma=False,
    )
```

time: 4900 us -> 703 us (0.14)
  waiting for transfers between devices: 4200 us -> 59.2 us
  Pallas kernels: 0 us -> 468 us
  matrix products: 305 us -> 99.4 us
  other arithmetic: 197 us -> 38 us
  local copies, waits for them, and re-layouts: 95.9 us -> 14.5 us
  blocking collectives: 74 us -> 0 us
    unnamed x14 -> x8, waiting for transfers between devices: 1750 us -> 1.32 us
    reduce_scatter x2 -> x4, waiting for transfers between devices: 1410 us -> 53 us  [scatter_groups(): return lax.psum_scatter(values, 'fsdp', scatter_dimension=0, tiled=True)]
    all_gather x10 -> x4, waiting for transfers between devices: 1040 us -> 4.81 us  [gather_groups(): return lax.all_gather(values, 'fsdp', axis=axis, tiled=True)]
    pallas_call x0 -> x15, Pallas kernels: none -> 468 us  [the longest x4 184 us: product_scatter(): pl.pallas_call(functools.partial(product_scatter_kernel, count, flipped),...]
    dot_general x48 -> x8, matrix products: 305 us -> 99.4 us  [the longest x2 26.8 us: weight_grad(): lax.dot_general(left, right, (((0,), (0,)), ((), ())), preferred_element_...]
    concatenate x5 -> x2, other arithmetic: 136 us -> 5.09 us  [the longest x1 3.16 us: body(): d_both = jnp.concatenate([d_gate, d_up], axis=1).astype(BF16)]
  transfers between devices with their start and end apart: 13 -> 8, of which waited for: 12 -> 2; matrix products, arithmetic and copies ran while one was open for 9% -> 16% of each run, Pallas kernels for 0% -> 50%
where the time goes in v1:
time: 703 us; the launch traced here: 694 us
  Pallas kernels  468 us (67%)
  matrix products  99.4 us (14%)
  waiting for transfers between devices  59.2 us (8%)
  other arithmetic  38 us (5%)
  between operations  14.9 us (2%)
  local copies, waits for them, and re-layouts  14.5 us (2%)
    pallas_call x4, Pallas kernels, product_scatter(): pl.pallas_call(functools.partial(product_scatter_kernel, count, flipped),...  184 us
    pallas_call x3, Pallas kernels, gather_ctx(): pl.pallas_call(functools.partial(gather_kernel, count), out_shape=jax.Sha...  119 us
    pallas_call x1, Pallas kernels, opening(): pl.pallas_call(functools.partial(opening_kernel, count), out_shape=[jax.S...  58.7 us
    reduce_scatter x4, waiting for transfers between devices, scatter_groups(): return lax.psum_scatter(values, 'fsdp', scatter_dimension=0, tiled=True)  53 us
    pallas_call x2, Pallas kernels, return_columns(): pl.pallas_call(functools.partial(return_kernel, count, spans), out_shape=...  30.9 us
    dot_general x2, matrix products, weight_grad(): lax.dot_general(left, right, (((0,), (0,)), ((), ())), preferred_element_...  26.8 us
    pallas_call x1, Pallas kernels, attention(): pl.pallas_call(functools.partial(attention_kernel, heads), out_shape=[sha...  20.7 us
    dot_general x1, matrix products, body(): both = jnp.dot(second, w_gu, preferred_element_type=F32)  19.2 us
  transfers between devices with their start and end apart: 8, of which 2 were waited for; matrix products, arithmetic and copies ran while one was open for 16% of the time, Pallas kernels for 50%

profile of v1, /device:TPU:0, one launch (start us, length us, event | category | flops | bytes accessed | tf_op | source)
XLA Modules:
  0.0 694.3 jit_solution(17945830512791287002)
XLA Ops:
  7.2 11.4 %shard_map.196 = bf16[8,64,512]{2,1,0:T(8,128)(2,1)} custom-call(bf16[64,4096]{1,0:T(8,128)(2,1)} %source.1), custom_call_target="tpu_custom_call" | custom-call | bytes 38400000 | tf_op jit(solution)/shard_map/pallas_call | solution.py:266
  25.2 58.7 %shard_map.195 = (bf16[2048,2048]{1,0:T(8,128)(2,1)}, s32[8,8,128]{2,1,0:T(8,128)}, bf16[8,64,1536]{2,1,0:T(8,128)(2,1)}) custom-call(bf16[256,2048]{1,0:T(8,128)(2,1)} %fusion.9.normed, s32[1,8,128]{2,1,0:T(8,128)} %scatter.4.runs, bf16[64,12288]{1,0:T(8,128)(2,1)} %weight.1), custom_call_target="tpu_custom_call" | custom-call | bytes 192000000 | tf_op jit(solution)/shard_map/pallas_call | solution.py:297
  85.9 40.0 %shard_map.201 = bf16[2048,2048]{1,0:T(8,128)(2,1)} custom-call(bf16[256,2048]{1,0:T(8,128)(2,1)} %bitcast.71), custom_call_target="tpu_custom_call" | custom-call | bytes 134400000 | tf_op jit(solution)/shard_map/pallas_call | solution.py:143
  131.5 10.4 %fusion.25.joined = f32[2048,512]{1,0:T(8,128)} fusion(bf16[2048,2048]{1,0:T(8,128)(2,1)} %get-tuple-element.39, bf16[2048,512]{1,0:T(8,128)(2,1)} %bitcast.83), kind=kOutput, calls=%fused_computation.73 | convolution fusion | flops 4294967296 | bytes 14680064 | tf_op jit(solution)/shard_map/dot_general | solution.py:851
  142.0 20.7 %shard_map.197 = (bf16[2048,256]{1,0:T(8,128)(2,1)}, f32[2048,512]{1,0:T(8,128)}, bf16[16,256,128]{2,1,0:T(8,128)(2,1)}, bf16[2048,128]{1,0:T(8,128)(2,1)}, bf16...) custom-call(s32[64]{0:T(128)} %reshape_squeeze.3.runs, f32[2048,512]{1,0:T(8,128)} %fusion.25.joined, ...), custom_call_target="tpu_custom_call" | custom-call | bytes 48000000 | tf_op jit(solution)/shard_map/pallas_call | solution.py:624
  162.7 44.1 %shard_map.198 = f32[256,2048]{1,0:T(8,128)} custom-call(bf16[2048,256]{1,0:T(8,128)(2,1)} %get-tuple-element.40.left, bf16[256,2048]{1,0:T(8,128)(2,1)} %all-gather.7.cloned.1.call-done.right), custom_call_target="tpu_custom_call" | custom-call | flops 2147483648 | bytes 144000000 | tf_op jit(solution)/shard_map/pallas_call | solution.py:510
  210.0 39.8 %shard_map.199 = bf16[2048,2048]{1,0:T(8,128)(2,1)} custom-call(bf16[256,2048]{1,0:T(8,128)(2,1)} %multiply_convert_fusion.1.source), custom_call_target="tpu_custom_call" | custom-call | bytes 134400000 | tf_op jit(solution)/shard_map/pallas_call | solution.py:143
  249.8 19.2 %fusion.26 = f32[2048,1536]{1,0:T(8,128)} fusion(bf16[2048,2048]{1,0:T(8,128)(2,1)} %shard_map.199, bf16[2048,1536]{1,0:T(8,128)(2,1)} %bitcast.81), kind=kOutput, calls=%fused_computation.74 | convolution fusion | flops 12884901888 | bytes 27262976 | tf_op jit(solution)/shard_map/dot_general | solution.py:857
  273.8 17.3 %fusion.2 = (bf16[2048,768]{1,0:T(8,128)(2,1)S(1)}, bf16[2048,768]{1,0:T(8,128)(2,1)S(1)}, bf16[2048,768]{1,0:T(8,128)(2,1)}) fusion(f32[2048,1536]{1,0:T(8,128)} %fusion.26, bf16[2048,2048]{1,0:T(8,128)(2,1)} %shard_map.201, bf16[768,2048]{1,0:T(8,128)(2,1)} %all-gather.11.cloned.1.call-done.right), kind=kOutput, calls=%fused_computation.5 | convolution fusion | flops 6470762496 | bytes 33554432 | tf_op jit(solution)/shard_map/dot_general | solution.py:866
  297.0 49.6 %shard_map.202 = f32[256,2048]{1,0:T(8,128)} custom-call(bf16[2048,1536]{1,0:T(8,128)(2,1)} %pad_maximum_fusion.left, bf16[2048,1536]{1,0:T(8,128)(2,1)} %bitcast.82), custom_call_target="tpu_custom_call" | custom-call | flops 12884901888 | bytes 144000000 | tf_op jit(solution)/shard_map/pallas_call | solution.py:510
  350.8 39.2 %shard_map.203 = bf16[2048,2048]{1,0:T(8,128)(2,1)} custom-call(bf16[256,2048]{1,0:T(8,128)(2,1)} %fusion.24.source), custom_call_target="tpu_custom_call" | custom-call | bytes 134400000 | tf_op jit(solution)/shard_map/pallas_call | solution.py:143
  390.1 6.7 convolution_convert_fusion.4
  396.8 7.0 %convolution_convert_fusion.5.d_attended = bf16[2048,256]{1,0:T(8,128)(2,1)} fusion(bf16[2048,2048]{1,0:T(8,128)(2,1)} %shard_map.203, bf16[256,2048]{1,0:T(8,128)(2,1)} %all-gather.7.cloned.1.call-done.right), kind=kOutput, calls=%fused_computation.22 | convolution fusion | flops 2148007936 | bytes 10485760 | tf_op jit(solution)/shard_map/dot_general | solution.py:887
  403.8 18.9 %shard_map.204 = (bf16[2048,256]{1,0:T(8,128)(2,1)}, f32[2048,128]{1,0:T(8,128)}, f32[2048,128]{1,0:T(8,128)}) custom-call(s32[64]{0:T(128)} %reshape_squeeze.3.runs, bf16[2048,256]{1,0:T(8,128)(2,1)} %convolution_convert_fusion.5.d_attended, bf16[16,256,128]{2,1,0:T(8,128)(2,1)} %get-tuple-element.43.queries, bf16[2048,128]{1,0:T(8,128)(2,1)} %get-tuple-element.44.keys, ...), custom_call_target="tpu_custom_call" | custom-call | bytes 80000000 | tf_op jit(solution)/shard_map/pallas_call | solution.py:709
  423.3 11.4 %shard_map.205 = (bf16[2048,512]{1,0:T(8,128)(2,1)}, f32[1,128]{1,0:T(1,128)}, f32[1,128]{1,0:T(1,128)}) custom-call(s32[64]{0:T(128)} %reshape_squeeze.3.runs, f32[2048,512]{1,0:T(8,128)} %get-tuple-element.42.raw, bf16[2048,256]{1,0:T(8,128)(2,1)} %get-tuple-element.48.d_queries, f32[2048,128]{1,0:T(8,128)} %get-tuple-element.49.d_keys, ...), custom_call_target="tpu_custom_call" | custom-call | bytes 25600000 | tf_op jit(solution)/shard_map/pallas_call | solution.py:773
  434.6 8.5 %convolution_convert_fusion.3 = bf16[2048,512]{1,0:T(8,128)(2,1)S(1)} fusion(bf16[2048,2048]{1,0:T(8,128)(2,1)} %get-tuple-element.39, bf16[2048,512]{1,0:T(8,128)(2,1)} %get-tuple-element.51.left), kind=kOutput, calls=%fused_computation.20 | convolution fusion | flops 4296015872 | bytes 12582912 | tf_op jit(solution)/shard_map/dot_general | solution.py:874
  444.7 12.0 %convolution_convert_fusion.1 = bf16[768,2048]{1,0:T(8,128)(2,1)} fusion(bf16[2048,768]{1,0:T(8,128)(2,1)} %get-tuple-element.62.left, bf16[2048,2048]{1,0:T(8,128)(2,1)} %shard_map.201), kind=kOutput, calls=%fused_computation.11 | convolution fusion | flops 6444023808 | bytes 14680064 | tf_op jit(solution)/shard_map/dot_general | solution.py:864
  456.9 18.2 %convolution_convert_fusion = bf16[2048,1536]{1,0:T(8,128)(2,1)S(1)} fusion(bf16[2048,2048]{1,0:T(8,128)(2,1)} %shard_map.199, bf16[2048,768]{1,0:T(8,128)(2,1)} %copy-done.5, bf16[2048,768]{1,0:T(8,128)(2,1)} %copy-done.4), kind=kOutput, calls=%fused_computation.2 | convolution fusion | flops 12900630528 | bytes 20971520 | tf_op jit(solution)/shard_map/dot_general | solution.py:874
  478.5 45.3 %shard_map.206 = f32[256,2048]{1,0:T(8,128)} custom-call(bf16[2048,512]{1,0:T(8,128)(2,1)} %get-tuple-element.51.left, bf16[2048,512]{1,0:T(8,128)(2,1)} %bitcast.84), custom_call_target="tpu_custom_call" | custom-call | flops 4294967296 | bytes 144000000 | tf_op jit(solution)/shard_map/pallas_call | solution.py:510
  526.9 12.9 %shard_map.207 = f32[40,128]{1,0:T(8,128)} custom-call(f32[40,128]{1,0:T(8,128)} %fusion.19.values), custom_call_target="tpu_custom_call" | custom-call | bytes 38400000 | tf_op jit(solution)/shard_map/pallas_call | solution.py:386
  542.4 45.1 %shard_map.200 = f32[256,2048]{1,0:T(8,128)} custom-call(bf16[2048,768]{1,0:T(8,128)(2,1)} %get-tuple-element.62.left, bf16[768,2048]{1,0:T(8,128)(2,1)} %all-gather.11.cloned.1.call-done.right), custom_call_target="tpu_custom_call" | custom-call | flops 6442450944 | bytes 144000000 | tf_op jit(solution)/shard_map/pallas_call | solution.py:510
  595.2 9.9 %shard_map.208 = bf16[64,4096]{1,0:T(8,128)(2,1)} custom-call(bf16[8,64,512]{2,1,0:T(8,128)(2,1)} %reduce-scatter.5.cloned.1.call-done.source), custom_call_target="tpu_custom_call" | custom-call | bytes 38400000 | tf_op jit(solution)/shard_map/pallas_call | solution.py:329
  609.7 53.0 %reduce-scatter.9.cloned.1.call-done.source = bf16[8,64,1536]{2,1,0:T(8,128)(2,1)} async-done(((bf16[32,64,1536]{2,1,0:T(8,128)(2,1)}), bf16[8,64,1536]{2,1,0:T(8,128)(2,1)}) %reduce-scatter.9.cloned.1.call-update) | async-done | bytes 1572880 | tf_op jit(solution)/shard_map/reduce_scatter | solution.py:837
  662.7 21.0 %shard_map.209 = bf16[64,12288]{1,0:T(8,128)(2,1)} custom-call(bf16[8,64,1536]{2,1,0:T(8,128)(2,1)} %reduce-scatter.9.cloned.1.call-done.source), custom_call_target="tpu_custom_call" | custom-call | bytes 38400000 | tf_op jit(solution)/shard_map/pallas_call | solution.py:329
  (82 shorter events, 58.9 us)
Async XLA Ops:
  7.2 16.0 %copy-start = (bf16[1,256,2048]{2,1,0:T(8,128)(2,1)S(1)}, bf16[1,256,2048]{2,1,0:T(8,128)(2,1)}, u32[]{:S(2)}) copy-start(bf16[1,256,2048]{2,1,0:T(8,128)(2,1)} %param.14) | copy-start | bytes 3145732
  7.2 124.3 %all-gather.5.cloned.1.call-start = ((), (), s32[]{:S(2)}) async-start(), calls=%async_computation.4 | async-start | bytes 2621440 | tf_op jit(solution)/shard_map/all_gather | solution.py:834
  18.7 144.0 %all-gather.7.cloned.1.call-start = ((), (), s32[]{:S(2)}) async-start(), calls=%async_computation.5 | async-start | bytes 1310720 | tf_op jit(solution)/shard_map/all_gather | solution.py:834
  19.4 230.3 %all-gather.9.cloned.1.call-start = ((), (), s32[]{:S(2)}) async-start(), calls=%async_computation.6 | async-start | bytes 7864320 | tf_op jit(solution)/shard_map/all_gather | solution.py:834
  23.2 60.7 %copy-start.9 = (f32[256]{0:T(256)}, f32[256]{0:T(256)S(1)}, u32[]{:S(2)}) copy-start(f32[256]{0:T(256)S(1)} %add_rsqrt_fusion.1) | copy-start | bytes 3076
  83.9 189.9 %all-gather.11.cloned.1.call-start = ((), (), s32[]{:S(2)}) async-start(), calls=%async_computation.7 | async-start | bytes 3932160 | tf_op jit(solution)/shard_map/all_gather | solution.py:834
  84.5 509.0 %reduce-scatter.7.cloned.1.call-start = ((), (), s32[]{:S(2)}) async-start(), calls=%async_computation.9 | async-start | bytes 1310720 | tf_op jit(solution)/shard_map/reduce_scatter | solution.py:837
  206.8 2.0 copy-start.7
  291.1 1.7 copy-start.4
  291.1 2.8 copy-start.5
  346.7 2.3 copy-start.2
  346.7 2.5 copy-start.3
  350.8 39.2 %copy-start.6 = (bf16[2048,256]{1,0:T(8,128)(2,1)S(1)}, bf16[2048,256]{1,0:T(8,128)(2,1)}, u32[]{:S(2)}) copy-start(bf16[2048,256]{1,0:T(8,128)(2,1)} %get-tuple-element.40.left) | copy-start | bytes 3145732
  396.8 198.4 %reduce-scatter.5.cloned.1.call-start = ((), (), s32[]{:S(2)}) async-start(), calls=%async_computation.8 | async-start | bytes 2621440 | tf_op jit(solution)/shard_map/reduce_scatter | solution.py:837
  444.7 162.6 %reduce-scatter.11.cloned.1.call-start = ((), (), s32[]{:S(2)}) async-start(), calls=%async_computation.11 | async-start | bytes 3932160 | tf_op jit(solution)/shard_map/reduce_scatter | solution.py:837
  456.8 205.9 %reduce-scatter.9.cloned.1.call-start = ((), (), s32[]{:S(2)}) async-start(), calls=%async_computation.10 | async-start | bytes 7864320 | tf_op jit(solution)/shard_map/reduce_scatter | solution.py:837
  478.5 45.4 %copy-start.1 = (bf16[1,256,2048]{2,1,0:T(8,128)(2,1)S(1)}, bf16[1,256,2048]{2,1,0:T(8,128)(2,1)}, u32[]{:S(2)}) copy-start(bf16[1,256,2048]{2,1,0:T(8,128)(2,1)} %param.14) | copy-start | bytes 3145732
  478.5 45.4 %copy-start.8 = (f32[2048]{0:T(1024)S(1)}, f32[2048]{0:T(1024)}, u32[]{:S(2)}) copy-start(f32[2048]{0:T(1024)} %param.17) | copy-start | bytes 24580
  478.5 45.4 %copy-start.10 = (f32[256]{0:T(256)S(1)}, f32[256]{0:T(256)}, u32[]{:S(2)}) copy-start(f32[256]{0:T(256)} %copy-done.9) | copy-start | bytes 3076
  523.9 2.3 copy-start.11
  523.9 2.3 copy-start.12
Sparse Core Ops, SparseCore 0:
  18.8 47.1 all-gather.4
  67.5 26.6 all-gather.6
  95.8 114.8 all-gather.8
  212.1 61.6 all-gather.10
  396.9 24.8 reduce-scatter.6
  444.8 41.6 reduce-scatter.4
  488.8 60.8 reduce-scatter.10
  552.0 110.7 reduce-scatter.8

commit v2 on v1

--- a/solution.py
+++ b/solution.py
@@ -3,6 +3,7 @@
 
 import jax
 import jax.numpy as jnp
+import numpy as np
 from jax import lax
 from jax.experimental import pallas as pl
 from jax.experimental.pallas import tpu as pltpu
@@ -68,87 +69,74 @@
     return [bit for bit in order if slot & bit][-1]
 
 
-def gather_rows(count, me, group, source, target, send, recv):
+def gather_rows(count, me, group, source, target, send, recv, own):
     rows = source.shape[0]
     half = rows // 2
     orders = gather_orders(count)
+    copies = []
+
+    def place(part, slot):
+        return pl.multiple_of(flip(me, slot) * rows + part * half, half)
 
     def copy(part, slot, bit):
-        start = pl.multiple_of(flip(me, slot) * rows + part * half, half)
-        place = target.at[pl.ds(start, half)]
-        origin = source.at[pl.ds(part * half, half)] if slot == 0 else place
+        there = target.at[pl.ds(place(part, slot), half)]
+        origin = source.at[pl.ds(part * half, half)] if slot == 0 else there
         number = part * count + (slot ^ bit)
         return pltpu.make_async_remote_copy(
             origin,
-            place,
+            there,
             send.at[number],
             recv.at[number],
             device_id=(flip(me, bit), group),
             device_id_type=MESH,
         )
 
-    own = pltpu.make_async_copy(
-        source, target.at[pl.ds(pl.multiple_of(me * rows, rows), rows)], send.at[0]
-    )
-    own.start()
-    copies = []
-    for step in range(len(orders[0])):
-        for part in (0, 1):
-            item = copy(part, 0, orders[part][step])
+    def keep(part):
+        there = target.at[pl.ds(place(part, 0), half)]
+        return pltpu.make_async_copy(source.at[pl.ds(part * half, half)], there, own.at[part])
+
+    def start(part):
+        for bit in orders[part]:
+            item = copy(part, 0, bit)
             item.start()
             copies.append(item)
-
-    def arrived(part, slot):
-        start = pl.multiple_of(flip(me, slot) * rows + part * half, half)
-        place = target.at[pl.ds(start, half)]
+        keep(part).start()
+
+    def wait(part, slot):
+        there = target.at[pl.ds(place(part, slot), half)]
         number = part * count + slot
         pltpu.make_async_remote_copy(
-            place,
-            place,
+            there,
+            there,
             send.at[number],
             recv.at[number],
             device_id=(flip(me, last_bit(orders[part], slot)), group),
             device_id_type=MESH,
         ).wait_recv()
 
-    def finish():
+    def finish(arrived=None):
         waits = []
         for part in (0, 1):
             order = orders[part]
             for slot in range(1, count):
                 last = order.index(last_bit(order, slot))
                 waits.append((last, bin(slot).count("1"), part, slot))
+            if arrived:
+                arrived(place(part, 0), source, part * half)
         for last, _, part, slot in sorted(waits):
-            arrived(part, slot)
+            wait(part, slot)
             for bit in orders[part][last + 1 :]:
                 item = copy(part, slot, bit)
                 item.start()
                 copies.append(item)
-        own.wait()
+            if arrived:
+                arrived(place(part, slot), target, place(part, slot))
+        for part in (0, 1):
+            keep(part).wait()
         for item in copies:
             item.wait_send()
 
-    return finish
-
-
-def gather_kernel(count, source, target, send, recv):
-    me = lax.axis_index("ctx")
-    group = lax.axis_index("fsdp")
-    greet([(flip(me, bit), group) for bit in bits_of(count)])
-    gather_rows(count, me, group, source, target, send, recv)()
-
-
-def gather_ctx(count, collective, values):
-    rows, width = values.shape
-    return pl.pallas_call(
-        functools.partial(gather_kernel, count),
-        out_shape=jax.ShapeDtypeStruct((count * rows, width), values.dtype),
-        in_specs=[ANY],
-        out_specs=ANY,
-        scratch_shapes=[DMA((2 * count,)), DMA((2 * count,))],
-        compiler_params=pltpu.CompilerParams(collective_id=collective, has_side_effects=True),
-        cost_estimate=cost(42),
-    )(values)
+    return start, finish
 
 
 def trade(count, me, group, pieces, source, target, send, recv):
@@ -253,91 +241,134 @@
     return [(flip(me, slot), group) for slot in range(1, count)]
 
 
-def spread_kernel(count, source, target, send, recv):
+def spread_kernel(count, qkv, mlp, qkv_parts, mlp_parts, send, recv, mlp_send, mlp_recv):
     me = lax.axis_index("ctx")
     group = lax.axis_index("fsdp")
     greet(everyone(count, me, group))
-    trade(count, me, group, outgoing(qkv_spans, count), source, target, send, recv)()
-
-
-def spread_qkv(count, collective, weight):
-    rows = weight.shape[0]
+    finish = trade(count, me, group, outgoing(qkv_spans, count), qkv, qkv_parts, send, recv)
+    finish_mlp = trade(count, me, group, outgoing(mlp_spans, count), mlp, mlp_parts, mlp_send, mlp_recv)
+    finish()
+    finish_mlp()
+
+
+def spread(count, collective, qkv, mlp):
+    rows = qkv.shape[0]
     width = QUERY_HEADS // count * HEAD + 2 * HEAD
     return pl.pallas_call(
         functools.partial(spread_kernel, count),
-        out_shape=jax.ShapeDtypeStruct((count, rows, width), weight.dtype),
-        in_specs=[ANY],
-        out_specs=ANY,
-        scratch_shapes=[DMA((3 * count,)), DMA((3 * count,))],
+        out_shape=[
+            jax.ShapeDtypeStruct((count, rows, width), BF16),
+            jax.ShapeDtypeStruct((count, rows, 2 * FF // count), BF16),
+        ],
+        in_specs=[ANY, ANY],
+        out_specs=[ANY, ANY],
+        scratch_shapes=[DMA((3 * count,)), DMA((3 * count,)), DMA((2 * count,)), DMA((2 * count,))],
         compiler_params=pltpu.CompilerParams(collective_id=collective, has_side_effects=True),
-        cost_estimate=cost(12),
-    )(weight)
-
-
-def opening_kernel(
-    count, normed, runs, weight, rows, all_runs, parts, send, recv, run_send, run_recv, part_send, part_recv
-):
+        cost_estimate=cost(28),
+    )(qkv, mlp)
+
+
+def opening_kernel(count, normed, runs, rows, all_runs, send, recv, own, run_send, run_recv):
     me = lax.axis_index("ctx")
     group = lax.axis_index("fsdp")
     greet(everyone(count, me, group))
     finish_runs = trade(
         count, me, group, lambda device, owner: [((0,), (owner,))], runs, all_runs, run_send, run_recv
     )
-    finish_rows = gather_rows(count, me, group, normed, rows, send, recv)
-    finish_parts = trade(
-        count, me, group, outgoing(mlp_spans, count), weight, parts, part_send, part_recv
-    )
-    finish_rows()
-    finish_parts()
+    start, finish = gather_rows(count, me, group, normed, rows, send, recv, own)
+    start(0)
+    start(1)
+    finish()
     finish_runs()
 
 
-def opening(count, collective, normed, runs, weight):
+def opening(count, collective, normed, runs):
     tokens, width = normed.shape
     return pl.pallas_call(
         functools.partial(opening_kernel, count),
         out_shape=[
             jax.ShapeDtypeStruct((count * tokens, width), BF16),
             jax.ShapeDtypeStruct((count, 8, 128), jnp.int32),
-            jax.ShapeDtypeStruct((count, weight.shape[0], 2 * FF // count), BF16),
         ],
-        in_specs=[ANY, ANY, ANY],
-        out_specs=[ANY, ANY, ANY],
-        scratch_shapes=[
-            DMA((2 * count,)),
-            DMA((2 * count,)),
-            DMA((count,)),
-            DMA((count,)),
-            DMA((2 * count,)),
-            DMA((2 * count,)),
-        ],
+        in_specs=[ANY, ANY],
+        out_specs=[ANY, ANY],
+        scratch_shapes=[DMA((2 * count,)), DMA((2 * count,)), DMA((2,)), DMA((count,)), DMA((count,))],
         compiler_params=pltpu.CompilerParams(collective_id=collective, has_side_effects=True),
-        cost_estimate=cost(60),
-    )(normed, runs, weight)
-
-
-def return_kernel(count, spans, source, target, send, recv):
+        cost_estimate=cost(45),
+    )(normed, runs)
+
+
+def across(count, bit, values):
+    return lax.ppermute(values, "ctx", [(index, index ^ bit) for index in range(count)])
+
+
+def join_kernel(count, slots, *refs):
+    blocks, (target, send, recv) = refs[:-3], refs[-3:]
     me = lax.axis_index("ctx")
     group = lax.axis_index("fsdp")
-    greet(everyone(count, me, group))
-    trade(count, me, group, incoming(spans, count), source, target, send, recv)()
-
-
-def return_columns(count, collective, spans, width, parts):
-    rows = parts.shape[1]
-    pieces = len(spans(count, 0, True))
+    other = flip(me, 1)
+    greet([(other, group)])
+    half = blocks[0].shape[1]
+    items = []
+    for block, (part, masks) in zip(blocks, slots):
+        items += [(block, index, part, mask) for index, mask in enumerate(masks)]
+
+    def place(number, owner):
+        _, _, part, mask = items[number]
+        return pl.ds(pl.multiple_of(flip(owner, mask) * 2 * half + part * half, half), half)
+
+    def copy(number, owner):
+        block, index = items[number][:2]
+        return pltpu.make_async_remote_copy(
+            block.at[index],
+            target.at[place(number, owner)],
+            send.at[number],
+            recv.at[number],
+            device_id=(other, group),
+            device_id_type=MESH,
+        )
+
+    for number in range(len(items)):
+        copy(number, me).start()
+    for number in range(len(items)):
+        block, index = items[number][:2]
+        target[place(number, me), :] = block[index]
+    for number in range(len(items)):
+        copy(number, other).wait_recv()
+    for number in range(len(items)):
+        copy(number, me).wait_send()
+
+
+def gather_step(count, masks, blocks, step):
+    arrived, filled = [], []
+    for part, order in enumerate(gather_orders(count)):
+        arrived.append(across(count, order[step], blocks[part]))
+        filled.append([mask ^ order[step] for mask in masks[part]])
+    return arrived, filled
+
+
+def gather_join(count, collective, masks, blocks, filled, arrived):
+    slots = []
+    for part in (0, 1):
+        slots += [(part, masks[part]), (part, filled[part])]
+    held = [block for pair in zip(blocks, arrived) for block in pair]
+    half, width = held[0].shape[1:]
     return pl.pallas_call(
-        functools.partial(return_kernel, count, spans),
-        out_shape=jax.ShapeDtypeStruct((rows, width), parts.dtype),
-        in_specs=[ANY],
-        out_specs=ANY,
-        scratch_shapes=[DMA((pieces * count,)), DMA((pieces * count,))],
-        compiler_params=pltpu.CompilerParams(collective_id=collective, has_side_effects=True),
-        cost_estimate=cost(12),
-    )(parts)
-
-
-def total_kernel(count, groups, values, result, near, far, send, recv, far_send, far_recv):
+        functools.partial(join_kernel, count, slots),
+        out_shape=jax.ShapeDtypeStruct((count * 2 * half, width), BF16),
+        in_specs=[VMEM] * len(held),
+        out_specs=VMEM,
+        scratch_shapes=[DMA((count,)), DMA((count,))],
+        compiler_params=pltpu.CompilerParams(
+            collective_id=collective, has_side_effects=True, vmem_limit_bytes=VMEM_LIMIT
+        ),
+        cost_estimate=cost(13),
+    )(*held)
+
+
+def last_kernel(
+    count, groups, values, parts, result, columns, near, far, send, recv, far_send, far_recv, part_send, part_recv
+):
     me = lax.axis_index("ctx")
     group = lax.axis_index("fsdp")
     others = [lax.rem(group + step, groups) for step in range(1, groups)]
@@ -354,6 +385,7 @@
         )
         item.start()
         copies.append(item)
+    finish = trade(count, me, group, incoming(qkv_spans, count), parts, columns, part_send, part_recv)
     near[me] = values[...]
     for item in copies:
         item.wait()
@@ -379,15 +411,20 @@
     for index in range(1, groups):
         summed = summed + far[index]
     result[...] = summed
-
-
-def total(count, groups, collective, values):
+    finish()
+
+
+def last(count, groups, collective, values, parts, width):
     shape = values.shape
+    pieces = len(qkv_spans(count, 0, True))
     return pl.pallas_call(
-        functools.partial(total_kernel, count, groups),
-        out_shape=jax.ShapeDtypeStruct(shape, F32),
-        in_specs=[VMEM],
-        out_specs=VMEM,
+        functools.partial(last_kernel, count, groups),
+        out_shape=[
+            jax.ShapeDtypeStruct(shape, F32),
+            jax.ShapeDtypeStruct((parts.shape[1], width), BF16),
+        ],
+        in_specs=[VMEM, ANY],
+        out_specs=[VMEM, ANY],
         scratch_shapes=[
             pltpu.VMEM((count,) + shape, F32),
             pltpu.VMEM((groups,) + shape, F32),
@@ -395,22 +432,19 @@
             DMA((count,)),
             DMA((groups,)),
             DMA((groups,)),
+            DMA((pieces * count,)),
+            DMA((pieces * count,)),
         ],
         compiler_params=pltpu.CompilerParams(collective_id=collective, has_side_effects=True),
-        cost_estimate=cost(12),
-    )(values)
-
-
-def product_scatter_kernel(
-    count, flipped, left, right, result, kept, near_out, near_in, far_out, far_in, ns, nr, fs, fr
-):
-    me = lax.axis_index("ctx")
-    group = lax.axis_index("fsdp")
-    rows, width = result.shape
+        cost_estimate=cost(14),
+    )(values, parts)
+
+
+def product_scatter(count, me, group, flipped, left, right, done, kept, near_out, near_in, far_out, far_in, ns, nr, fs, fr):
+    rows, width = kept.shape
     half = rows // 2
     bits = bits_of(count)
     orders = [bits[1:][::-1], bits[1:]]
-    greet([(flip(me, bit), group) for bit in bits])
     tile = min(512, width)
 
     def product(slot, store):
@@ -420,9 +454,7 @@
         def step(index, carry):
             columns = pl.ds(pl.multiple_of(index * tile, tile), tile)
             if flipped:
-                value = lax.dot_general(
-                    block, right[columns, :], (((1,), (1,)), ((), ())), preferred_element_type=F32
-                )
+                value = nt(block, right[columns, :])
             else:
                 value = jnp.dot(block, right[:, columns], preferred_element_type=F32)
             store(columns, value)
@@ -443,13 +475,16 @@
             device_id_type=MESH,
         )
 
+    def number(part, pair):
+        return part * (count // 2 - 1) + pair - 1
+
     def far(part, pair):
-        number = part * (count // 2) + pair
+        index = number(part, pair)
         return pltpu.make_async_remote_copy(
-            far_out.at[number],
-            far_in.at[number],
-            fs.at[number],
-            fr.at[number],
+            far_out.at[index],
+            far_in.at[index],
+            fs.at[index],
+            fr.at[index],
             device_id=(flip(me, first(part, 2 * pair)), group),
             device_id_type=MESH,
         )
@@ -463,71 +498,324 @@
         return found
 
     def settle(part, pair):
-        span_rows = pl.ds(part * half, half)
-        value = kept[pair, span_rows, :]
+        if pair == 0:
+            value = kept[pl.ds(part * half, half), :]
+        else:
+            value = far_out[number(part, pair)].astype(F32)
         for other in needs(part, pair):
             far(part, other).wait_recv()
-            value = value + far_in[part * (count // 2) + other].astype(F32)
+            value = value + far_in[number(part, other)].astype(F32)
         if pair == 0:
-            result[span_rows, :] = value
+            done(part, value)
         else:
-            far_out[part * (count // 2) + pair] = value.astype(BF16)
+            far_out[number(part, pair)] = value.astype(BF16)
             far(part, pair).start()
 
     pairs = list(range(count // 2))[::-1]
-    for pair in pairs:
-
-        def store_near(columns, value):
+
+    def send_near(pair):
+        def store(columns, value):
             near_out[pair, :, columns] = value.astype(BF16)
 
-        def store_kept(columns, value):
-            kept[pair, :, columns] = value
-
-        product(2 * pair + 1, store_near)
+        product(2 * pair + 1, store)
         near(pair).start()
-        product(2 * pair, store_kept)
+
+    def sum_near(pair):
         near(pair).wait_recv()
-        kept[pair] = kept[pair] + near_in[pair].astype(F32)
+
+        def store(columns, value):
+            value = value + near_in[pair, :, columns].astype(F32)
+            if pair == 0:
+                kept[:, columns] = value
+            else:
+                for part in (0, 1):
+                    far_out[number(part, pair), :, columns] = value[part * half : (part + 1) * half].astype(BF16)
+
+        product(2 * pair, store)
         for part in (0, 1):
             if pair and not needs(part, pair):
-                settle(part, pair)
-    for pair in pairs:
-        for part in (0, 1):
-            if not pair or needs(part, pair):
-                settle(part, pair)
-    for pair in pairs:
-        near(pair).wait_send()
-        for part in (0, 1):
+                far(part, pair).start()
+
+    def begin():
+        send_near(pairs[0])
+        for pair in pairs:
             if pair:
-                far(part, pair).wait_send()
-
-
-def product_scatter(count, collective, left, right, flipped):
-    tokens, depth = left.shape
-    width = right.shape[0] if flipped else right.shape[1]
-    rows = tokens // count
+                send_near(pair - 1)
+            sum_near(pair)
+
+    def end():
+        for pair in pairs:
+            for part in (0, 1):
+                if needs(part, pair):
+                    settle(part, pair)
+        for pair in pairs:
+            near(pair).wait_send()
+            for part in (0, 1):
+                if pair:
+                    far(part, pair).wait_send()
+
+    return begin, end
+
+
+def scatter_scratch(count, rows, width):
     pairs = count // 2
+    links = 2 * (pairs - 1)
+    return [
+        pltpu.VMEM((rows, width), F32),
+        pltpu.VMEM((pairs, rows, width), BF16),
+        pltpu.VMEM((pairs, rows, width), BF16),
+        pltpu.VMEM((links, rows // 2, width), BF16),
+        pltpu.VMEM((links, rows // 2, width), BF16),
+        DMA((pairs,)),
+        DMA((pairs,)),
+        DMA((links,)),
+        DMA((links,)),
+    ]
+
+
+SCATTER = 9
+
+
+def comm_params(collective):
+    return pltpu.CompilerParams(
+        collective_id=collective, has_side_effects=True, vmem_limit_bytes=VMEM_LIMIT
+    )
+
+
+def row_blocks(first, count, step):
+    def body(index, carry):
+        step(pl.multiple_of(first + index * 32, 32), pl.multiple_of(index * 32, 32))
+        return carry
+
+    lax.fori_loop(0, count // 32, body, 0)
+
+
+def norm_back(values, gain, grad):
+    scale = lax.rsqrt(jnp.mean(values * values, axis=-1, keepdims=True) + EPS)
+    scaled = values * scale
+    pushed = grad * gain
+    back = scale * (pushed - scaled * jnp.mean(pushed * scaled, axis=-1, keepdims=True))
+    return back, jnp.sum(grad * scaled, axis=0, keepdims=True)
+
+
+def norm_rows(values, gain):
+    return values * lax.rsqrt(jnp.mean(values * values, axis=-1, keepdims=True) + EPS) * gain
+
+
+def middle_kernel(count, left, right, hidden, gain, middle, gathered, own_rows, sums, *scratch):
+    me = lax.axis_index("ctx")
+    group = lax.axis_index("fsdp")
+    rows = middle.shape[0]
+    half = rows // 2
+    greet([(flip(me, bit), group) for bit in bits_of(count)])
+    start, finish = gather_rows(count, me, group, own_rows, gathered, *scratch[SCATTER:])
+
+    def done(part, value):
+        sums[...] = value
+
+        def step(row, place):
+            total_rows = hidden[pl.ds(row, 32), :].astype(F32) + sums[pl.ds(place, 32), :]
+            middle[pl.ds(row, 32), :] = total_rows
+            own_rows[pl.ds(row, 32), :] = norm_rows(total_rows, gain[...]).astype(BF16)
+
+        row_blocks(part * half, half, step)
+        start(part)
+
+    begin, end = product_scatter(count, me, group, False, left, right, done, *scratch[:SCATTER])
+    begin()
+    end()
+    finish()
+
+
+def gather_scratch(count):
+    return [DMA((2 * count,)), DMA((2 * count,)), DMA((2,))]
+
+
+def middle_and_second(count, collective, left, right, hidden, gain):
+    rows, width = hidden.shape
     return pl.pallas_call(
-        functools.partial(product_scatter_kernel, count, flipped),
-        out_shape=jax.ShapeDtypeStruct((rows, width), F32),
-        in_specs=[VMEM, VMEM],
+        functools.partial(middle_kernel, count),
+        out_shape=[
+            jax.ShapeDtypeStruct((rows, width), F32),
+            jax.ShapeDtypeStruct((count * rows, width), BF16),
+        ],
+        in_specs=[VMEM] * 4,
+        out_specs=[VMEM, ANY],
+        scratch_shapes=[pltpu.VMEM((rows, width), BF16), pltpu.VMEM((rows // 2, width), F32)]
+        + scatter_scratch(count, rows, width)
+        + gather_scratch(count),
+        compiler_params=comm_params(collective),
+        cost_estimate=cost(80, 2 * left.shape[0] * left.shape[1] * width),
+    )(left, right, hidden, gain)
+
+
+def back_kernel(
+    count,
+    left,
+    right,
+    middle,
+    cotangent,
+    gain,
+    attended,
+    out_weight,
+    d_middle,
+    d_gain,
+    d_attended,
+    d_out,
+    own_rows,
+    sums,
+    gathered,
+    turned,
+    out_sum,
+    *scratch,
+):
+    me = lax.axis_index("ctx")
+    group = lax.axis_index("fsdp")
+    rows, width = middle.shape
+    half = rows // 2
+    greet([(flip(me, bit), group) for bit in bits_of(count)])
+    start, finish = gather_rows(count, me, group, own_rows, gathered, *scratch[SCATTER:])
+    d_gain[...] = jnp.zeros_like(d_gain)
+
+    def done(part, value):
+        sums[...] = value
+
+        def step(row, place):
+            span_rows = pl.ds(row, 32)
+            back, gain_part = norm_back(middle[span_rows, :], gain[...], sums[pl.ds(place, 32), :])
+            back = back + cotangent[span_rows, :].astype(F32)
+            d_middle[span_rows, :] = back
+            own_rows[span_rows, :] = back.astype(BF16)
+            d_gain[...] += gain_part
+
+        row_blocks(part * half, half, step)
+        start(part)
+
+    begin, end = product_scatter(count, me, group, True, left, right, done, *scratch[:SCATTER])
+    begin()
+    out_sum[...] = jnp.zeros_like(out_sum)
+
+    def turn(index, carry):
+        span_rows = pl.ds(pl.multiple_of(index * 256, 256), 256)
+        turned[:, span_rows] = attended[span_rows, :].astype(F32).T.astype(BF16)
+        return carry
+
+    lax.fori_loop(0, attended.shape[0] // 256, turn, 0)
+    end()
+
+    def arrived(row, ref, place):
+        block = ref[pl.ds(place, half), :]
+        d_attended[pl.ds(row, half), :] = nt(block, out_weight[...]).astype(BF16)
+        if half % 128 == 0:
+            out_sum[...] += jnp.dot(turned[:, pl.ds(row, half)], block, preferred_element_type=F32)
+
+    finish(arrived)
+    if half % 128:
+        out_sum[...] = jnp.dot(turned[...], gathered[...], preferred_element_type=F32)
+    d_out[...] = out_sum[...].astype(BF16)
+
+
+def back_through_middle(count, collective, left, right, middle, cotangent, gain, attended, out_weight):
+    rows, width = middle.shape
+    tokens, wide = attended.shape
+    shape = jax.ShapeDtypeStruct
+    return pl.pallas_call(
+        functools.partial(back_kernel, count),
+        out_shape=[
+            shape((rows, width), F32),
+            shape((1, width), F32),
+            shape((tokens, wide), BF16),
+            shape((wide, width), BF16),
+        ],
+        in_specs=[VMEM] * 7,
+        out_specs=[VMEM] * 4,
+        scratch_shapes=[
+            pltpu.VMEM((rows, width), BF16),
+            pltpu.VMEM((rows // 2, width), F32),
+            pltpu.VMEM((tokens, width), BF16),
+            pltpu.VMEM((wide, tokens), BF16),
+            pltpu.VMEM((wide, width), F32),
+        ]
+        + scatter_scratch(count, rows, width)
+        + gather_scratch(count),
+        compiler_params=comm_params(collective),
+        cost_estimate=cost(85, 2 * left.shape[0] * left.shape[1] * width),
+    )(left, right, middle, cotangent, gain, attended, out_weight)
+
+
+def input_kernel(
+    count, left, right, hidden, d_middle, gain, parts, d_hidden, d_gain, columns, sums, send, recv, *scratch
+):
+    me = lax.axis_index("ctx")
+    group = lax.axis_index("fsdp")
+    half = hidden.shape[0] // 2
+    greet(everyone(count, me, group))
+    finish = trade(count, me, group, incoming(mlp_spans, count), parts, columns, send, recv)
+    d_gain[...] = jnp.zeros_like(d_gain)
+
+    def done(part, value):
+        sums[...] = value
+
+        def step(row, place):
+            span_rows = pl.ds(row, 32)
+            values = hidden[span_rows, :].astype(F32)
+            back, gain_part = norm_back(values, gain[...], sums[pl.ds(place, 32), :])
+            d_hidden[span_rows, :] = d_middle[span_rows, :] + back
+            d_gain[...] += gain_part
+
+        row_blocks(part * half, half, step)
+
+    begin, end = product_scatter(count, me, group, True, left, right, done, *scratch)
+    begin()
+    end()
+    finish()
+
+
+def back_to_input(count, collective, left, right, hidden, d_middle, gain, parts):
+    rows, width = hidden.shape
+    shape = jax.ShapeDtypeStruct
+    return pl.pallas_call(
+        functools.partial(input_kernel, count),
+        out_shape=[
+            shape((rows, width), F32),
+            shape((1, width), F32),
+            shape((parts.shape[1], 2 * FF), BF16),
+        ],
+        in_specs=[VMEM] * 5 + [ANY],
+        out_specs=[VMEM, VMEM, ANY],
+        scratch_shapes=[pltpu.VMEM((rows // 2, width), F32), DMA((2 * count,)), DMA((2 * count,))]
+        + scatter_scratch(count, rows, width),
+        compiler_params=comm_params(collective),
+        cost_estimate=cost(60, 2 * left.shape[0] * left.shape[1] * width),
+    )(left, right, hidden, d_middle, gain, parts)
+
+
+def output_kernel(count, left, right, middle, output, *scratch):
+    me = lax.axis_index("ctx")
+    group = lax.axis_index("fsdp")
+    half = middle.shape[0] // 2
+    greet([(flip(me, bit), group) for bit in bits_of(count)])
+
+    def done(part, value):
+        span_rows = pl.ds(part * half, half)
+        output[span_rows, :] = (middle[span_rows, :] + value).astype(BF16)
+
+    begin, end = product_scatter(count, me, group, False, left, right, done, *scratch)
+    begin()
+    end()
+
+
+def output_rows(count, collective, left, right, middle):
+    rows, width = middle.shape
+    return pl.pallas_call(
+        functools.partial(output_kernel, count),
+        out_shape=jax.ShapeDtypeStruct((rows, width), BF16),
+        in_specs=[VMEM] * 3,
         out_specs=VMEM,
-        scratch_shapes=[
-            pltpu.VMEM((pairs, rows, width), F32),
-            pltpu.VMEM((pairs, rows, width), BF16),
-            pltpu.VMEM((pairs, rows, width), BF16),
-            pltpu.VMEM((2 * pairs, rows // 2, width), BF16),
-            pltpu.VMEM((2 * pairs, rows // 2, width), BF16),
-            DMA((pairs,)),
-            DMA((pairs,)),
-            DMA((2 * pairs,)),
-            DMA((2 * pairs,)),
-        ],
-        compiler_params=pltpu.CompilerParams(
-            collective_id=collective, has_side_effects=True, vmem_limit_bytes=VMEM_LIMIT
-        ),
-        cost_estimate=cost(45, 2 * tokens * depth * width),
-    )(left, right)
+        scratch_shapes=scatter_scratch(count, rows, width),
+        compiler_params=comm_params(collective),
+        cost_estimate=cost(45, 2 * left.shape[0] * left.shape[1] * width),
+    )(left, right, middle)
 
 
 def swap_halves(value):
@@ -781,25 +1069,15 @@
     )(runs, raw, d_queries, d_keys, d_values, cosine, sine, q_gain, k_gain, share)
 
 
-def norm_back(values, gain, grad):
-    scale = lax.rsqrt(jnp.mean(values * values, axis=-1, keepdims=True) + EPS)
-    scaled = values * scale
-    pushed = grad * gain
-    back = scale * (pushed - scaled * jnp.mean(pushed * scaled, axis=-1, keepdims=True))
-    return back, jnp.sum(grad * scaled, axis=0)
-
-
-def norm_rows(values, gain):
-    return values * lax.rsqrt(jnp.mean(values * values, axis=-1, keepdims=True) + EPS) * gain
-
-
 def rotary(tokens):
-    index = jnp.arange(tokens, dtype=jnp.int32)
-    place = jnp.where(index < PROMPT, index, PROMPT + (index - PROMPT) % CONT).astype(F32)
-    exponent = jnp.arange(HEAD // 2, dtype=F32) * (2.0 / HEAD)
-    angles = place[:, None] * jnp.power(ROPE_BASE, -exponent)[None, :]
-    cosine, sine = jnp.cos(angles), jnp.sin(angles)
-    return jnp.concatenate([cosine, cosine], axis=1), jnp.concatenate([-sine, sine], axis=1)
+    index = np.arange(tokens)
+    place = np.where(index < PROMPT, index, PROMPT + (index - PROMPT) % CONT).astype(np.float32)
+    exponent = np.arange(HEAD // 2, dtype=np.float32) * np.float32(2.0 / HEAD)
+    inverse = np.power(np.float32(ROPE_BASE), -exponent).astype(np.float32)
+    angles = place[:, None] * inverse[None, :]
+    cosine, sine = np.cos(angles), np.sin(angles)
+    tables = np.concatenate([cosine, cosine], axis=1), np.concatenate([-sine, sine], axis=1)
+    return tuple(jnp.asarray(table, F32) for table in tables)
 
 
 def body(
@@ -837,31 +1115,45 @@
         return lax.psum_scatter(values, "fsdp", scatter_dimension=0, tiled=True)
 
     w_out = gather_groups(out_weight, 0)
+    qkv_parts, mlp_parts = spread(count, 1, qkv_weight, gate_up)
+    qkv_parts, w_out = lax.optimization_barrier((qkv_parts, w_out))
+    w_qkv = gather_groups(qkv_parts, 1).reshape(width, -1)
+    normed_local = norm_rows(hidden, attn_gain).astype(BF16)
+    normed_local, qkv_parts = lax.optimization_barrier((normed_local, qkv_parts))
+    normed, all_runs = opening(count, 2, normed_local, runs)
+    mlp_parts, w_qkv, normed, upstream = lax.optimization_barrier((mlp_parts, w_qkv, normed, cotangent[0]))
+    w_gu = gather_groups(mlp_parts, 1).reshape(width, -1)
     w_down = gather_groups(down_weight, 0)
-    qkv_parts = spread_qkv(count, 1, qkv_weight)
-    normed_local = norm_rows(hidden, attn_gain).astype(BF16)
-    normed, all_runs, mlp_parts = opening(count, 2, normed_local, runs, gate_up)
-    w_qkv = gather_groups(qkv_parts, 1).reshape(width, -1)
-    w_gu = gather_groups(mlp_parts, 1).reshape(width, -1)
     run_order = all_runs[:, 0, : rows // RUN].reshape(-1)
     cosine, sine = rotary(tokens)
     q_gain_row = query_norm_gain[None, :]
     k_gain_row = k_gain[None, :]
 
-    joined = jnp.dot(normed, w_qkv, preferred_element_type=F32)
+    blocks, masks = [upstream[None, : rows // 2], upstream[None, rows // 2 :]], [[0], [0]]
+    chip_steps = len(bits_of(count)) - 1
+    for step in range(chip_steps - 1):
+        arrived, filled = gather_step(count, masks, blocks, step)
+        if step == 0:
+            joined = jnp.dot(normed, w_qkv, preferred_element_type=F32)
+            joined, arrived = lax.optimization_barrier((joined, arrived))
+        blocks = [jnp.concatenate(pair) for pair in zip(blocks, arrived)]
+        masks = [held + more for held, more in zip(masks, filled)]
+    arrived, filled = gather_step(count, masks, blocks, chip_steps - 1)
     attended, raw, queries, keys, values, mixed, lse = attention(
         heads, run_order, joined, cosine, sine, q_gain_row, k_gain_row
     )
-    middle = hidden + product_scatter(count, 3, attended, w_out, False)
-    second = gather_ctx(count, 4, norm_rows(middle, mlp_gain).astype(BF16))
+    attended, arrived = lax.optimization_barrier((attended, arrived))
+    middle, second = middle_and_second(count, 3, attended, w_out, hidden_in[0], mlp_gain[None, :])
     both = jnp.dot(second, w_gu, preferred_element_type=F32)
     own = both.shape[1] // 2
     gate, up = both[:, :own], both[:, own:]
     sigmoid = jax.nn.sigmoid(gate)
     activated = (gate * sigmoid * up).astype(BF16)
 
-    upstream = gather_ctx(count, 5, cotangent[0])
+    activated, arrived = lax.optimization_barrier((activated, arrived))
+    upstream = gather_join(count, 5, masks, blocks, filled, arrived)
     d_down = jnp.dot(activated.T, upstream, preferred_element_type=F32).astype(BF16)
+    d_down, upstream = lax.optimization_barrier((d_down, upstream))
     d_down = scatter_groups(d_down)
     d_activated = lax.dot_general(
         upstream, w_down, (((1,), (1,)), ((), ())), preferred_element_type=F32
@@ -873,20 +1165,14 @@
     def weight_grad(left, right):
         grad = lax.dot_general(left, right, (((0,), (0,)), ((), ())), preferred_element_type=F32)
         grad = grad.astype(BF16).reshape(count, groups, -1, right.shape[1])
-        return scatter_groups(grad.transpose(1, 0, 2, 3).reshape(groups * count, -1, right.shape[1]))
-
-    gu_parts = weight_grad(second, d_both)
-    d_second = product_scatter(count, 6, d_both, w_gu, True)
-    middle_back, mlp_gain_grad = norm_back(middle, mlp_gain, d_second)
-    d_middle = cotangent[0].astype(F32) + middle_back
-    middle_low = gather_ctx(count, 7, d_middle.astype(BF16))
-    d_out = lax.dot_general(
-        attended, middle_low, (((0,), (0,)), ((), ())), preferred_element_type=F32
-    ).astype(BF16)
-    d_out = scatter_groups(d_out)
-    d_attended = lax.dot_general(
-        middle_low, w_out, (((1,), (1,)), ((), ())), preferred_element_type=F32
-    ).astype(BF16)
+        return grad.transpose(1, 0, 2, 3).reshape(groups * count, -1, right.shape[1])
+
+    gu_parts, d_both = lax.optimization_barrier((weight_grad(second, d_both), d_both))
+    gu_parts = scatter_groups(gu_parts)
+    d_middle, mlp_gain_grad, d_attended, d_out = back_through_middle(
+        count, 6, d_both, w_gu, middle, cotangent[0], mlp_gain[None, :], attended, w_out
+    )
+    d_attended, d_down = lax.optimization_barrier((d_attended, d_down))
     d_queries, d_keys, d_values = attention_back(
         heads, run_order, d_attended, queries, keys, values, mixed, lse
     )
@@ -900,21 +1186,25 @@
     d_joined, q_gain_grad, k_gain_grad = joined_back(
         heads, run_order, raw, d_queries, d_keys, d_values, cosine, sine, q_gain_row, k_gain_row, share
     )
-    qkv_grad_parts = weight_grad(normed, d_joined)
-    d_normed = product_scatter(count, 8, d_joined, w_qkv, True)
-    output = middle + product_scatter(count, 9, activated, w_down, False)
-    hidden_back, attn_gain_grad = norm_back(hidden, attn_gain, d_normed)
-    d_hidden = d_middle + hidden_back
-
-    d_gate_up = return_columns(count, 10, mlp_spans, 2 * FF, gu_parts)
-    qkv_width = qkv_weight.shape[1]
-    d_qkv = return_columns(count, 11, qkv_spans, qkv_width, qkv_grad_parts)
-    small = jnp.concatenate([attn_gain_grad, mlp_gain_grad, q_gain_grad[0], k_gain_grad[0]])
+    qkv_grad_parts, d_joined = lax.optimization_barrier((weight_grad(normed, d_joined), d_joined))
+    qkv_grad_parts, gu_parts = lax.optimization_barrier((qkv_grad_parts, gu_parts))
+    qkv_grad_parts = scatter_groups(qkv_grad_parts)
+    d_hidden, attn_gain_grad, d_gate_up = back_to_input(
+        count, 8, d_joined, w_qkv, hidden_in[0], d_middle, attn_gain[None, :], gu_parts
+    )
+    d_out, qkv_grad_parts, d_hidden, activated = lax.optimization_barrier(
+        (d_out, qkv_grad_parts, d_hidden, activated)
+    )
+    d_out = scatter_groups(d_out)
+    output = output_rows(count, 9, activated, w_down, middle)
+
+    small = jnp.concatenate([attn_gain_grad[0], mlp_gain_grad[0], q_gain_grad[0], k_gain_grad[0]])
     padded = -(-small.shape[0] // 1024) * 1024
     small = jnp.pad(small, (0, padded - small.shape[0])).reshape(-1, 128)
-    summed = total(count, groups, 12, small).reshape(-1)
+    summed, d_qkv = last(count, groups, 11, small, qkv_grad_parts, qkv_weight.shape[1])
+    summed = summed.reshape(-1)
     return (
-        output.astype(BF16)[None],
+        output[None],
         d_hidden[None],
         summed[:width],
         d_qkv.astype(F32),

time: 703 us -> 593 us (0.84)
  waiting for transfers between devices: 59.2 us -> 9.81 us
  Pallas kernels: 468 us -> 443 us
  matrix products: 99.4 us -> 77.4 us
  other arithmetic: 38 us -> 18.5 us
    reduce_scatter x4, waiting for transfers between devices: 53 us -> 0.05 us  [scatter_groups(): return lax.psum_scatter(values, 'fsdp', scatter_dimension=0, tiled=True)]
    pallas_call x1, Pallas kernels: 58.7 us -> 42.1 us  [opening(): pl.pallas_call(functools.partial(opening_kernel, count), out_shape=[jax.S...]
    dot_general x2 -> x0, matrix products: 13.7 us -> none  [the longest x1 6.97 us: body(): lax.dot_general(middle_low, w_out, (((1,), (1,)), ((), ())), preferred_el...]
    pallas_call x11 -> x7, Pallas kernels: 358 us -> 350 us  [the longest x1 98.1 us: back_through_middle(): pl.pallas_call(functools.partial(back_kernel, count), out_shape=[shape((r...]
  transfers between devices with their start and end apart: 8 -> 12, of which waited for: 2 -> 6; matrix products, arithmetic and copies ran while one was open for 16% -> 18% of each run, Pallas kernels for 50% -> 75%
where the time goes in v2:
time: 593 us; the launch traced here: 588 us
  Pallas kernels  443 us (75%)
  matrix products  77.4 us (13%)
  other arithmetic  18.5 us (3%)
  local copies, waits for them, and re-layouts  18.3 us (3%)
  between operations  14.9 us (3%)
  waiting for transfers between devices  9.81 us (2%)
    pallas_call x1, Pallas kernels, back_through_middle(): pl.pallas_call(functools.partial(back_kernel, count), out_shape=[shape((r...  98.1 us
    pallas_call x1, Pallas kernels, middle_and_second(): pl.pallas_call(functools.partial(middle_kernel, count), out_shape=[jax.Sh...  85.6 us
    pallas_call x1, Pallas kernels, back_to_input(): pl.pallas_call(functools.partial(input_kernel, count), out_shape=[shape((...  61.5 us
    pallas_call x1, Pallas kernels, output_rows(): pl.pallas_call(functools.partial(output_kernel, count), out_shape=jax.Sha...  47.6 us
    pallas_call x1, Pallas kernels, opening(): pl.pallas_call(functools.partial(opening_kernel, count), out_shape=[jax.S...  42.1 us
    pallas_call x1, Pallas kernels, spread(): pl.pallas_call(functools.partial(spread_kernel, count), out_shape=[jax.Sh...  28.6 us
    dot_general x2, matrix products, weight_grad(): lax.dot_general(left, right, (((0,), (0,)), ((), ())), preferred_element_...  24.2 us
    pallas_call x1, Pallas kernels, attention(): pl.pallas_call(functools.partial(attention_kernel, heads), out_shape=[sha...  20.5 us
  transfers between devices with their start and end apart: 12, of which 6 were waited for; matrix products, arithmetic and copies ran while one was open for 18% of the time, Pallas kernels for 75%

profile of v2, /device:TPU:0, one launch (start us, length us, event | category | flops | bytes accessed | tf_op | source)
XLA Modules:
  0.0 587.6 jit_solution(1358650651868871709)
XLA Ops:
  8.0 28.6 %shard_map.213 = (bf16[8,64,512]{2,1,0:T(8,128)(2,1)}, bf16[8,64,1536]{2,1,0:T(8,128)(2,1)}) custom-call(bf16[64,4096]{1,0:T(8,128)(2,1)} %qkv.1, bf16[64,12288]{1,0:T(8,128)(2,1)} %mlp.1), custom_call_target="tpu_custom_call" | custom-call | bytes 89600000 | tf_op jit(solution)/shard_map/pallas_call | solution.py:257
  36.6 3.7 all-gather.5.cloned.1.call-done.right.out_weight
  44.0 2.5 fusion.7.normed
  46.5 42.1 %shard_map.214 = (bf16[2048,2048]{1,0:T(8,128)(2,1)}, s32[8,8,128]{2,1,0:T(8,128)}) custom-call(bf16[256,2048]{1,0:T(8,128)(2,1)} %fusion.7.normed, s32[1,8,128]{2,1,0:T(8,128)} %scatter.4.runs), custom_call_target="tpu_custom_call" | custom-call | bytes 144000000 | tf_op jit(solution)/shard_map/pallas_call | solution.py:287
  91.9 10.9 %fusion.9.joined = f32[2048,512]{1,0:T(8,128)} fusion(bf16[2048,2048]{1,0:T(8,128)(2,1)} %get-tuple-element.86, bf16[2048,512]{1,0:T(8,128)(2,1)} %bitcast.82), kind=kOutput, calls=%fused_computation.39 | convolution fusion | flops 4294967296 | bytes 14680064 | tf_op jit(solution)/shard_map/dot_general | solution.py:1137
  108.4 20.5 %shard_map.215 = (bf16[2048,256]{1,0:T(8,128)(2,1)}, f32[2048,512]{1,0:T(8,128)}, bf16[16,256,128]{2,1,0:T(8,128)(2,1)}, bf16[2048,128]{1,0:T(8,128)(2,1)}, bf16...) custom-call(s32[64]{0:T(128)} %reshape_squeeze.3.runs, f32[2048,512]{1,0:T(8,128)} %fusion.9.joined, ...), custom_call_target="tpu_custom_call" | custom-call | bytes 48000000 | tf_op jit(solution)/shard_map/pallas_call | solution.py:912
  129.7 85.6 %shard_map.216 = (f32[256,2048]{1,0:T(8,128)}, bf16[2048,2048]{1,0:T(8,128)(2,1)}) custom-call(bf16[2048,256]{1,0:T(8,128)(2,1)} %get-tuple-element.93.left.attended, bf16[256,2048]{1,0:T(8,128)(2,1)} %all-gather.5.cloned.1.call-done.right.out_weight, bf16[256,2048]{1,0:T(8,128)(2,1)} %bitcast.64, f32[1,2048]{1,0:T(1,128)} %bitcast.84), custom_call_target="tpu_custom_call" | custom-call | flops 2147483648 | bytes 256000000 | tf_op jit(solution)/shard_map/pallas_call | solution.py:636
  215.4 17.4 %fusion.10 = f32[2048,1536]{1,0:T(8,128)S(1)} fusion(bf16[2048,2048]{1,0:T(8,128)(2,1)} %get-tuple-element.95, bf16[2048,1536]{1,0:T(8,128)(2,1)} %bitcast.80), kind=kOutput, calls=%fused_computation.40 | convolution fusion | flops 12884901888 | bytes 27262976 | tf_op jit(solution)/shard_map/dot_general | solution.py:1147
  232.8 4.5 copy-done
  239.4 14.0 %shard_map.217 = bf16[2048,2048]{1,0:T(8,128)(2,1)} custom-call(bf16[2,128,2048]{2,1,0:T(8,128)(2,1)} %copy-done.2, bf16[2,128,2048]{2,1,0:T(8,128)(2,1)} %collective-permute-done.2.refs_1_, bf16[2,128,2048]{2,1,0:T(8,128)(2,1)} %copy-done.1, bf16[2,128,2048]{2,1,0:T(8,128)(2,1)} %copy-done.5), custom_call_target="tpu_custom_call" | custom-call | bytes 41600000 | tf_op jit(solution)/shard_map/pallas_call | solution.py:356
  253.4 10.7 %convolution_convert_fusion.2 = bf16[768,2048]{1,0:T(8,128)(2,1)} fusion(bf16[2048,768]{1,0:T(8,128)(2,1)S(1)} %multiply_convert_fusion.left, bf16[2048,2048]{1,0:T(8,128)(2,1)} %shard_map.217), kind=kOutput, calls=%fused_computation.12 | convolution fusion | flops 6444023808 | bytes 14680064 | tf_op jit(solution)/shard_map/dot_general | solution.py:1155
  264.2 2.7 all-gather.11.cloned.1.call-done.right
  267.0 14.2 %fusion.2 = (bf16[2048,768]{1,0:T(8,128)(2,1)S(1)}, bf16[2048,768]{1,0:T(8,128)(2,1)S(1)}) fusion(f32[2048,1536]{1,0:T(8,128)} %copy-done, bf16[2048,2048]{1,0:T(8,128)(2,1)} %shard_map.217, bf16[768,2048]{1,0:T(8,128)(2,1)} %all-gather.11.cloned.1.call-done.right), kind=kOutput, calls=%fused_computation.5 | convolution fusion | flops 6466043904 | bytes 30408704 | tf_op jit(solution)/shard_map/dot_general | solution.py:1158
  281.2 15.5 %convolution_convert_fusion = bf16[2048,1536]{1,0:T(8,128)(2,1)S(1)} fusion(bf16[2048,2048]{1,0:T(8,128)(2,1)} %get-tuple-element.95, bf16[2048,768]{1,0:T(8,128)(2,1)S(1)} %get-tuple-element.139, bf16[2048,768]{1,0:T(8,128)(2,1)S(1)} %get-tuple-element.138), kind=kOutput, calls=%fused_computation.2 | convolution fusion | flops 12900630528 | bytes 20971520 | tf_op jit(solution)/shard_map/dot_general | solution.py:1166
  296.7 3.3 copy.27
  300.0 3.1 pad_maximum_fusion.left
  303.2 98.1 %shard_map.218 = (f32[256,2048]{1,0:T(8,128)}, f32[1,2048]{1,0:T(1,128)}, bf16[2048,256]{1,0:T(8,128)(2,1)}, bf16[256,2048]{1,0:T(8,128)(2,1)}) custom-call(bf16[2048,1536]{1,0:T(8,128)(2,1)} %pad_maximum_fusion.left, bf16[2048,1536]{1,0:T(8,128)(2,1)} %bitcast.81, f32[256,2048]{1,0:T(8,128)} %get-tuple-element.104.middle, bf16[256,2048]{1,0:T(8,128)(2,1)} %bitcast.68, ...), custom_call_target="tpu_custom_call" | custom-call | flops 12884901888 | bytes 272000000 | tf_op jit(solution)/shard_map/pallas_call | solution.py:722
  401.4 18.9 %shard_map.219 = (bf16[2048,256]{1,0:T(8,128)(2,1)}, f32[2048,128]{1,0:T(8,128)}, f32[2048,128]{1,0:T(8,128)}) custom-call(s32[64]{0:T(128)} %reshape_squeeze.3.runs, bf16[2048,256]{1,0:T(8,128)(2,1)} %get-tuple-element.109.d_attended, bf16[16,256,128]{2,1,0:T(8,128)(2,1)} %get-tuple-element.110.queries, bf16[2048,128]{1,0:T(8,128)(2,1)} %get-tuple-element.111.keys, ...), custom_call_target="tpu_custom_call" | custom-call | bytes 80000000 | tf_op jit(solution)/shard_map/pallas_call | solution.py:997
  420.8 11.4 %shard_map.220 = (bf16[2048,512]{1,0:T(8,128)(2,1)}, f32[1,128]{1,0:T(1,128)}, f32[1,128]{1,0:T(1,128)}) custom-call(s32[64]{0:T(128)} %reshape_squeeze.3.runs, f32[2048,512]{1,0:T(8,128)} %get-tuple-element.106.raw, bf16[2048,256]{1,0:T(8,128)(2,1)} %get-tuple-element.115.d_queries, f32[2048,128]{1,0:T(8,128)} %get-tuple-element.116.d_keys, ...), custom_call_target="tpu_custom_call" | custom-call | bytes 25600000 | tf_op jit(solution)/shard_map/pallas_call | solution.py:1061
  432.2 8.7 %convolution_convert_fusion.3 = bf16[2048,512]{1,0:T(8,128)(2,1)S(1)} fusion(bf16[2048,2048]{1,0:T(8,128)(2,1)} %get-tuple-element.86, bf16[2048,512]{1,0:T(8,128)(2,1)} %get-tuple-element.122.left), kind=kOutput, calls=%fused_computation.13 | convolution fusion | flops 4296015872 | bytes 12582912 | tf_op jit(solution)/shard_map/dot_general | solution.py:1166
  442.4 61.5 %shard_map.221 = (f32[256,2048]{1,0:T(8,128)}, f32[1,2048]{1,0:T(1,128)}, bf16[64,12288]{1,0:T(8,128)(2,1)}) custom-call(bf16[2048,512]{1,0:T(8,128)(2,1)} %get-tuple-element.122.left, bf16[2048,512]{1,0:T(8,128)(2,1)} %bitcast.83, bf16[256,2048]{1,0:T(8,128)(2,1)} %bitcast.65, f32[256,2048]{1,0:T(8,128)} %get-tuple-element.123.d_middle, ...), custom_call_target="tpu_custom_call" | custom-call | flops 4294967296 | bytes 192000000 | tf_op jit(solution)/shard_map/pallas_call | solution.py:777
  505.4 3.3 convert_element_type.49
  509.3 14.8 %shard_map.223 = (f32[40,128]{1,0:T(8,128)}, bf16[64,4096]{1,0:T(8,128)(2,1)}) custom-call(f32[40,128]{1,0:T(8,128)} %fusion.8.values, bf16[8,64,512]{2,1,0:T(8,128)(2,1)} %reduce-scatter.9.cloned.1.call-done.parts), custom_call_target="tpu_custom_call" | custom-call | bytes 44800000 | tf_op jit(solution)/shard_map/pallas_call | solution.py:420
  526.2 47.6 %shard_map.222 = bf16[256,2048]{1,0:T(8,128)(2,1)} custom-call(bf16[2048,768]{1,0:T(8,128)(2,1)} %copy-done.3, bf16[768,2048]{1,0:T(8,128)(2,1)} %all-gather.11.cloned.1.call-done.right, f32[256,2048]{1,0:T(8,128)} %get-tuple-element.104.middle), custom_call_target="tpu_custom_call" | custom-call | flops 6442450944 | bytes 144000000 | tf_op jit(solution)/shard_map/pallas_call | solution.py:810
  (77 shorter events, 29.0 us)
Async XLA Ops:
  7.2 81.6 %copy-start.6 = (bf16[1,256,2048]{2,1,0:T(8,128)(2,1)S(1)}, bf16[1,256,2048]{2,1,0:T(8,128)(2,1)}, u32[]{:S(2)}) copy-start(bf16[1,256,2048]{2,1,0:T(8,128)(2,1)} %param.27) | copy-start | bytes 3145732
  7.2 33.1 %all-gather.5.cloned.1.call-start = ((), (), s32[]{:S(2)}) async-start(), calls=%async_computation.4 | async-start | bytes 1310720 | tf_op jit(solution)/shard_map/all_gather | solution.py:1112
  7.9 80.7 %all-gather.7.cloned.1.call-start = ((), (), s32[]{:S(2)}) async-start(), calls=%async_computation.5 | async-start | bytes 2621440 | tf_op jit(solution)/shard_map/all_gather | solution.py:1112
  40.3 175.1 %all-gather.9.cloned.1.call-start = ((), (), s32[]{:S(2)}) async-start(), calls=%async_computation.6 | async-start | bytes 7864320 | tf_op jit(solution)/shard_map/all_gather | solution.py:1112
  88.7 178.3 %all-gather.11.cloned.1.call-start = ((), (), s32[]{:S(2)}) async-start(), calls=%async_computation.7 | async-start | bytes 3932160 | tf_op jit(solution)/shard_map/all_gather | solution.py:1112
  88.8 14.3 %collective-permute-start = (bf16[1,128,2048]{2,1,0:T(8,128)(2,1)S(1)}, bf16[1,128,2048]{2,1,0:T(8,128)(2,1)S(1)}, u32[]{:S(2)}, u32[]{:S(2)}) collective-permute-start(bf16[1,128,2048]{2,1,0:T(8,128)(2,1)S(1)} %get-tuple-element.141), channel_id=1, source_target_pairs={{0,8},{4,12},{8,0},{12,4},{16,24},{20,28},{24,16},{28,20},{1,9},{5... | collective-permute-start | bytes 1572872 | tf_op jit(solution)/shard_map/ppermute | solution.py:302
  90.5 14.0 %collective-permute-start.1 = (bf16[1,128,2048]{2,1,0:T(8,128)(2,1)S(1)}, bf16[1,128,2048]{2,1,0:T(8,128)(2,1)S(1)}, u32[]{:S(2)}, u32[]{:S(2)}) collective-permute-start(bf16[1,128,2048]{2,1,0:T(8,128)(2,1)S(1)} %get-tuple-element.140), channel_id=1, source_target_pairs={{0,16},{4,20},{8,24},{12,28},{16,0},{20,4},{24,8},{28,12},{1,17},{... | collective-permute-start | bytes 1572872 | tf_op jit(solution)/shard_map/ppermute | solution.py:302
  104.5 110.8 %copy-start.1 = (bf16[2,128,2048]{2,1,0:T(8,128)(2,1)}, bf16[2,128,2048]{2,1,0:T(8,128)(2,1)S(1)}, u32[]{:S(2)}) copy-start(bf16[2,128,2048]{2,1,0:T(8,128)(2,1)S(1)} %pad_maximum_fusion.2.refs_2_) | copy-start | bytes 3145732
  104.6 24.6 %collective-permute-start.3 = (bf16[2,128,2048]{2,1,0:T(8,128)(2,1)S(1)}, bf16[2,128,2048]{2,1,0:T(8,128)(2,1)S(1)}, u32[]{:S(2)}, u32[]{:S(2)}) collective-permute-start(bf16[2,128,2048]{2,1,0:T(8,128)(2,1)S(1)} %pad_maximum_fusion.2.refs_2_), channel_id=1, source_target_pairs={{0,8},{4,12},{8,0},{12,4},{16,24},{20,28},{24,16},{28,20},{1,9},{5... | collective-permute-start | bytes 3145736 | tf_op jit(solution)/shard_map/ppermute | solution.py:302
  105.2 110.2 %copy-start.2 = (bf16[2,128,2048]{2,1,0:T(8,128)(2,1)}, bf16[2,128,2048]{2,1,0:T(8,128)(2,1)S(1)}, u32[]{:S(2)}) copy-start(bf16[2,128,2048]{2,1,0:T(8,128)(2,1)S(1)} %pad_maximum_fusion.1.refs_0_) | copy-start | bytes 3145732
  105.2 24.5 %collective-permute-start.2 = (bf16[2,128,2048]{2,1,0:T(8,128)(2,1)S(1)}, bf16[2,128,2048]{2,1,0:T(8,128)(2,1)}, u32[]{:S(2)}, u32[]{:S(2)}) collective-permute-start(bf16[2,128,2048]{2,1,0:T(8,128)(2,1)S(1)} %pad_maximum_fusion.1.refs_0_), channel_id=1, source_target_pairs={{0,16},{4,20},{8,24},{12,28},{16,0},{20,4},{24,8},{28,12},{1,17},{... | collective-permute-start | bytes 3145736 | tf_op jit(solution)/shard_map/ppermute | solution.py:302
  106.8 294.6 %reduce-scatter.5.cloned.1.call-start = ((), (), s32[]{:S(2)}) async-start(), calls=%async_computation.8 | async-start | bytes 3932160 | tf_op jit(solution)/shard_map/reduce_scatter | solution.py:1115
  129.1 86.3 %copy-start.5 = (bf16[2,128,2048]{2,1,0:T(8,128)(2,1)}, bf16[2,128,2048]{2,1,0:T(8,128)(2,1)S(1)}, u32[]{:S(2)}) copy-start(bf16[2,128,2048]{2,1,0:T(8,128)(2,1)S(1)} %collective-permute-done.3.refs_3_) | copy-start | bytes 3145732
  239.4 14.0 %copy-start.3 = (bf16[2048,768]{1,0:T(8,128)(2,1)}, bf16[2048,768]{1,0:T(8,128)(2,1)S(1)}, u32[]{:S(2)}) copy-start(bf16[2048,768]{1,0:T(8,128)(2,1)S(1)} %multiply_convert_fusion.left) | copy-start | bytes 9437188
  264.2 178.2 %reduce-scatter.7.cloned.1.call-start = ((), (), s32[]{:S(2)}) async-start(), calls=%async_computation.9 | async-start | bytes 7864320 | tf_op jit(solution)/shard_map/reduce_scatter | solution.py:1115
  303.2 200.8 %reduce-scatter.9.cloned.1.call-start = ((), (), s32[]{:S(2)}) async-start(), calls=%async_computation.10 | async-start | bytes 2621440 | tf_op jit(solution)/shard_map/reduce_scatter | solution.py:1115
  442.4 132.6 %reduce-scatter.11.cloned.1.call-start = ((), (), s32[]{:S(2)}) async-start(), calls=%async_computation.11 | async-start | bytes 1310720 | tf_op jit(solution)/shard_map/reduce_scatter | solution.py:1115
  442.4 61.6 %copy-start.7 = (bf16[192,2048]{1,0:T(8,128)(2,1)S(1)}, bf16[192,2048]{1,0:T(8,128)(2,1)}, u32[]{:S(2)}) copy-start(bf16[192,2048]{1,0:T(8,128)(2,1)} %reduce-scatter.5.cloned.1.call-done) | copy-start | bytes 2359300
  503.9 4.7 copy-start.9
  503.9 4.7 copy-start.10
  503.9 4.7 copy-start.11
  504.0 4.7 copy-start.12
  526.2 47.6 %copy-start.8 = (f32[40,128]{1,0:T(8,128)S(1)}, f32[40,128]{1,0:T(8,128)}, u32[]{:S(2)}) copy-start(f32[40,128]{1,0:T(8,128)} %get-tuple-element.133) | copy-start | bytes 61444
  526.2 52.8 %copy-start.4 = (f32[256,2048]{1,0:T(8,128)S(1)}, f32[256,2048]{1,0:T(8,128)}, u32[]{:S(2)}) copy-start(f32[256,2048]{1,0:T(8,128)} %get-tuple-element.127) | copy-start | bytes 6291460
  (1 other events, 4.5 us)
Sparse Core Ops, SparseCore 0:
  9.6 30.6 all-gather.4
  41.8 45.4 all-gather.6
  88.9 114.8 all-gather.8
  205.2 61.6 all-gather.10
  269.7 58.8 reduce-scatter.4
  330.8 110.7 reduce-scatter.6
  444.4 44.3 reduce-scatter.8
  504.1 28.0 reduce-scatter.10

commit v3 on v2

--- a/solution.py
+++ b/solution.py
@@ -30,8 +30,8 @@
 VMEM_LIMIT = 60 * 2**20
 
 
-def cost(us, flops=0):
-    return pl.CostEstimate(flops=flops, bytes_accessed=int(us * 3.2e6), transcendentals=0)
+def cost(us):
+    return pl.CostEstimate(flops=0, bytes_accessed=int(us * 1e6), transcendentals=0)
 
 
 def flip(me, mask):
@@ -69,18 +69,19 @@
     return [bit for bit in order if slot & bit][-1]
 
 
-def gather_rows(count, me, group, source, target, send, recv, own):
-    rows = source.shape[0]
-    half = rows // 2
+def gather_rows(count, me, group, parts, source, target, send, recv, own=None):
+    rows = target.shape[0] // count
+    piece = rows // parts
     orders = gather_orders(count)
     copies = []
 
     def place(part, slot):
-        return pl.multiple_of(flip(me, slot) * rows + part * half, half)
+        return pl.multiple_of(flip(me, slot) * rows + part * piece, piece)
 
     def copy(part, slot, bit):
-        there = target.at[pl.ds(place(part, slot), half)]
-        origin = source.at[pl.ds(part * half, half)] if slot == 0 else there
+        there = target.at[pl.ds(place(part, slot), piece)]
+        own_place = slot == 0 and source is not None
+        origin = source.at[pl.ds(part * piece, piece)] if own_place else there
         number = part * count + (slot ^ bit)
         return pltpu.make_async_remote_copy(
             origin,
@@ -92,47 +93,52 @@
         )
 
     def keep(part):
-        there = target.at[pl.ds(place(part, 0), half)]
-        return pltpu.make_async_copy(source.at[pl.ds(part * half, half)], there, own.at[part])
+        there = target.at[pl.ds(place(part, 0), piece)]
+        return pltpu.make_async_copy(source.at[pl.ds(part * piece, piece)], there, own.at[part])
 
     def start(part):
-        for bit in orders[part]:
+        for bit in orders[part % 2]:
             item = copy(part, 0, bit)
             item.start()
             copies.append(item)
-        keep(part).start()
+        if source is not None:
+            keep(part).start()
 
     def wait(part, slot):
-        there = target.at[pl.ds(place(part, slot), half)]
+        there = target.at[pl.ds(place(part, slot), piece)]
         number = part * count + slot
         pltpu.make_async_remote_copy(
             there,
             there,
             send.at[number],
             recv.at[number],
-            device_id=(flip(me, last_bit(orders[part], slot)), group),
+            device_id=(flip(me, last_bit(orders[part % 2], slot)), group),
             device_id_type=MESH,
         ).wait_recv()
 
     def finish(arrived=None):
         waits = []
-        for part in (0, 1):
-            order = orders[part]
+        for part in range(parts):
+            order = orders[part % 2]
             for slot in range(1, count):
                 last = order.index(last_bit(order, slot))
-                waits.append((last, bin(slot).count("1"), part, slot))
-            if arrived:
-                arrived(place(part, 0), source, part * half)
-        for last, _, part, slot in sorted(waits):
+                waits.append((part // 2 + last, last, bin(slot).count("1"), part, slot))
+        if arrived:
+            for part in range(0, parts, 2):
+                arrived(place(part, 0), 2 * piece)
+        there = set()
+        for _, last, _, part, slot in sorted(waits):
             wait(part, slot)
-            for bit in orders[part][last + 1 :]:
+            for bit in orders[part % 2][last + 1 :]:
                 item = copy(part, slot, bit)
                 item.start()
                 copies.append(item)
-            if arrived:
-                arrived(place(part, slot), target, place(part, slot))
-        for part in (0, 1):
-            keep(part).wait()
+            there.add((part, slot))
+            if arrived and (part ^ 1, slot) in there:
+                arrived(place(part // 2 * 2, slot), 2 * piece)
+        for part in range(parts):
+            if source is not None:
+                keep(part).wait()
         for item in copies:
             item.wait_send()
 
@@ -275,7 +281,7 @@
     finish_runs = trade(
         count, me, group, lambda device, owner: [((0,), (owner,))], runs, all_runs, run_send, run_recv
     )
-    start, finish = gather_rows(count, me, group, normed, rows, send, recv, own)
+    start, finish = gather_rows(count, me, group, 2, normed, rows, send, recv, own)
     start(0)
     start(1)
     finish()
@@ -290,7 +296,7 @@
             jax.ShapeDtypeStruct((count * tokens, width), BF16),
             jax.ShapeDtypeStruct((count, 8, 128), jnp.int32),
         ],
-        in_specs=[ANY, ANY],
+        in_specs=[VMEM, ANY],
         out_specs=[ANY, ANY],
         scratch_shapes=[DMA((2 * count,)), DMA((2 * count,)), DMA((2,)), DMA((count,)), DMA((count,))],
         compiler_params=pltpu.CompilerParams(collective_id=collective, has_side_effects=True),
@@ -367,7 +373,24 @@
 
 
 def last_kernel(
-    count, groups, values, parts, result, columns, near, far, send, recv, far_send, far_recv, part_send, part_recv
+    count,
+    groups,
+    values,
+    parts,
+    attn_gain,
+    mlp_gain,
+    q_gain,
+    k_gain,
+    d_qkv,
+    columns,
+    near,
+    far,
+    send,
+    recv,
+    far_send,
+    far_recv,
+    part_send,
+    part_recv,
 ):
     me = lax.axis_index("ctx")
     group = lax.axis_index("fsdp")
@@ -410,22 +433,29 @@
     summed = far[0]
     for index in range(1, groups):
         summed = summed + far[index]
-    result[...] = summed
+    rows = attn_gain.shape[0]
+    attn_gain[...] = summed[:rows]
+    mlp_gain[...] = summed[rows : 2 * rows]
+    q_gain[...] = summed[2 * rows : 2 * rows + 1]
+    k_gain[...] = summed[2 * rows + 1 : 2 * rows + 2]
     finish()
-
-
-def last(count, groups, collective, values, parts, width):
+    d_qkv[...] = columns[...].astype(F32)
+
+
+def last(count, groups, collective, values, parts, width, columns):
     shape = values.shape
+    long, short = (width // 128, 128), (1, 128)
     pieces = len(qkv_spans(count, 0, True))
     return pl.pallas_call(
         functools.partial(last_kernel, count, groups),
         out_shape=[
-            jax.ShapeDtypeStruct(shape, F32),
-            jax.ShapeDtypeStruct((parts.shape[1], width), BF16),
+            jax.ShapeDtypeStruct(size, F32)
+            for size in (long, long, short, short, (parts.shape[1], columns))
         ],
         in_specs=[VMEM, ANY],
-        out_specs=[VMEM, ANY],
+        out_specs=[VMEM] * 5,
         scratch_shapes=[
+            pltpu.VMEM((parts.shape[1], columns), BF16),
             pltpu.VMEM((count,) + shape, F32),
             pltpu.VMEM((groups,) + shape, F32),
             DMA((count,)),
@@ -440,12 +470,15 @@
     )(values, parts)
 
 
-def product_scatter(count, me, group, flipped, left, right, done, kept, near_out, near_in, far_out, far_in, ns, nr, fs, fr):
+def product_scatter(
+    count, me, group, parts, flipped, left, right, done, kept, near_out, near_in, far_out, far_in, ns, nr, fs, fr
+):
     rows, width = kept.shape
-    half = rows // 2
+    piece = rows // parts
     bits = bits_of(count)
     orders = [bits[1:][::-1], bits[1:]]
     tile = min(512, width)
+    pairs = list(range(count // 2))[::-1]
 
     def product(slot, store):
         start = pl.multiple_of(flip(me, slot) * rows, rows)
@@ -463,7 +496,7 @@
         lax.fori_loop(0, width // tile, step, 0)
 
     def first(part, slot):
-        return [bit for bit in orders[part] if slot & bit][0]
+        return [bit for bit in orders[part % 2] if slot & bit][0]
 
     def near(pair):
         return pltpu.make_async_remote_copy(
@@ -491,7 +524,7 @@
 
     def needs(part, pair):
         found = []
-        for bit in orders[part]:
+        for bit in orders[part % 2]:
             if 2 * pair & bit:
                 break
             found.append((2 * pair ^ bit) // 2)
@@ -499,7 +532,7 @@
 
     def settle(part, pair):
         if pair == 0:
-            value = kept[pl.ds(part * half, half), :]
+            value = kept[pl.ds(part * piece, piece), :]
         else:
             value = far_out[number(part, pair)].astype(F32)
         for other in needs(part, pair):
@@ -511,14 +544,20 @@
             far_out[number(part, pair)] = value.astype(BF16)
             far(part, pair).start()
 
-    pairs = list(range(count // 2))[::-1]
-
     def send_near(pair):
         def store(columns, value):
             near_out[pair, :, columns] = value.astype(BF16)
 
         product(2 * pair + 1, store)
         near(pair).start()
+
+    def batch_parts(batch):
+        return (2 * batch, 2 * batch + 1)
+
+    def send_pair(batch, pair):
+        for part in batch_parts(batch):
+            if pair and not needs(part, pair):
+                far(part, pair).start()
 
     def sum_near(pair):
         near(pair).wait_recv()
@@ -528,13 +567,13 @@
             if pair == 0:
                 kept[:, columns] = value
             else:
-                for part in (0, 1):
-                    far_out[number(part, pair), :, columns] = value[part * half : (part + 1) * half].astype(BF16)
+                for part in range(parts):
+                    far_out[number(part, pair), :, columns] = value[
+                        part * piece : (part + 1) * piece
+                    ].astype(BF16)
 
         product(2 * pair, store)
-        for part in (0, 1):
-            if pair and not needs(part, pair):
-                far(part, pair).start()
+        send_pair(0, pair)
 
     def begin():
         send_near(pairs[0])
@@ -543,29 +582,39 @@
                 send_near(pair - 1)
             sum_near(pair)
 
-    def end():
+    def send(batch):
         for pair in pairs:
-            for part in (0, 1):
-                if needs(part, pair):
+            send_pair(batch, pair)
+
+    def pass_on(batch):
+        for pair in pairs:
+            for part in batch_parts(batch):
+                if pair and needs(part, pair):
                     settle(part, pair)
+
+    def end(batch):
+        for part in batch_parts(batch):
+            settle(part, 0)
+
+    def close():
         for pair in pairs:
             near(pair).wait_send()
-            for part in (0, 1):
+            for part in range(parts):
                 if pair:
                     far(part, pair).wait_send()
 
-    return begin, end
-
-
-def scatter_scratch(count, rows, width):
+    return begin, send, pass_on, end, close
+
+
+def scatter_scratch(count, rows, width, parts=2):
     pairs = count // 2
-    links = 2 * (pairs - 1)
+    links = parts * (pairs - 1)
     return [
         pltpu.VMEM((rows, width), F32),
         pltpu.VMEM((pairs, rows, width), BF16),
         pltpu.VMEM((pairs, rows, width), BF16),
-        pltpu.VMEM((links, rows // 2, width), BF16),
-        pltpu.VMEM((links, rows // 2, width), BF16),
+        pltpu.VMEM((links, rows // parts, width), BF16),
+        pltpu.VMEM((links, rows // parts, width), BF16),
         DMA((pairs,)),
         DMA((pairs,)),
         DMA((links,)),
@@ -574,6 +623,8 @@
 
 
 SCATTER = 9
+PARTS = 4
+BACK_PARTS = 2
 
 
 def comm_params(collective):
@@ -605,10 +656,9 @@
 def middle_kernel(count, left, right, hidden, gain, middle, gathered, own_rows, sums, *scratch):
     me = lax.axis_index("ctx")
     group = lax.axis_index("fsdp")
-    rows = middle.shape[0]
-    half = rows // 2
+    piece = middle.shape[0] // PARTS
     greet([(flip(me, bit), group) for bit in bits_of(count)])
-    start, finish = gather_rows(count, me, group, own_rows, gathered, *scratch[SCATTER:])
+    start, finish = gather_rows(count, me, group, PARTS, own_rows, gathered, *scratch[SCATTER:])
 
     def done(part, value):
         sums[...] = value
@@ -618,17 +668,24 @@
             middle[pl.ds(row, 32), :] = total_rows
             own_rows[pl.ds(row, 32), :] = norm_rows(total_rows, gain[...]).astype(BF16)
 
-        row_blocks(part * half, half, step)
+        row_blocks(part * piece, piece, step)
         start(part)
 
-    begin, end = product_scatter(count, me, group, False, left, right, done, *scratch[:SCATTER])
+    begin, send, pass_on, end, close = product_scatter(
+        count, me, group, PARTS, False, left, right, done, *scratch[:SCATTER]
+    )
     begin()
-    end()
+    pass_on(0)
+    send(1)
+    end(0)
+    pass_on(1)
+    end(1)
     finish()
-
-
-def gather_scratch(count):
-    return [DMA((2 * count,)), DMA((2 * count,)), DMA((2,))]
+    close()
+
+
+def gather_scratch(count, parts):
+    return [DMA((parts * count,)), DMA((parts * count,)), DMA((parts,))]
 
 
 def middle_and_second(count, collective, left, right, hidden, gain):
@@ -641,11 +698,11 @@
         ],
         in_specs=[VMEM] * 4,
         out_specs=[VMEM, ANY],
-        scratch_shapes=[pltpu.VMEM((rows, width), BF16), pltpu.VMEM((rows // 2, width), F32)]
-        + scatter_scratch(count, rows, width)
-        + gather_scratch(count),
+        scratch_shapes=[pltpu.VMEM((rows, width), BF16), pltpu.VMEM((rows // PARTS, width), F32)]
+        + scatter_scratch(count, rows, width, PARTS)
+        + gather_scratch(count, PARTS),
         compiler_params=comm_params(collective),
-        cost_estimate=cost(80, 2 * left.shape[0] * left.shape[1] * width),
+        cost_estimate=cost(80),
     )(left, right, hidden, gain)
 
 
@@ -662,7 +719,6 @@
     d_gain,
     d_attended,
     d_out,
-    own_rows,
     sums,
     gathered,
     turned,
@@ -671,10 +727,10 @@
 ):
     me = lax.axis_index("ctx")
     group = lax.axis_index("fsdp")
-    rows, width = middle.shape
-    half = rows // 2
+    piece = middle.shape[0] // BACK_PARTS
+    own = me * middle.shape[0]
     greet([(flip(me, bit), group) for bit in bits_of(count)])
-    start, finish = gather_rows(count, me, group, own_rows, gathered, *scratch[SCATTER:])
+    start, finish = gather_rows(count, me, group, BACK_PARTS, None, gathered, *scratch[SCATTER:])
     d_gain[...] = jnp.zeros_like(d_gain)
 
     def done(part, value):
@@ -685,13 +741,15 @@
             back, gain_part = norm_back(middle[span_rows, :], gain[...], sums[pl.ds(place, 32), :])
             back = back + cotangent[span_rows, :].astype(F32)
             d_middle[span_rows, :] = back
-            own_rows[span_rows, :] = back.astype(BF16)
+            gathered[pl.ds(pl.multiple_of(own + row, 32), 32), :] = back.astype(BF16)
             d_gain[...] += gain_part
 
-        row_blocks(part * half, half, step)
+        row_blocks(part * piece, piece, step)
         start(part)
 
-    begin, end = product_scatter(count, me, group, True, left, right, done, *scratch[:SCATTER])
+    begin, _, pass_on, end, close = product_scatter(
+        count, me, group, BACK_PARTS, True, left, right, done, *scratch[:SCATTER]
+    )
     begin()
     out_sum[...] = jnp.zeros_like(out_sum)
 
@@ -701,16 +759,18 @@
         return carry
 
     lax.fori_loop(0, attended.shape[0] // 256, turn, 0)
-    end()
-
-    def arrived(row, ref, place):
-        block = ref[pl.ds(place, half), :]
-        d_attended[pl.ds(row, half), :] = nt(block, out_weight[...]).astype(BF16)
-        if half % 128 == 0:
-            out_sum[...] += jnp.dot(turned[:, pl.ds(row, half)], block, preferred_element_type=F32)
+    pass_on(0)
+    end(0)
+
+    def arrived(row, size):
+        block = gathered[pl.ds(row, size), :]
+        d_attended[pl.ds(row, size), :] = nt(block, out_weight[...]).astype(BF16)
+        if size % 128 == 0:
+            out_sum[...] += jnp.dot(turned[:, pl.ds(row, size)], block, preferred_element_type=F32)
 
     finish(arrived)
-    if half % 128:
+    close()
+    if 2 * piece % 128:
         out_sum[...] = jnp.dot(turned[...], gathered[...], preferred_element_type=F32)
     d_out[...] = out_sum[...].astype(BF16)
 
@@ -730,21 +790,20 @@
         in_specs=[VMEM] * 7,
         out_specs=[VMEM] * 4,
         scratch_shapes=[
-            pltpu.VMEM((rows, width), BF16),
-            pltpu.VMEM((rows // 2, width), F32),
+            pltpu.VMEM((rows // BACK_PARTS, width), F32),
             pltpu.VMEM((tokens, width), BF16),
             pltpu.VMEM((wide, tokens), BF16),
             pltpu.VMEM((wide, width), F32),
         ]
-        + scatter_scratch(count, rows, width)
-        + gather_scratch(count),
+        + scatter_scratch(count, rows, width, BACK_PARTS)
+        + gather_scratch(count, BACK_PARTS)[:2],
         compiler_params=comm_params(collective),
-        cost_estimate=cost(85, 2 * left.shape[0] * left.shape[1] * width),
+        cost_estimate=cost(85),
     )(left, right, middle, cotangent, gain, attended, out_weight)
 
 
 def input_kernel(
-    count, left, right, hidden, d_middle, gain, parts, d_hidden, d_gain, columns, sums, send, recv, *scratch
+    count, left, right, hidden, d_middle, gain, parts, d_hidden, d_gain, d_gate_up, columns, sums, send, recv, *scratch
 ):
     me = lax.axis_index("ctx")
     group = lax.axis_index("fsdp")
@@ -765,10 +824,15 @@
 
         row_blocks(part * half, half, step)
 
-    begin, end = product_scatter(count, me, group, True, left, right, done, *scratch)
+    begin, _, pass_on, end, close = product_scatter(
+        count, me, group, 2, True, left, right, done, *scratch
+    )
     begin()
-    end()
+    pass_on(0)
+    end(0)
     finish()
+    close()
+    d_gate_up[...] = columns[...].astype(F32)
 
 
 def back_to_input(count, collective, left, right, hidden, d_middle, gain, parts):
@@ -779,43 +843,171 @@
         out_shape=[
             shape((rows, width), F32),
             shape((1, width), F32),
-            shape((parts.shape[1], 2 * FF), BF16),
+            shape((parts.shape[1], 2 * FF), F32),
         ],
         in_specs=[VMEM] * 5 + [ANY],
-        out_specs=[VMEM, VMEM, ANY],
-        scratch_shapes=[pltpu.VMEM((rows // 2, width), F32), DMA((2 * count,)), DMA((2 * count,))]
+        out_specs=[VMEM] * 3,
+        scratch_shapes=[
+            pltpu.VMEM((parts.shape[1], 2 * FF), BF16),
+            pltpu.VMEM((rows // 2, width), F32),
+            DMA((2 * count,)),
+            DMA((2 * count,)),
+        ]
         + scatter_scratch(count, rows, width),
         compiler_params=comm_params(collective),
-        cost_estimate=cost(60, 2 * left.shape[0] * left.shape[1] * width),
+        cost_estimate=cost(60),
     )(left, right, hidden, d_middle, gain, parts)
 
 
-def output_kernel(count, left, right, middle, output, *scratch):
+def mlp_kernel(
+    count,
+    groups,
+    activated,
+    weight,
+    middle,
+    upstream,
+    both,
+    second,
+    output,
+    d_both,
+    parts,
+    up_slots,
+    both_slots,
+    second_slots,
+    part_slots,
+    up_in,
+    both_in,
+    second_in,
+    parts_out,
+    *scratch,
+):
     me = lax.axis_index("ctx")
     group = lax.axis_index("fsdp")
     half = middle.shape[0] // 2
+    tokens, own = activated.shape
+    block = up_slots.shape[1]
+    columns = second_slots.shape[2]
     greet([(flip(me, bit), group) for bit in bits_of(count)])
+
+    def rows_in(index):
+        slot = lax.rem(index, 2)
+        rows = pl.ds(pl.multiple_of(index * block, block), block)
+        return (
+            pltpu.make_async_copy(upstream.at[rows], up_slots.at[slot], up_in.at[slot]),
+            pltpu.make_async_copy(both.at[rows], both_slots.at[slot], both_in.at[slot]),
+        )
+
+    def second_copy(index):
+        slot = lax.rem(index, 2)
+        span_columns = pl.ds(pl.multiple_of(index * columns, columns), columns)
+        return pltpu.make_async_copy(second.at[:, span_columns], second_slots.at[slot], second_in.at[slot])
+
+    def part_copies(index):
+        slot = lax.rem(index, 2)
+        rows = columns // groups
+        return [
+            pltpu.make_async_copy(
+                part_slots.at[slot, pl.ds(owner * rows, rows)],
+                parts.at[owner, index],
+                parts_out.at[slot, owner],
+            )
+            for owner in range(groups)
+        ]
+
+    for item in rows_in(0):
+        item.start()
+    second_copy(0).start()
 
     def done(part, value):
         span_rows = pl.ds(part * half, half)
         output[span_rows, :] = (middle[span_rows, :] + value).astype(BF16)
 
-    begin, end = product_scatter(count, me, group, False, left, right, done, *scratch)
+    begin, _, pass_on, end, close = product_scatter(
+        count, me, group, 2, False, activated, weight, done, *scratch
+    )
     begin()
-    end()
-
-
-def output_rows(count, collective, left, right, middle):
+    steps = tokens // block
+
+    def activation(index, carry):
+        @pl.when(index + 1 < steps)
+        def _():
+            for item in rows_in(index + 1):
+                item.start()
+
+        for item in rows_in(index):
+            item.wait()
+        slot = lax.rem(index, 2)
+        rows = pl.ds(pl.multiple_of(index * block, block), block)
+        grad = nt(up_slots[slot], weight[...]).astype(BF16).astype(F32)
+        gate = both_slots[slot, :, :own]
+        up = both_slots[slot, :, own:]
+        sigmoid = 1.0 / (1.0 + jnp.exp(-gate))
+        d_both[rows, :own] = (grad * up * sigmoid * (1.0 + gate * (1.0 - sigmoid))).astype(BF16)
+        d_both[rows, own:] = (grad * gate * sigmoid).astype(BF16)
+        return carry
+
+    lax.fori_loop(0, steps, activation, 0)
+
+    def weight_grad(index, carry):
+        @pl.when(index + 1 < count)
+        def _():
+            second_copy(index + 1).start()
+
+        second_copy(index).wait()
+
+        @pl.when(index >= 2)
+        def _():
+            for item in part_copies(index - 2):
+                item.wait()
+
+        slot = lax.rem(index, 2)
+        value = lax.dot_general(
+            second_slots[slot], d_both[...], (((0,), (0,)), ((), ())), preferred_element_type=F32
+        )
+        part_slots[slot] = value.astype(BF16)
+        for item in part_copies(index):
+            item.start()
+        return carry
+
+    lax.fori_loop(0, count // 2, weight_grad, 0)
+    pass_on(0)
+    lax.fori_loop(count // 2, count, weight_grad, 0)
+    for index in (count - 2, count - 1):
+        for item in part_copies(index):
+            item.wait()
+    end(0)
+    close()
+
+
+def back_through_mlp(count, groups, collective, activated, weight, middle, upstream, both, second):
     rows, width = middle.shape
+    tokens, own = activated.shape
+    block = 256
+    columns = width // count
+    shape = jax.ShapeDtypeStruct
     return pl.pallas_call(
-        functools.partial(output_kernel, count),
-        out_shape=jax.ShapeDtypeStruct((rows, width), BF16),
-        in_specs=[VMEM] * 3,
-        out_specs=VMEM,
-        scratch_shapes=scatter_scratch(count, rows, width),
+        functools.partial(mlp_kernel, count, groups),
+        out_shape=[
+            shape((rows, width), BF16),
+            shape((tokens, 2 * own), BF16),
+            shape((groups, count, columns // groups, 2 * own), BF16),
+        ],
+        in_specs=[VMEM] * 3 + [ANY] * 3,
+        out_specs=[VMEM, VMEM, ANY],
+        scratch_shapes=[
+            pltpu.VMEM((2, block, width), BF16),
+            pltpu.VMEM((2, block, 2 * own), F32),
+            pltpu.VMEM((2, tokens, columns), BF16),
+            pltpu.VMEM((2, columns, 2 * own), BF16),
+            DMA((2,)),
+            DMA((2,)),
+            DMA((2,)),
+            DMA((2, groups)),
+        ]
+        + scatter_scratch(count, rows, width),
         compiler_params=comm_params(collective),
-        cost_estimate=cost(45, 2 * left.shape[0] * left.shape[1] * width),
-    )(left, right, middle)
+        cost_estimate=cost(48),
+    )(activated, weight, middle, upstream, both, second)
 
 
 def swap_halves(value):
@@ -1056,6 +1248,95 @@
     lax.fori_loop(0, tokens // RUN, unsort, 0)
 
 
+def attention_and_joined_back_kernel(
+    heads,
+    runs,
+    d_attended,
+    queries,
+    keys,
+    values,
+    mixed,
+    lse,
+    raw,
+    cosine,
+    sine,
+    q_gain,
+    k_gain,
+    share,
+    d_joined,
+    d_q_gain,
+    d_k_gain,
+    d_queries,
+    d_keys,
+    d_values,
+    arrived,
+    keys_turned,
+    raw_here,
+    cosine_here,
+    sine_here,
+    placed,
+    loaded,
+):
+    loads = [
+        pltpu.make_async_copy(source, target, loaded.at[index])
+        for index, (source, target) in enumerate(
+            [(raw, raw_here), (cosine, cosine_here), (sine, sine_here)]
+        )
+    ]
+    for item in loads:
+        item.start()
+    attention_back_kernel(
+        heads, runs, d_attended, queries, keys, values, mixed, lse, d_queries, d_keys, d_values, arrived, keys_turned
+    )
+    for item in loads:
+        item.wait()
+    joined_back_kernel(
+        heads,
+        runs,
+        raw_here,
+        d_queries,
+        d_keys,
+        d_values,
+        cosine_here,
+        sine_here,
+        q_gain,
+        k_gain,
+        share,
+        d_joined,
+        d_q_gain,
+        d_k_gain,
+        placed,
+    )
+
+
+def attention_and_joined_back(
+    heads, runs, d_attended, queries, keys, values, mixed, lse, raw, cosine, sine, q_gain, k_gain, share
+):
+    tokens = keys.shape[0]
+    wide = heads * CONT
+    shape = jax.ShapeDtypeStruct
+    return pl.pallas_call(
+        functools.partial(attention_and_joined_back_kernel, heads),
+        out_shape=[shape(raw.shape, BF16), shape((1, HEAD), F32), shape((1, HEAD), F32)],
+        in_specs=[SMEM] + [VMEM] * 6 + [ANY] * 3 + [VMEM] * 3,
+        out_specs=[VMEM] * 3,
+        scratch_shapes=[
+            pltpu.VMEM((tokens, wide), BF16),
+            pltpu.VMEM((tokens, HEAD), F32),
+            pltpu.VMEM((tokens, HEAD), F32),
+            pltpu.VMEM((tokens, wide), BF16),
+            pltpu.VMEM((HEAD, tokens), BF16),
+            pltpu.VMEM(raw.shape, F32),
+            pltpu.VMEM(cosine.shape, F32),
+            pltpu.VMEM(sine.shape, F32),
+            pltpu.VMEM(raw.shape, BF16),
+            DMA((3,)),
+        ],
+        compiler_params=pltpu.CompilerParams(vmem_limit_bytes=VMEM_LIMIT),
+        cost_estimate=cost(30),
+    )(runs, d_attended, queries, keys, values, mixed, lse, raw, cosine, sine, q_gain, k_gain, share)
+
+
 def joined_back(heads, runs, raw, d_queries, d_keys, d_values, cosine, sine, q_gain, k_gain, share):
     shape = jax.ShapeDtypeStruct
     return pl.pallas_call(
@@ -1101,7 +1382,6 @@
     tokens = rows * count
     heads = QUERY_HEADS // count
     repeat = sharing(count)
-    me = lax.axis_index("ctx")
 
     first = segment_ids[0, ::RUN]
     place = positions[0, ::RUN]
@@ -1147,72 +1427,70 @@
     both = jnp.dot(second, w_gu, preferred_element_type=F32)
     own = both.shape[1] // 2
     gate, up = both[:, :own], both[:, own:]
-    sigmoid = jax.nn.sigmoid(gate)
-    activated = (gate * sigmoid * up).astype(BF16)
+    activated = (gate * jax.nn.sigmoid(gate) * up).astype(BF16)
 
     activated, arrived = lax.optimization_barrier((activated, arrived))
     upstream = gather_join(count, 5, masks, blocks, filled, arrived)
     d_down = jnp.dot(activated.T, upstream, preferred_element_type=F32).astype(BF16)
     d_down, upstream = lax.optimization_barrier((d_down, upstream))
     d_down = scatter_groups(d_down)
-    d_activated = lax.dot_general(
-        upstream, w_down, (((1,), (1,)), ((), ())), preferred_element_type=F32
-    ).astype(BF16).astype(F32)
-    d_gate = d_activated * up * sigmoid * (1.0 + gate * (1.0 - sigmoid))
-    d_up = d_activated * gate * sigmoid
-    d_both = jnp.concatenate([d_gate, d_up], axis=1).astype(BF16)
+    output, d_both, gu_parts = back_through_mlp(
+        count, groups, 9, activated, w_down, middle, upstream, both, second
+    )
+    gu_parts, d_both = lax.optimization_barrier((gu_parts, d_both))
+    gu_parts = scatter_groups(gu_parts.reshape((groups * count,) + gu_parts.shape[2:]))
 
     def weight_grad(left, right):
         grad = lax.dot_general(left, right, (((0,), (0,)), ((), ())), preferred_element_type=F32)
         grad = grad.astype(BF16).reshape(count, groups, -1, right.shape[1])
         return grad.transpose(1, 0, 2, 3).reshape(groups * count, -1, right.shape[1])
 
-    gu_parts, d_both = lax.optimization_barrier((weight_grad(second, d_both), d_both))
-    gu_parts = scatter_groups(gu_parts)
     d_middle, mlp_gain_grad, d_attended, d_out = back_through_middle(
         count, 6, d_both, w_gu, middle, cotangent[0], mlp_gain[None, :], attended, w_out
     )
     d_attended, d_down = lax.optimization_barrier((d_attended, d_down))
-    d_queries, d_keys, d_values = attention_back(
-        heads, run_order, d_attended, queries, keys, values, mixed, lse
-    )
     share = jnp.ones((2, HEAD), F32)
-    if repeat > 1:
-        swap = [(index, index ^ 1) for index in range(count)]
-        d_keys = d_keys + lax.ppermute(d_keys, "ctx", swap)
-        d_values = d_values + lax.ppermute(d_values, "ctx", swap)
-        mine = lax.rem(me, 2) == jnp.arange(2)
+    tables = (cosine, sine, q_gain_row, k_gain_row)
+    if repeat == 1:
+        d_joined, q_gain_grad, k_gain_grad = attention_and_joined_back(
+            heads, run_order, d_attended, queries, keys, values, mixed, lse, raw, *tables, share
+        )
+    else:
+        d_queries, d_keys, d_values = attention_back(
+            heads, run_order, d_attended, queries, keys, values, mixed, lse
+        )
+        d_keys = d_keys + across(count, 1, d_keys)
+        d_values = d_values + across(count, 1, d_values)
+        mine = lax.rem(lax.axis_index("ctx"), 2) == jnp.arange(2)
         share = share * mine[:, None].astype(F32)
-    d_joined, q_gain_grad, k_gain_grad = joined_back(
-        heads, run_order, raw, d_queries, d_keys, d_values, cosine, sine, q_gain_row, k_gain_row, share
-    )
+        d_joined, q_gain_grad, k_gain_grad = joined_back(
+            heads, run_order, raw, d_queries, d_keys, d_values, *tables, share
+        )
+    normed, d_joined, gu_parts = lax.optimization_barrier((normed, d_joined, gu_parts))
     qkv_grad_parts, d_joined = lax.optimization_barrier((weight_grad(normed, d_joined), d_joined))
-    qkv_grad_parts, gu_parts = lax.optimization_barrier((qkv_grad_parts, gu_parts))
+    d_out, gu_parts = lax.optimization_barrier((d_out, gu_parts))
+    d_out = scatter_groups(d_out)
     qkv_grad_parts = scatter_groups(qkv_grad_parts)
     d_hidden, attn_gain_grad, d_gate_up = back_to_input(
         count, 8, d_joined, w_qkv, hidden_in[0], d_middle, attn_gain[None, :], gu_parts
     )
-    d_out, qkv_grad_parts, d_hidden, activated = lax.optimization_barrier(
-        (d_out, qkv_grad_parts, d_hidden, activated)
-    )
-    d_out = scatter_groups(d_out)
-    output = output_rows(count, 9, activated, w_down, middle)
+    d_hidden, qkv_grad_parts = lax.optimization_barrier((d_hidden, qkv_grad_parts))
 
     small = jnp.concatenate([attn_gain_grad[0], mlp_gain_grad[0], q_gain_grad[0], k_gain_grad[0]])
     padded = -(-small.shape[0] // 1024) * 1024
     small = jnp.pad(small, (0, padded - small.shape[0])).reshape(-1, 128)
-    summed, d_qkv = last(count, groups, 11, small, qkv_grad_parts, qkv_weight.shape[1])
-    summed = summed.reshape(-1)
+    gains = last(count, groups, 11, small, qkv_grad_parts, width, qkv_weight.shape[1])
+    attn_gain_sum, mlp_gain_sum, q_gain_sum, k_gain_sum, d_qkv = gains
     return (
         output[None],
         d_hidden[None],
-        summed[:width],
-        d_qkv.astype(F32),
-        summed[2 * width : 2 * width + HEAD],
-        summed[2 * width + HEAD : 2 * width + 2 * HEAD],
+        attn_gain_sum.reshape(-1),
+        d_qkv,
+        q_gain_sum.reshape(-1),
+        k_gain_sum.reshape(-1),
         d_out.astype(F32),
-        summed[width : 2 * width],
-        d_gate_up.astype(F32),
+        mlp_gain_sum.reshape(-1),
+        d_gate_up,
         d_down.astype(F32),
     )
 

time: 593 us -> 554 us (0.934)
  matrix products: 77.4 us -> 47.3 us
  other arithmetic: 18.5 us -> 10.3 us
    dot_general x2 -> x1, matrix products: 24.2 us -> 8.53 us  [weight_grad(): lax.dot_general(left, right, (((0,), (0,)), ((), ())), preferred_element_...]
    dot_general x1 -> x0, matrix products: 14.2 us -> none  [body(): lax.dot_general(upstream, w_down, (((1,), (1,)), ((), ())), preferred_ele...]
    pallas_call x3 -> x2, Pallas kernels: 77.8 us -> 80.4 us  [the longest x1 55.3 us: back_through_mlp(): pl.pallas_call(functools.partial(mlp_kernel, count, groups), out_shape=[s...]
  transfers between devices with their start and end apart: 12 -> 12, of which waited for: 6 -> 5; matrix products, arithmetic and copies ran while one was open for 18% -> 12% of each run, Pallas kernels for 75% -> 78%
where the time goes in v3:
time: 554 us; the launch traced here: 548 us
  Pallas kernels  441 us (80%)
  matrix products  47.3 us (9%)
  local copies, waits for them, and re-layouts  17.4 us (3%)
  between operations  15 us (3%)
  waiting for transfers between devices  11.6 us (2%)
  other arithmetic  10.3 us (2%)
  starting transfers between devices  6 us (1%)
    pallas_call x1, Pallas kernels, back_through_middle(): pl.pallas_call(functools.partial(back_kernel, count), out_shape=[shape((r...  94.6 us
    pallas_call x1, Pallas kernels, middle_and_second(): pl.pallas_call(functools.partial(middle_kernel, count), out_shape=[jax.Sh...  83.7 us
    pallas_call x1, Pallas kernels, back_to_input(): pl.pallas_call(functools.partial(input_kernel, count), out_shape=[shape((...  62.7 us
    pallas_call x1, Pallas kernels, back_through_mlp(): pl.pallas_call(functools.partial(mlp_kernel, count, groups), out_shape=[s...  55.3 us
    pallas_call x1, Pallas kernels, opening(): pl.pallas_call(functools.partial(opening_kernel, count), out_shape=[jax.S...  43.3 us
    pallas_call x1, Pallas kernels, spread(): pl.pallas_call(functools.partial(spread_kernel, count), out_shape=[jax.Sh...  28.6 us
    pallas_call x1, Pallas kernels, attention_and_joined_back(): pl.pallas_call(functools.partial(attention_and_joined_back_kernel, heads)...  25.1 us
    pallas_call x1, Pallas kernels, attention(): pl.pallas_call(functools.partial(attention_kernel, heads), out_shape=[sha...  20.5 us
  transfers between devices with their start and end apart: 12, of which 5 were waited for; matrix products, arithmetic and copies ran while one was open for 12% of the time, Pallas kernels for 78%

profile of v3, /device:TPU:0, one launch (start us, length us, event | category | flops | bytes accessed | tf_op | source)
XLA Modules:
  0.0 548.3 jit_solution(7588704573019669897)
XLA Ops:
  8.0 28.6 %shard_map.213 = (bf16[8,64,512]{2,1,0:T(8,128)(2,1)}, bf16[8,64,1536]{2,1,0:T(8,128)(2,1)}) custom-call(bf16[64,4096]{1,0:T(8,128)(2,1)} %qkv.1, bf16[64,12288]{1,0:T(8,128)(2,1)} %mlp.1), custom_call_target="tpu_custom_call" | custom-call | bytes 28000000 | tf_op jit(solution)/shard_map/pallas_call | solution.py:263
  36.6 3.7 all-gather.5.cloned.1.call-done.right.out_weight
  42.5 1.5 fusion.1
  44.0 2.0 fusion.3.normed
  46.0 43.3 %shard_map.214 = (bf16[2048,2048]{1,0:T(8,128)(2,1)}, s32[8,8,128]{2,1,0:T(8,128)}) custom-call(bf16[256,2048]{1,0:T(8,128)(2,1)} %fusion.3.normed, s32[1,8,128]{2,1,0:T(8,128)} %scatter.4.runs), custom_call_target="tpu_custom_call" | custom-call | bytes 45000000 | tf_op jit(solution)/shard_map/pallas_call | solution.py:293
  89.5 1.6 collective-permute-start
  92.6 10.9 %fusion.5.joined = f32[2048,512]{1,0:T(8,128)} fusion(bf16[2048,2048]{1,0:T(8,128)(2,1)} %get-tuple-element.123, bf16[2048,512]{1,0:T(8,128)(2,1)} %bitcast.59), kind=kOutput, calls=%fused_computation.25 | convolution fusion | flops 4294967296 | bytes 14680064 | tf_op jit(solution)/shard_map/dot_general | solution.py:1417
  105.9 1.5 collective-permute-start.2
  109.4 20.5 %shard_map.215 = (bf16[2048,256]{1,0:T(8,128)(2,1)}, f32[2048,512]{1,0:T(8,128)}, bf16[16,256,128]{2,1,0:T(8,128)(2,1)}, bf16[2048,128]{1,0:T(8,128)(2,1)}, bf16...) custom-call(s32[64]{0:T(128)} %reshape_squeeze.3.runs, f32[2048,512]{1,0:T(8,128)} %fusion.5.joined, ...), custom_call_target="tpu_custom_call" | custom-call | bytes 15000000 | tf_op jit(solution)/shard_map/pallas_call | solution.py:1104
  130.4 83.7 %shard_map.216 = (f32[256,2048]{1,0:T(8,128)}, bf16[2048,2048]{1,0:T(8,128)(2,1)}) custom-call(bf16[2048,256]{1,0:T(8,128)(2,1)} %get-tuple-element.97.left.attended, bf16[256,2048]{1,0:T(8,128)(2,1)} %all-gather.5.cloned.1.call-done.right.out_weight, bf16[256,2048]{1,0:T(8,128)(2,1)} %bitcast.51, f32[1,2048]{1,0:T(1,128)} %bitcast.64), custom_call_target="tpu_custom_call" | custom-call | bytes 80000000 | tf_op jit(solution)/shard_map/pallas_call | solution.py:693
  214.2 17.4 %fusion.6.both = f32[2048,1536]{1,0:T(8,128)S(1)} fusion(bf16[2048,2048]{1,0:T(8,128)(2,1)} %get-tuple-element.99.second, bf16[2048,1536]{1,0:T(8,128)(2,1)} %bitcast.55), kind=kOutput, calls=%fused_computation.26 | convolution fusion | flops 12884901888 | bytes 27262976 | tf_op jit(solution)/shard_map/dot_general | solution.py:1427
  231.6 4.5 copy-done
  236.1 2.1 fusion.activated
  238.2 14.0 %shard_map.217.upstream = bf16[2048,2048]{1,0:T(8,128)(2,1)} custom-call(bf16[2,128,2048]{2,1,0:T(8,128)(2,1)} %copy-done.5, bf16[2,128,2048]{2,1,0:T(8,128)(2,1)} %collective-permute-done.2.refs_1_, bf16[2,128,2048]{2,1,0:T(8,128)(2,1)} %copy-done.4, bf16[2,128,2048]{2,1,0:T(8,128)(2,1)} %copy-done.8), custom_call_target="tpu_custom_call" | custom-call | bytes 13000000 | tf_op jit(solution)/shard_map/pallas_call | solution.py:362
  252.2 10.5 %convolution_convert_fusion = bf16[768,2048]{1,0:T(8,128)(2,1)} fusion(bf16[2048,768]{1,0:T(8,128)(2,1)S(1)} %fusion.activated, bf16[2048,2048]{1,0:T(8,128)(2,1)} %shard_map.217.upstream), kind=kOutput, calls=%fused_computation.2 | convolution fusion | flops 6444023808 | bytes 14680064 | tf_op jit(solution)/shard_map/dot_general | solution.py:1434
  262.8 4.9 all-gather.11.cloned.1.call-done.weight
  267.6 55.3 %shard_map.218 = (bf16[256,2048]{1,0:T(8,128)(2,1)}, bf16[2048,1536]{1,0:T(8,128)(2,1)}, bf16[4,8,64,1536]{3,2,1,0:T(8,128)(2,1)}) custom-call(bf16[2048,768]{1,0:T(8,128)(2,1)} %copy-done.2, bf16[768,2048]{1,0:T(8,128)(2,1)} %all-gather.11.cloned.1.call-done.weight, f32[256,2048]{1,0:T(8,128)} %get-tuple-element.104.middle, ...), custom_call_target="tpu_custom_call" | custom-call | bytes 48000000 | tf_op jit(solution)/shard_map/pallas_call | solution.py:988
  323.0 94.6 %shard_map.219 = (f32[256,2048]{1,0:T(8,128)}, f32[1,2048]{1,0:T(1,128)}, bf16[2048,256]{1,0:T(8,128)(2,1)}, bf16[256,2048]{1,0:T(8,128)(2,1)}) custom-call(bf16[2048,1536]{1,0:T(8,128)(2,1)} %get-tuple-element.111.left, bf16[2048,1536]{1,0:T(8,128)(2,1)} %bitcast.56, f32[256,2048]{1,0:T(8,128)} %get-tuple-element.104.middle, bf16[256,2048]{1,0:T(8,128)(2,1)} %bitcast.57, ...), custom_call_target="tpu_custom_call" | custom-call | bytes 85000000 | tf_op jit(solution)/shard_map/pallas_call | solution.py:782
  418.2 25.1 %shard_map.220 = (bf16[2048,512]{1,0:T(8,128)(2,1)}, f32[1,128]{1,0:T(1,128)}, f32[1,128]{1,0:T(1,128)}) custom-call(s32[64]{0:T(128)} %reshape_squeeze.3.runs, bf16[2048,256]{1,0:T(8,128)(2,1)} %get-tuple-element.114.d_attended, bf16[16,256,128]{2,1,0:T(8,128)(2,1)} %get-tuple-element.115.queries, bf16[2048,128]{1,0:T(8,128)(2,1)} %get-tuple-element.116.keys, ...), custom_call_target="tpu_custom_call" | custom-call | bytes 30000000 | tf_op jit(solution)/shard_map/pallas_call | solution.py:1318
  443.4 8.5 %convolution_convert_fusion.1 = bf16[2048,512]{1,0:T(8,128)(2,1)S(1)} fusion(bf16[2048,2048]{1,0:T(8,128)(2,1)} %get-tuple-element.123, bf16[2048,512]{1,0:T(8,128)(2,1)} %get-tuple-element.125.left), kind=kOutput, calls=%fused_computation.3 | convolution fusion | flops 4296015872 | bytes 12582912 | tf_op jit(solution)/shard_map/dot_general | solution.py:1444
  454.7 62.7 %shard_map.221 = (f32[256,2048]{1,0:T(8,128)}, f32[1,2048]{1,0:T(1,128)}, f32[64,12288]{1,0:T(8,128)}) custom-call(bf16[2048,512]{1,0:T(8,128)(2,1)} %get-tuple-element.125.left, bf16[2048,512]{1,0:T(8,128)(2,1)} %bitcast.60, bf16[256,2048]{1,0:T(8,128)(2,1)} %bitcast.52, f32[256,2048]{1,0:T(8,128)} %get-tuple-element.126.d_middle, f32[1,2048]{1,0:T(1,128)} %bitcast.66, ...), custom_call_target="tpu_custom_call" | custom-call | bytes 60000000 | tf_op jit(solution)/shard_map/pallas_call | solution.py:841
  518.9 1.8 convert_element_type.28
  520.7 13.0 %shard_map.222 = (f32[16,128]{1,0:T(8,128)}, f32[16,128]{1,0:T(8,128)}, f32[1,128]{1,0:T(1,128)}, f32[1,128]{1,0:T(1,128)}, f32[64,4096]{1,0:T(8,128)}) custom-call(f32[40,128]{1,0:T(8,128)} %fusion.4.values, bf16[8,64,512]{2,1,0:T(8,128)(2,1)} %reduce-scatter.9.cloned.1.call-done.parts), custom_call_target="tpu_custom_call" | custom-call | bytes 14000000 | tf_op jit(solution)/shard_map/pallas_call | solution.py:449
  539.3 1.7 copy.40
  (86 shorter events, 20.0 us)
Async XLA Ops:
  7.2 36.8 %copy-start.1 = (bf16[1,256,2048]{2,1,0:T(8,128)(2,1)S(1)}, bf16[1,256,2048]{2,1,0:T(8,128)(2,1)}, u32[]{:S(2)}) copy-start(bf16[1,256,2048]{2,1,0:T(8,128)(2,1)} %param.16) | copy-start | bytes 3145732
  7.2 33.1 %all-gather.5.cloned.1.call-start = ((), (), s32[]{:S(2)}) async-start(), calls=%async_computation.4 | async-start | bytes 1310720 | tf_op jit(solution)/shard_map/all_gather | solution.py:1392
  7.9 81.5 %copy-start.3 = (bf16[1,256,2048]{2,1,0:T(8,128)(2,1)S(1)}, bf16[1,256,2048]{2,1,0:T(8,128)(2,1)}, u32[]{:S(2)}) copy-start(bf16[1,256,2048]{2,1,0:T(8,128)(2,1)} %param.27) | copy-start | bytes 3145732
  7.9 81.4 %all-gather.7.cloned.1.call-start = ((), (), s32[]{:S(2)}) async-start(), calls=%async_computation.5 | async-start | bytes 2621440 | tf_op jit(solution)/shard_map/all_gather | solution.py:1392
  40.3 173.9 %all-gather.9.cloned.1.call-start = ((), (), s32[]{:S(2)}) async-start(), calls=%async_computation.6 | async-start | bytes 7864320 | tf_op jit(solution)/shard_map/all_gather | solution.py:1392
  89.4 178.3 %all-gather.11.cloned.1.call-start = ((), (), s32[]{:S(2)}) async-start(), calls=%async_computation.7 | async-start | bytes 3932160 | tf_op jit(solution)/shard_map/all_gather | solution.py:1392
  89.5 14.3 %collective-permute-start = (bf16[1,128,2048]{2,1,0:T(8,128)(2,1)S(1)}, bf16[1,128,2048]{2,1,0:T(8,128)(2,1)S(1)}, u32[]{:S(2)}, u32[]{:S(2)}) collective-permute-start(bf16[1,128,2048]{2,1,0:T(8,128)(2,1)S(1)} %get-tuple-element.147), channel_id=1, source_target_pairs={{0,8},{4,12},{8,0},{12,4},{16,24},{20,28},{24,16},{28,20},{1,9},{5... | collective-permute-start | bytes 1572872 | tf_op jit(solution)/shard_map/ppermute | solution.py:308
  91.2 14.0 %collective-permute-start.1 = (bf16[1,128,2048]{2,1,0:T(8,128)(2,1)S(1)}, bf16[1,128,2048]{2,1,0:T(8,128)(2,1)S(1)}, u32[]{:S(2)}, u32[]{:S(2)}) collective-permute-start(bf16[1,128,2048]{2,1,0:T(8,128)(2,1)S(1)} %get-tuple-element.146), channel_id=1, source_target_pairs={{0,16},{4,20},{8,24},{12,28},{16,0},{20,4},{24,8},{28,12},{1,17},{... | collective-permute-start | bytes 1572872 | tf_op jit(solution)/shard_map/ppermute | solution.py:308
  105.2 24.7 %copy-start.4 = (bf16[2,128,2048]{2,1,0:T(8,128)(2,1)}, bf16[2,128,2048]{2,1,0:T(8,128)(2,1)S(1)}, u32[]{:S(2)}) copy-start(bf16[2,128,2048]{2,1,0:T(8,128)(2,1)S(1)} %pad_maximum_fusion.1.refs_2_) | copy-start | bytes 3145732
  105.2 24.7 %collective-permute-start.3 = (bf16[2,128,2048]{2,1,0:T(8,128)(2,1)S(1)}, bf16[2,128,2048]{2,1,0:T(8,128)(2,1)S(1)}, u32[]{:S(2)}, u32[]{:S(2)}) collective-permute-start(bf16[2,128,2048]{2,1,0:T(8,128)(2,1)S(1)} %pad_maximum_fusion.1.refs_2_), channel_id=1, source_target_pairs={{0,8},{4,12},{8,0},{12,4},{16,24},{20,28},{24,16},{28,20},{1,9},{5... | collective-permute-start | bytes 3145736 | tf_op jit(solution)/shard_map/ppermute | solution.py:308
  105.9 108.3 %copy-start.5 = (bf16[2,128,2048]{2,1,0:T(8,128)(2,1)}, bf16[2,128,2048]{2,1,0:T(8,128)(2,1)S(1)}, u32[]{:S(2)}) copy-start(bf16[2,128,2048]{2,1,0:T(8,128)(2,1)S(1)} %pad_maximum_fusion.refs_0_) | copy-start | bytes 3145732
  105.9 24.5 %collective-permute-start.2 = (bf16[2,128,2048]{2,1,0:T(8,128)(2,1)S(1)}, bf16[2,128,2048]{2,1,0:T(8,128)(2,1)}, u32[]{:S(2)}, u32[]{:S(2)}) collective-permute-start(bf16[2,128,2048]{2,1,0:T(8,128)(2,1)S(1)} %pad_maximum_fusion.refs_0_), channel_id=1, source_target_pairs={{0,16},{4,20},{8,24},{12,28},{16,0},{20,4},{24,8},{28,12},{1,17},{... | collective-permute-start | bytes 3145736 | tf_op jit(solution)/shard_map/ppermute | solution.py:308
  107.5 310.2 %reduce-scatter.5.cloned.1.call-start = ((), (), s32[]{:S(2)}) async-start(), calls=%async_computation.8 | async-start | bytes 3932160 | tf_op jit(solution)/shard_map/reduce_scatter | solution.py:1395
  129.9 84.3 %copy-start.8 = (bf16[2,128,2048]{2,1,0:T(8,128)(2,1)}, bf16[2,128,2048]{2,1,0:T(8,128)(2,1)S(1)}, u32[]{:S(2)}) copy-start(bf16[2,128,2048]{2,1,0:T(8,128)(2,1)S(1)} %collective-permute-done.3.refs_3_) | copy-start | bytes 3145732
  238.2 14.0 %copy-start.2 = (bf16[2048,768]{1,0:T(8,128)(2,1)}, bf16[2048,768]{1,0:T(8,128)(2,1)S(1)}, u32[]{:S(2)}) copy-start(bf16[2048,768]{1,0:T(8,128)(2,1)S(1)} %fusion.activated) | copy-start | bytes 9437188
  262.7 180.6 %reduce-scatter.7.cloned.1.call-start = ((), (), s32[]{:S(2)}) async-start(), calls=%async_computation.9 | async-start | bytes 7864320 | tf_op jit(solution)/shard_map/reduce_scatter | solution.py:1395
  323.0 195.9 %reduce-scatter.11.cloned.1.call-start = ((), (), s32[]{:S(2)}) async-start(), calls=%async_computation.11 | async-start | bytes 1310720 | tf_op jit(solution)/shard_map/reduce_scatter | solution.py:1395
  443.3 77.4 %reduce-scatter.9.cloned.1.call-start = ((), (), s32[]{:S(2)}) async-start(), calls=%async_computation.10 | async-start | bytes 2621440 | tf_op jit(solution)/shard_map/reduce_scatter | solution.py:1395
  454.7 62.7 %copy-start.12 = (f32[1,2048]{1,0:T(1,128)S(1)}, f32[1,2048]{1,0:T(1,128)}, u32[]{:S(2)}) copy-start(f32[1,2048]{1,0:T(1,128)} %get-tuple-element.134) | copy-start | bytes 24580
  454.7 62.7 %copy-start.15 = (f32[1,128]{1,0:T(1,128)S(1)}, f32[1,128]{1,0:T(1,128)}, u32[]{:S(2)}) copy-start(f32[1,128]{1,0:T(1,128)} %get-tuple-element.135) | copy-start | bytes 1540
  454.7 62.7 %copy-start.16 = (f32[1,128]{1,0:T(1,128)S(1)}, f32[1,128]{1,0:T(1,128)}, u32[]{:S(2)}) copy-start(f32[1,128]{1,0:T(1,128)} %get-tuple-element.136) | copy-start | bytes 1540
  454.7 79.0 %copy-start.9 = (bf16[256,2048]{1,0:T(8,128)(2,1)S(1)}, bf16[256,2048]{1,0:T(8,128)(2,1)}, u32[]{:S(2)}) copy-start(bf16[256,2048]{1,0:T(8,128)(2,1)} %get-tuple-element.108) | copy-start | bytes 3145732
  517.4 17.4 %copy-start.7 = (f32[256,2048]{1,0:T(8,128)S(1)}, f32[256,2048]{1,0:T(8,128)}, u32[]{:S(2)}) copy-start(f32[256,2048]{1,0:T(8,128)} %get-tuple-element.132) | copy-start | bytes 6291460
  533.8 5.5 %copy-start.6 = (f32[64,12288]{1,0:T(8,128)S(1)}, f32[64,12288]{1,0:T(8,128)}, u32[]{:S(2)}) copy-start(f32[64,12288]{1,0:T(8,128)} %get-tuple-element.166) | copy-start | bytes 9437188
  (7 other events, 24.6 us)
Sparse Core Ops, SparseCore 0:
  9.6 30.6 all-gather.4
  41.8 45.4 all-gather.6
  89.5 114.9 all-gather.8
  205.9 61.6 all-gather.10
  269.8 58.8 reduce-scatter.4
  330.9 110.8 reduce-scatter.6
  444.0 27.6 reduce-scatter.10
  474.7 42.4 reduce-scatter.8

commit v4 on v3

--- a/solution.py
+++ b/solution.py
@@ -470,8 +470,81 @@
     )(values, parts)
 
 
+def product_slots(count):
+    slots = []
+    for pair in range(count // 2)[::-1]:
+        slots += [2 * pair - 1, 2 * pair] if slots and pair else [2 * pair + 1, 2 * pair - 1, 2 * pair] if pair else [0]
+    return slots
+
+
+def load_operands(count, me, flipped, left_from, right_from, left, right, left_in, right_in):
+    rows = left.shape[0] // count
+    width = right.shape[0] if flipped else right.shape[1]
+    tile = min(512, width)
+
+    def left_copy(slot):
+        span_rows = pl.ds(pl.multiple_of(flip(me, slot) * rows, rows), rows)
+        return pltpu.make_async_copy(left_from.at[span_rows], left.at[span_rows], left_in.at[slot])
+
+    def right_copy(index):
+        span_tile = pl.ds(pl.multiple_of(index * tile, tile), tile)
+        place = (span_tile,) if flipped else (slice(None), span_tile)
+        return pltpu.make_async_copy(right_from.at[place], right.at[place], right_in.at[index])
+
+    slots = product_slots(count)
+    right_copy(0).start()
+    left_copy(slots[0]).start()
+    for index in range(1, width // tile):
+        right_copy(index).start()
+    for slot in slots[1:]:
+        left_copy(slot).start()
+    return lambda slot: left_copy(slot).wait(), lambda index: right_copy(index).wait()
+
+
+def operand_scratch(count, left, right, flipped):
+    width = right.shape[0] if flipped else right.shape[1]
+    return [
+        pltpu.VMEM(left.shape, BF16),
+        pltpu.VMEM(right.shape, BF16),
+        DMA((count,)),
+        DMA((width // min(512, width),)),
+    ]
+
+
+def fetch(sources, targets, arrived):
+    items = [
+        pltpu.make_async_copy(source, target, arrived.at[index])
+        for index, (source, target) in enumerate(zip(sources, targets))
+    ]
+    for item in items:
+        item.start()
+
+    def wait():
+        for item in items:
+            item.wait()
+
+    return wait
+
+
 def product_scatter(
-    count, me, group, parts, flipped, left, right, done, kept, near_out, near_in, far_out, far_in, ns, nr, fs, fr
+    count,
+    me,
+    group,
+    parts,
+    flipped,
+    left,
+    right,
+    done,
+    kept,
+    near_out,
+    near_in,
+    far_out,
+    far_in,
+    ns,
+    nr,
+    fs,
+    fr,
+    ready=None,
 ):
     rows, width = kept.shape
     piece = rows // parts
@@ -482,10 +555,14 @@
 
     def product(slot, store):
         start = pl.multiple_of(flip(me, slot) * rows, rows)
+        if ready:
+            ready[0](slot)
         block = left[pl.ds(start, rows), :]
 
         def step(index, carry):
             columns = pl.ds(pl.multiple_of(index * tile, tile), tile)
+            if ready and slot == count - 1:
+                ready[1](index)
             if flipped:
                 value = nt(block, right[columns, :])
             else:
@@ -708,13 +785,13 @@
 
 def back_kernel(
     count,
-    left,
-    right,
-    middle,
-    cotangent,
+    left_from,
+    right_from,
+    middle_from,
+    cotangent_from,
     gain,
-    attended,
-    out_weight,
+    attended_from,
+    out_weight_from,
     d_middle,
     d_gain,
     d_attended,
@@ -723,12 +800,27 @@
     gathered,
     turned,
     out_sum,
+    left,
+    right,
+    left_in,
+    right_in,
+    middle,
+    cotangent,
+    attended,
+    out_weight,
+    others_in,
     *scratch,
 ):
     me = lax.axis_index("ctx")
     group = lax.axis_index("fsdp")
     piece = middle.shape[0] // BACK_PARTS
     own = me * middle.shape[0]
+    ready = load_operands(count, me, True, left_from, right_from, left, right, left_in, right_in)
+    fetched = fetch(
+        (middle_from, cotangent_from, attended_from, out_weight_from),
+        (middle, cotangent, attended, out_weight),
+        others_in,
+    )
     greet([(flip(me, bit), group) for bit in bits_of(count)])
     start, finish = gather_rows(count, me, group, BACK_PARTS, None, gathered, *scratch[SCATTER:])
     d_gain[...] = jnp.zeros_like(d_gain)
@@ -748,9 +840,10 @@
         start(part)
 
     begin, _, pass_on, end, close = product_scatter(
-        count, me, group, BACK_PARTS, True, left, right, done, *scratch[:SCATTER]
+        count, me, group, BACK_PARTS, True, left, right, done, *scratch[:SCATTER], ready=ready
     )
     begin()
+    fetched()
     out_sum[...] = jnp.zeros_like(out_sum)
 
     def turn(index, carry):
@@ -787,13 +880,21 @@
             shape((tokens, wide), BF16),
             shape((wide, width), BF16),
         ],
-        in_specs=[VMEM] * 7,
+        in_specs=[ANY] * 4 + [VMEM] + [ANY] * 2,
         out_specs=[VMEM] * 4,
         scratch_shapes=[
             pltpu.VMEM((rows // BACK_PARTS, width), F32),
             pltpu.VMEM((tokens, width), BF16),
             pltpu.VMEM((wide, tokens), BF16),
             pltpu.VMEM((wide, width), F32),
+        ]
+        + operand_scratch(count, left, right, True)
+        + [
+            pltpu.VMEM((rows, width), F32),
+            pltpu.VMEM((rows, width), BF16),
+            pltpu.VMEM((tokens, wide), BF16),
+            pltpu.VMEM((wide, width), BF16),
+            DMA((4,)),
         ]
         + scatter_scratch(count, rows, width, BACK_PARTS)
         + gather_scratch(count, BACK_PARTS)[:2],
@@ -862,9 +963,9 @@
 def mlp_kernel(
     count,
     groups,
-    activated,
-    weight,
-    middle,
+    activated_from,
+    weight_from,
+    middle_from,
     upstream,
     both,
     second,
@@ -879,6 +980,12 @@
     both_in,
     second_in,
     parts_out,
+    activated,
+    weight,
+    activated_in,
+    weight_in,
+    middle,
+    others_in,
     *scratch,
 ):
     me = lax.axis_index("ctx")
@@ -887,10 +994,14 @@
     tokens, own = activated.shape
     block = up_slots.shape[1]
     columns = second_slots.shape[2]
+    ready = load_operands(
+        count, me, False, activated_from, weight_from, activated, weight, activated_in, weight_in
+    )
+    fetched = fetch((middle_from,), (middle,), others_in)
     greet([(flip(me, bit), group) for bit in bits_of(count)])
 
     def rows_in(index):
-        slot = lax.rem(index, 2)
+        slot = lax.rem(index, 4)
         rows = pl.ds(pl.multiple_of(index * block, block), block)
         return (
             pltpu.make_async_copy(upstream.at[rows], up_slots.at[slot], up_in.at[slot]),
@@ -914,7 +1025,7 @@
             for owner in range(groups)
         ]
 
-    for item in rows_in(0):
+    for item in rows_in(0) + rows_in(1):
         item.start()
     second_copy(0).start()
 
@@ -923,30 +1034,32 @@
         output[span_rows, :] = (middle[span_rows, :] + value).astype(BF16)
 
     begin, _, pass_on, end, close = product_scatter(
-        count, me, group, 2, False, activated, weight, done, *scratch
+        count, me, group, 2, False, activated, weight, done, *scratch, ready=ready
     )
     begin()
+    fetched()
     steps = tokens // block
 
     def activation(index, carry):
-        @pl.when(index + 1 < steps)
+        @pl.when(2 * index + 2 < steps)
         def _():
-            for item in rows_in(index + 1):
+            for item in rows_in(2 * index + 2) + rows_in(2 * index + 3):
                 item.start()
 
-        for item in rows_in(index):
+        for item in rows_in(2 * index) + rows_in(2 * index + 1):
             item.wait()
-        slot = lax.rem(index, 2)
-        rows = pl.ds(pl.multiple_of(index * block, block), block)
-        grad = nt(up_slots[slot], weight[...]).astype(BF16).astype(F32)
-        gate = both_slots[slot, :, :own]
-        up = both_slots[slot, :, own:]
-        sigmoid = 1.0 / (1.0 + jnp.exp(-gate))
-        d_both[rows, :own] = (grad * up * sigmoid * (1.0 + gate * (1.0 - sigmoid))).astype(BF16)
-        d_both[rows, own:] = (grad * gate * sigmoid).astype(BF16)
+        slots = [lax.rem(2 * index + turn, 4) for turn in (0, 1)]
+        grads = [nt(up_slots[slot], weight[...]).astype(BF16).astype(F32) for slot in slots]
+        for turn, (slot, grad) in enumerate(zip(slots, grads)):
+            rows = pl.ds(pl.multiple_of((2 * index + turn) * block, block), block)
+            gate = both_slots[slot, :, :own]
+            up = both_slots[slot, :, own:]
+            sigmoid = 1.0 / (1.0 + jnp.exp(-gate))
+            d_both[rows, :own] = (grad * up * sigmoid * (1.0 + gate * (1.0 - sigmoid))).astype(BF16)
+            d_both[rows, own:] = (grad * gate * sigmoid).astype(BF16)
         return carry
 
-    lax.fori_loop(0, steps, activation, 0)
+    lax.fori_loop(0, steps // 2, activation, 0)
 
     def weight_grad(index, carry):
         @pl.when(index + 1 < count)
@@ -992,18 +1105,20 @@
             shape((tokens, 2 * own), BF16),
             shape((groups, count, columns // groups, 2 * own), BF16),
         ],
-        in_specs=[VMEM] * 3 + [ANY] * 3,
+        in_specs=[ANY] * 6,
         out_specs=[VMEM, VMEM, ANY],
         scratch_shapes=[
-            pltpu.VMEM((2, block, width), BF16),
-            pltpu.VMEM((2, block, 2 * own), F32),
+            pltpu.VMEM((4, block, width), BF16),
+            pltpu.VMEM((4, block, 2 * own), F32),
             pltpu.VMEM((2, tokens, columns), BF16),
             pltpu.VMEM((2, columns, 2 * own), BF16),
-            DMA((2,)),
-            DMA((2,)),
+            DMA((4,)),
+            DMA((4,)),
             DMA((2,)),
             DMA((2, groups)),
         ]
+        + operand_scratch(count, activated, weight, False)
+        + [pltpu.VMEM((rows, width), F32), DMA((1,))]
         + scatter_scratch(count, rows, width),
         compiler_params=comm_params(collective),
         cost_estimate=cost(48),
@@ -1250,6 +1365,8 @@
 
 def attention_and_joined_back_kernel(
     heads,
+    count,
+    groups,
     runs,
     d_attended,
     queries,
@@ -1263,9 +1380,12 @@
     q_gain,
     k_gain,
     share,
+    normed,
+    d_out,
     d_joined,
     d_q_gain,
     d_k_gain,
+    parts,
     d_queries,
     d_keys,
     d_values,
@@ -1275,8 +1395,17 @@
     cosine_here,
     sine_here,
     placed,
+    normed_slots,
     loaded,
+    normed_in,
 ):
+    columns = normed_slots.shape[2]
+
+    def normed_copy(index):
+        slot = lax.rem(index, 2)
+        span_columns = pl.ds(pl.multiple_of(index * columns, columns), columns)
+        return pltpu.make_async_copy(normed.at[:, span_columns], normed_slots.at[slot], normed_in.at[slot])
+
     loads = [
         pltpu.make_async_copy(source, target, loaded.at[index])
         for index, (source, target) in enumerate(
@@ -1285,6 +1414,7 @@
     ]
     for item in loads:
         item.start()
+    normed_copy(0).start()
     attention_back_kernel(
         heads, runs, d_attended, queries, keys, values, mixed, lse, d_queries, d_keys, d_values, arrived, keys_turned
     )
@@ -1307,19 +1437,65 @@
         d_k_gain,
         placed,
     )
+    rows = columns // groups
+    width = d_joined.shape[1]
+
+    def weight_grad(index, carry):
+        @pl.when(index + 1 < count)
+        def _():
+            normed_copy(index + 1).start()
+
+        normed_copy(index).wait()
+        value = lax.dot_general(
+            normed_slots[lax.rem(index, 2)], d_joined[...], (((0,), (0,)), ((), ())), preferred_element_type=F32
+        ).astype(BF16)
+        for owner in range(groups):
+            parts[owner, index] = value[owner * rows : (owner + 1) * rows]
+        return carry
+
+    lax.fori_loop(0, count, weight_grad, 0)
+    for owner in range(groups):
+        for extra in range(d_out.shape[1] // width):
+            parts[owner, count + extra] = d_out[
+                owner * rows : (owner + 1) * rows, extra * width : (extra + 1) * width
+            ]
 
 
 def attention_and_joined_back(
-    heads, runs, d_attended, queries, keys, values, mixed, lse, raw, cosine, sine, q_gain, k_gain, share
+    heads,
+    count,
+    groups,
+    runs,
+    d_attended,
+    queries,
+    keys,
+    values,
+    mixed,
+    lse,
+    raw,
+    cosine,
+    sine,
+    q_gain,
+    k_gain,
+    share,
+    normed,
+    d_out,
 ):
     tokens = keys.shape[0]
+    columns = normed.shape[1] // count
+    blocks = count + d_out.shape[1] // raw.shape[1]
     wide = heads * CONT
     shape = jax.ShapeDtypeStruct
     return pl.pallas_call(
-        functools.partial(attention_and_joined_back_kernel, heads),
-        out_shape=[shape(raw.shape, BF16), shape((1, HEAD), F32), shape((1, HEAD), F32)],
-        in_specs=[SMEM] + [VMEM] * 6 + [ANY] * 3 + [VMEM] * 3,
-        out_specs=[VMEM] * 3,
+        functools.partial(attention_and_joined_back_kernel, heads, count, groups),
+        out_shape=[
+            shape(raw.shape, BF16),
+            shape((1, HEAD), F32),
+            shape((1, HEAD), F32),
+            shape((groups, blocks, columns // groups, raw.shape[1]), BF16),
+        ],
+        in_specs=[SMEM] + [VMEM] * 6 + [ANY] * 3 + [VMEM] * 3 + [ANY, VMEM],
+        out_specs=[VMEM] * 4,
         scratch_shapes=[
             pltpu.VMEM((tokens, wide), BF16),
             pltpu.VMEM((tokens, HEAD), F32),
@@ -1330,11 +1506,13 @@
             pltpu.VMEM(cosine.shape, F32),
             pltpu.VMEM(sine.shape, F32),
             pltpu.VMEM(raw.shape, BF16),
+            pltpu.VMEM((2, tokens, columns), BF16),
             DMA((3,)),
+            DMA((2,)),
         ],
         compiler_params=pltpu.CompilerParams(vmem_limit_bytes=VMEM_LIMIT),
         cost_estimate=cost(30),
-    )(runs, d_attended, queries, keys, values, mixed, lse, raw, cosine, sine, q_gain, k_gain, share)
+    )(runs, d_attended, queries, keys, values, mixed, lse, raw, cosine, sine, q_gain, k_gain, share, normed, d_out)
 
 
 def joined_back(heads, runs, raw, d_queries, d_keys, d_values, cosine, sine, q_gain, k_gain, share):
@@ -1452,9 +1630,26 @@
     share = jnp.ones((2, HEAD), F32)
     tables = (cosine, sine, q_gain_row, k_gain_row)
     if repeat == 1:
-        d_joined, q_gain_grad, k_gain_grad = attention_and_joined_back(
-            heads, run_order, d_attended, queries, keys, values, mixed, lse, raw, *tables, share
+        d_joined, q_gain_grad, k_gain_grad, parts = attention_and_joined_back(
+            heads,
+            count,
+            groups,
+            run_order,
+            d_attended,
+            queries,
+            keys,
+            values,
+            mixed,
+            lse,
+            raw,
+            *tables,
+            share,
+            normed,
+            d_out,
         )
+        parts, gu_parts, d_joined = lax.optimization_barrier((parts, gu_parts, d_joined))
+        qkv_grad_parts = scatter_groups(parts.reshape((-1,) + parts.shape[2:]))
+        d_out = qkv_grad_parts[count:].transpose(1, 0, 2).reshape(-1, width)
     else:
         d_queries, d_keys, d_values = attention_back(
             heads, run_order, d_attended, queries, keys, values, mixed, lse
@@ -1466,11 +1661,8 @@
         d_joined, q_gain_grad, k_gain_grad = joined_back(
             heads, run_order, raw, d_queries, d_keys, d_values, *tables, share
         )
-    normed, d_joined, gu_parts = lax.optimization_barrier((normed, d_joined, gu_parts))
-    qkv_grad_parts, d_joined = lax.optimization_barrier((weight_grad(normed, d_joined), d_joined))
-    d_out, gu_parts = lax.optimization_barrier((d_out, gu_parts))
-    d_out = scatter_groups(d_out)
-    qkv_grad_parts = scatter_groups(qkv_grad_parts)
+        d_out = scatter_groups(d_out)
+        qkv_grad_parts = scatter_groups(weight_grad(normed, d_joined))
     d_hidden, attn_gain_grad, d_gate_up = back_to_input(
         count, 8, d_joined, w_qkv, hidden_in[0], d_middle, attn_gain[None, :], gu_parts
     )

time: 554 us -> 544 us (0.982)
  matrix products: 47.3 us -> 38.7 us
    pallas_call x1, Pallas kernels: 25.1 us -> 33.7 us  [attention_and_joined_back(): pl.pallas_call(functools.partial(attention_and_joined_back_kernel, heads,...]
    dot_general x1 -> x0, matrix products: 8.53 us -> none  [weight_grad(): lax.dot_general(left, right, (((0,), (0,)), ((), ())), preferred_element_...]
    pallas_call x1, Pallas kernels: 55.3 us -> 49.7 us  [back_through_mlp(): pl.pallas_call(functools.partial(mlp_kernel, count, groups), out_shape=[s...]
  transfers between devices with their start and end apart: 12 -> 11, of which waited for: 5 -> 5; matrix products, arithmetic and copies ran while one was open for 12% -> 10% of each run, Pallas kernels for 78% -> 79%
where the time goes in v4:
time: 544 us; the launch traced here: 539 us
  Pallas kernels  441 us (81%)
  matrix products  38.7 us (7%)
  local copies, waits for them, and re-layouts  16.7 us (3%)
  between operations  14.9 us (3%)
  waiting for transfers between devices  11.6 us (2%)
  other arithmetic  9.62 us (2%)
  starting transfers between devices  5.9 us (1%)
    pallas_call x1, Pallas kernels, back_through_middle(): pl.pallas_call(functools.partial(back_kernel, count), out_shape=[shape((r...  92.2 us
    pallas_call x1, Pallas kernels, middle_and_second(): pl.pallas_call(functools.partial(middle_kernel, count), out_shape=[jax.Sh...  83.7 us
    pallas_call x1, Pallas kernels, back_to_input(): pl.pallas_call(functools.partial(input_kernel, count), out_shape=[shape((...  62.3 us
    pallas_call x1, Pallas kernels, back_through_mlp(): pl.pallas_call(functools.partial(mlp_kernel, count, groups), out_shape=[s...  49.7 us
    pallas_call x1, Pallas kernels, opening(): pl.pallas_call(functools.partial(opening_kernel, count), out_shape=[jax.S...  43.3 us
    pallas_call x1, Pallas kernels, attention_and_joined_back(): pl.pallas_call(functools.partial(attention_and_joined_back_kernel, heads,...  33.7 us
    pallas_call x1, Pallas kernels, spread(): pl.pallas_call(functools.partial(spread_kernel, count), out_shape=[jax.Sh...  28.6 us
    pallas_call x1, Pallas kernels, attention(): pl.pallas_call(functools.partial(attention_kernel, heads), out_shape=[sha...  20.5 us
  transfers between devices with their start and end apart: 11, of which 5 were waited for; matrix products, arithmetic and copies ran while one was open for 10% of the time, Pallas kernels for 79%

profile of v4, /device:TPU:0, one launch (start us, length us, event | category | flops | bytes accessed | tf_op | source)
XLA Modules:
  0.0 538.9 jit_solution(15906061077998692596)
XLA Ops:
  8.0 28.6 %shard_map.213 = (bf16[8,64,512]{2,1,0:T(8,128)(2,1)}, bf16[8,64,1536]{2,1,0:T(8,128)(2,1)}) custom-call(bf16[64,4096]{1,0:T(8,128)(2,1)} %qkv.1, bf16[64,12288]{1,0:T(8,128)(2,1)} %mlp.1), custom_call_target="tpu_custom_call" | custom-call | bytes 28000000 | tf_op jit(solution)/shard_map/pallas_call | solution.py:263
  36.6 3.7 all-gather.5.cloned.1.call-done.right.out_weight_from
  42.5 1.5 fusion.1
  44.0 2.0 fusion.3.normed
  46.0 43.3 %shard_map.214 = (bf16[2048,2048]{1,0:T(8,128)(2,1)}, s32[8,8,128]{2,1,0:T(8,128)}) custom-call(bf16[256,2048]{1,0:T(8,128)(2,1)} %fusion.3.normed, s32[1,8,128]{2,1,0:T(8,128)} %scatter.4.runs), custom_call_target="tpu_custom_call" | custom-call | bytes 45000000 | tf_op jit(solution)/shard_map/pallas_call | solution.py:293
  89.5 1.6 collective-permute-start
  91.2 1.5 collective-permute-start.1
  92.6 10.9 %fusion.5.joined = f32[2048,512]{1,0:T(8,128)} fusion(bf16[2048,2048]{1,0:T(8,128)(2,1)} %get-tuple-element.87.normed, bf16[2048,512]{1,0:T(8,128)(2,1)} %bitcast.58), kind=kOutput, calls=%fused_computation.25 | convolution fusion | flops 4294967296 | bytes 14680064 | tf_op jit(solution)/shard_map/dot_general | solution.py:1595
  105.9 1.5 collective-permute-start.2
  109.3 20.5 %shard_map.215 = (bf16[2048,256]{1,0:T(8,128)(2,1)}, f32[2048,512]{1,0:T(8,128)}, bf16[16,256,128]{2,1,0:T(8,128)(2,1)}, bf16[2048,128]{1,0:T(8,128)(2,1)}, bf16...) custom-call(s32[64]{0:T(128)} %reshape_squeeze.3.runs, f32[2048,512]{1,0:T(8,128)} %fusion.5.joined, ...), custom_call_target="tpu_custom_call" | custom-call | bytes 15000000 | tf_op jit(solution)/shard_map/pallas_call | solution.py:1219
  130.4 83.7 %shard_map.216 = (f32[256,2048]{1,0:T(8,128)}, bf16[2048,2048]{1,0:T(8,128)(2,1)}) custom-call(bf16[2048,256]{1,0:T(8,128)(2,1)} %get-tuple-element.94.left.attended_from, bf16[256,2048]{1,0:T(8,128)(2,1)} %all-gather.5.cloned.1.call-done.right.out_weight_from, bf16[256,2048]{1,0:T(8,128)(2,1)} %bitcast.50, f32[1,2048]{1,0:T(1,128)} %bitcast.63), custom_call_target="tpu_custom_call" | custom-call | bytes 80000000 | tf_op jit(solution)/shard_map/pallas_call | solution.py:770
  214.2 17.4 %fusion.6.both = f32[2048,1536]{1,0:T(8,128)S(1)} fusion(bf16[2048,2048]{1,0:T(8,128)(2,1)} %get-tuple-element.96.second, bf16[2048,1536]{1,0:T(8,128)(2,1)} %bitcast.53), kind=kOutput, calls=%fused_computation.26 | convolution fusion | flops 12884901888 | bytes 27262976 | tf_op jit(solution)/shard_map/dot_general | solution.py:1605
  231.6 4.5 copy-done
  236.1 2.1 fusion.activated_from
  238.2 14.0 %shard_map.217.upstream = bf16[2048,2048]{1,0:T(8,128)(2,1)} custom-call(bf16[2,128,2048]{2,1,0:T(8,128)(2,1)} %copy-done.5, bf16[2,128,2048]{2,1,0:T(8,128)(2,1)} %collective-permute-done.2.refs_1_, bf16[2,128,2048]{2,1,0:T(8,128)(2,1)} %copy-done.4, bf16[2,128,2048]{2,1,0:T(8,128)(2,1)} %copy-done.8), custom_call_target="tpu_custom_call" | custom-call | bytes 13000000 | tf_op jit(solution)/shard_map/pallas_call | solution.py:362
  252.2 10.5 %convolution_convert_fusion = bf16[768,2048]{1,0:T(8,128)(2,1)} fusion(bf16[2048,768]{1,0:T(8,128)(2,1)S(1)} %fusion.activated_from, bf16[2048,2048]{1,0:T(8,128)(2,1)} %shard_map.217.upstream), kind=kOutput, calls=%fused_computation.2 | convolution fusion | flops 6444023808 | bytes 14680064 | tf_op jit(solution)/shard_map/dot_general | solution.py:1612
  262.8 4.9 all-gather.11.cloned.1.call-done.weight_from
  267.6 49.7 %shard_map.218 = (bf16[256,2048]{1,0:T(8,128)(2,1)}, bf16[2048,1536]{1,0:T(8,128)(2,1)}, bf16[4,8,64,1536]{3,2,1,0:T(8,128)(2,1)}) custom-call(bf16[2048,768]{1,0:T(8,128)(2,1)} %copy-done.2, bf16[768,2048]{1,0:T(8,128)(2,1)} %all-gather.11.cloned.1.call-done.weight_from, f32[256,2048]{1,0:T(8,128)} %get-tuple-element.101.middle_from, ...), custom_call_target="tpu_custom_call" | custom-call | bytes 48000000 | tf_op jit(solution)/shard_map/pallas_call | solution.py:1101
  317.4 92.2 %shard_map.219 = (f32[256,2048]{1,0:T(8,128)}, f32[1,2048]{1,0:T(1,128)}, bf16[2048,256]{1,0:T(8,128)(2,1)}, bf16[256,2048]{1,0:T(8,128)(2,1)}) custom-call(bf16[2048,1536]{1,0:T(8,128)(2,1)} %get-tuple-element.108.left_from, bf16[2048,1536]{1,0:T(8,128)(2,1)} %bitcast.54, f32[256,2048]{1,0:T(8,128)} %get-tuple-element.101.middle_from, ...), custom_call_target="tpu_custom_call" | custom-call | bytes 85000000 | tf_op jit(solution)/shard_map/pallas_call | solution.py:875
  410.2 33.7 %shard_map.220 = (bf16[2048,512]{1,0:T(8,128)(2,1)}, f32[1,128]{1,0:T(1,128)}, f32[1,128]{1,0:T(1,128)}, bf16[4,12,64,512]{3,2,1,0:T(8,128)(2,1)}) custom-call(s32[64]{0:T(128)} %reshape_squeeze.3.runs, bf16[2048,256]{1,0:T(8,128)(2,1)} %get-tuple-element.111.d_attended, bf16[16,256,128]{2,1,0:T(8,128)(2,1)} %get-tuple-element.112.queries, ...), custom_call_target="tpu_custom_call" | custom-call | bytes 30000000 | tf_op jit(solution)/shard_map/pallas_call | solution.py:1489
  445.4 62.3 %shard_map.221 = (f32[256,2048]{1,0:T(8,128)}, f32[1,2048]{1,0:T(1,128)}, f32[64,12288]{1,0:T(8,128)}) custom-call(bf16[2048,512]{1,0:T(8,128)(2,1)} %get-tuple-element.122.left, bf16[2048,512]{1,0:T(8,128)(2,1)} %bitcast.59, bf16[256,2048]{1,0:T(8,128)(2,1)} %bitcast.51, f32[256,2048]{1,0:T(8,128)} %get-tuple-element.123.d_middle, f32[1,2048]{1,0:T(1,128)} %bitcast.65, ...), custom_call_target="tpu_custom_call" | custom-call | bytes 60000000 | tf_op jit(solution)/shard_map/pallas_call | solution.py:942
  507.8 1.5 fusion.4.values
  509.2 13.2 %shard_map.222 = (f32[16,128]{1,0:T(8,128)}, f32[16,128]{1,0:T(8,128)}, f32[1,128]{1,0:T(1,128)}, f32[1,128]{1,0:T(1,128)}, f32[64,4096]{1,0:T(8,128)}) custom-call(f32[40,128]{1,0:T(8,128)} %fusion.4.values, bf16[12,64,512]{2,1,0:T(8,128)(2,1)} %reduce-scatter.8.cloned.1.call-done.parts), custom_call_target="tpu_custom_call" | custom-call | bytes 14000000 | tf_op jit(solution)/shard_map/pallas_call | solution.py:449
  529.9 1.7 copy.41
  (82 shorter events, 17.5 us)
Async XLA Ops:
  7.2 36.8 %copy-start.1 = (bf16[1,256,2048]{2,1,0:T(8,128)(2,1)S(1)}, bf16[1,256,2048]{2,1,0:T(8,128)(2,1)}, u32[]{:S(2)}) copy-start(bf16[1,256,2048]{2,1,0:T(8,128)(2,1)} %param.16) | copy-start | bytes 3145732
  7.2 33.1 %all-gather.5.cloned.1.call-start = ((), (), s32[]{:S(2)}) async-start(), calls=%async_computation.3 | async-start | bytes 1310720 | tf_op jit(solution)/shard_map/all_gather | solution.py:1570
  7.9 81.5 %copy-start.3 = (bf16[1,256,2048]{2,1,0:T(8,128)(2,1)S(1)}, bf16[1,256,2048]{2,1,0:T(8,128)(2,1)}, u32[]{:S(2)}) copy-start(bf16[1,256,2048]{2,1,0:T(8,128)(2,1)} %param.27) | copy-start | bytes 3145732
  7.9 81.4 %all-gather.7.cloned.1.call-start = ((), (), s32[]{:S(2)}) async-start(), calls=%async_computation.4 | async-start | bytes 2621440 | tf_op jit(solution)/shard_map/all_gather | solution.py:1570
  40.3 173.9 %all-gather.9.cloned.1.call-start = ((), (), s32[]{:S(2)}) async-start(), calls=%async_computation.5 | async-start | bytes 7864320 | tf_op jit(solution)/shard_map/all_gather | solution.py:1570
  89.4 178.3 %all-gather.11.cloned.1.call-start = ((), (), s32[]{:S(2)}) async-start(), calls=%async_computation.6 | async-start | bytes 3932160 | tf_op jit(solution)/shard_map/all_gather | solution.py:1570
  89.5 14.3 %collective-permute-start = (bf16[1,128,2048]{2,1,0:T(8,128)(2,1)S(1)}, bf16[1,128,2048]{2,1,0:T(8,128)(2,1)S(1)}, u32[]{:S(2)}, u32[]{:S(2)}) collective-permute-start(bf16[1,128,2048]{2,1,0:T(8,128)(2,1)S(1)} %get-tuple-element.141), channel_id=1, source_target_pairs={{0,8},{4,12},{8,0},{12,4},{16,24},{20,28},{24,16},{28,20},{1,9},{5... | collective-permute-start | bytes 1572872 | tf_op jit(solution)/shard_map/ppermute | solution.py:308
  91.2 14.0 %collective-permute-start.1 = (bf16[1,128,2048]{2,1,0:T(8,128)(2,1)S(1)}, bf16[1,128,2048]{2,1,0:T(8,128)(2,1)S(1)}, u32[]{:S(2)}, u32[]{:S(2)}) collective-permute-start(bf16[1,128,2048]{2,1,0:T(8,128)(2,1)S(1)} %get-tuple-element.140), channel_id=1, source_target_pairs={{0,16},{4,20},{8,24},{12,28},{16,0},{20,4},{24,8},{28,12},{1,17},{... | collective-permute-start | bytes 1572872 | tf_op jit(solution)/shard_map/ppermute | solution.py:308
  105.2 24.6 %copy-start.4 = (bf16[2,128,2048]{2,1,0:T(8,128)(2,1)}, bf16[2,128,2048]{2,1,0:T(8,128)(2,1)S(1)}, u32[]{:S(2)}) copy-start(bf16[2,128,2048]{2,1,0:T(8,128)(2,1)S(1)} %pad_maximum_fusion.1.refs_2_) | copy-start | bytes 3145732
  105.2 24.6 %collective-permute-start.3 = (bf16[2,128,2048]{2,1,0:T(8,128)(2,1)S(1)}, bf16[2,128,2048]{2,1,0:T(8,128)(2,1)S(1)}, u32[]{:S(2)}, u32[]{:S(2)}) collective-permute-start(bf16[2,128,2048]{2,1,0:T(8,128)(2,1)S(1)} %pad_maximum_fusion.1.refs_2_), channel_id=1, source_target_pairs={{0,8},{4,12},{8,0},{12,4},{16,24},{20,28},{24,16},{28,20},{1,9},{5... | collective-permute-start | bytes 3145736 | tf_op jit(solution)/shard_map/ppermute | solution.py:308
  105.9 108.3 %copy-start.5 = (bf16[2,128,2048]{2,1,0:T(8,128)(2,1)}, bf16[2,128,2048]{2,1,0:T(8,128)(2,1)S(1)}, u32[]{:S(2)}) copy-start(bf16[2,128,2048]{2,1,0:T(8,128)(2,1)S(1)} %pad_maximum_fusion.refs_0_) | copy-start | bytes 3145732
  105.9 24.5 %collective-permute-start.2 = (bf16[2,128,2048]{2,1,0:T(8,128)(2,1)S(1)}, bf16[2,128,2048]{2,1,0:T(8,128)(2,1)}, u32[]{:S(2)}, u32[]{:S(2)}) collective-permute-start(bf16[2,128,2048]{2,1,0:T(8,128)(2,1)S(1)} %pad_maximum_fusion.refs_0_), channel_id=1, source_target_pairs={{0,16},{4,20},{8,24},{12,28},{16,0},{20,4},{24,8},{28,12},{1,17},{... | collective-permute-start | bytes 3145736 | tf_op jit(solution)/shard_map/ppermute | solution.py:308
  107.5 302.2 %reduce-scatter.4.cloned.1.call-start = ((), (), s32[]{:S(2)}) async-start(), calls=%async_computation.7 | async-start | bytes 3932160 | tf_op jit(solution)/shard_map/reduce_scatter | solution.py:1573
  129.9 84.3 %copy-start.8 = (bf16[2,128,2048]{2,1,0:T(8,128)(2,1)}, bf16[2,128,2048]{2,1,0:T(8,128)(2,1)S(1)}, u32[]{:S(2)}) copy-start(bf16[2,128,2048]{2,1,0:T(8,128)(2,1)S(1)} %collective-permute-done.3.refs_3_) | copy-start | bytes 3145732
  238.2 14.0 %copy-start.2 = (bf16[2048,768]{1,0:T(8,128)(2,1)}, bf16[2048,768]{1,0:T(8,128)(2,1)S(1)}, u32[]{:S(2)}) copy-start(bf16[2048,768]{1,0:T(8,128)(2,1)S(1)} %fusion.activated_from) | copy-start | bytes 9437188
  262.7 181.3 %reduce-scatter.6.cloned.1.call-start = ((), (), s32[]{:S(2)}) async-start(), calls=%async_computation.8 | async-start | bytes 7864320 | tf_op jit(solution)/shard_map/reduce_scatter | solution.py:1573
  317.3 191.9 %reduce-scatter.8.cloned.1.call-start = ((), (), s32[]{:S(2)}) async-start(), calls=%async_computation.9 | async-start | bytes 3932160 | tf_op jit(solution)/shard_map/reduce_scatter | solution.py:1573
  410.2 33.8 %copy-start.11 = (bf16[192,2048]{1,0:T(8,128)(2,1)S(1)}, bf16[192,2048]{1,0:T(8,128)(2,1)}, u32[]{:S(2)}) copy-start(bf16[192,2048]{1,0:T(8,128)(2,1)} %reduce-scatter.4.cloned.1.call-done) | copy-start | bytes 2359300
  445.4 62.4 %copy-start.12 = (f32[1,2048]{1,0:T(1,128)S(1)}, f32[1,2048]{1,0:T(1,128)}, u32[]{:S(2)}) copy-start(f32[1,2048]{1,0:T(1,128)} %get-tuple-element.129) | copy-start | bytes 24580
  445.4 62.4 %copy-start.15 = (f32[1,128]{1,0:T(1,128)S(1)}, f32[1,128]{1,0:T(1,128)}, u32[]{:S(2)}) copy-start(f32[1,128]{1,0:T(1,128)} %get-tuple-element.130) | copy-start | bytes 1540
  445.4 62.4 %copy-start.16 = (f32[1,128]{1,0:T(1,128)S(1)}, f32[1,128]{1,0:T(1,128)}, u32[]{:S(2)}) copy-start(f32[1,128]{1,0:T(1,128)} %get-tuple-element.131) | copy-start | bytes 1540
  445.4 79.0 %copy-start.9 = (bf16[256,2048]{1,0:T(8,128)(2,1)S(1)}, bf16[256,2048]{1,0:T(8,128)(2,1)}, u32[]{:S(2)}) copy-start(bf16[256,2048]{1,0:T(8,128)(2,1)} %get-tuple-element.105) | copy-start | bytes 3145732
  507.7 17.7 %copy-start.7 = (f32[256,2048]{1,0:T(8,128)S(1)}, f32[256,2048]{1,0:T(8,128)}, u32[]{:S(2)}) copy-start(f32[256,2048]{1,0:T(8,128)} %get-tuple-element.127) | copy-start | bytes 6291460
  524.4 5.5 %copy-start.6 = (f32[64,12288]{1,0:T(8,128)S(1)}, f32[64,12288]{1,0:T(8,128)}, u32[]{:S(2)}) copy-start(f32[64,12288]{1,0:T(8,128)} %get-tuple-element.160) | copy-start | bytes 9437188
  (6 other events, 26.9 us)
Sparse Core Ops, SparseCore 0:
  9.6 30.6 all-gather.4
  41.8 45.4 all-gather.6
  89.5 114.9 all-gather.8
  205.9 61.6 all-gather.10
  269.8 58.8 reduce-scatter.3
  330.9 110.7 reduce-scatter.5
  444.6 60.8 reduce-scatter.7

commit v5 on v4

--- a/solution.py
+++ b/solution.py
@@ -148,25 +148,27 @@
 def trade(count, me, group, pieces, source, target, send, recv):
     copies = []
     local = []
-    for slot in list(range(1, count)) + [0]:
-        peer = flip(me, slot)
-        for number, (origin, place) in enumerate(pieces(peer, me)):
-            total = len(pieces(peer, me))
-            index = slot * total + number
-            if slot == 0:
-                item = pltpu.make_async_copy(source.at[origin], target.at[place], send.at[index])
-                local.append(item)
-            else:
-                item = pltpu.make_async_remote_copy(
-                    source.at[origin],
-                    target.at[place],
-                    send.at[index],
-                    recv.at[index],
-                    device_id=(peer, group),
-                    device_id_type=MESH,
-                )
-                copies.append(item)
-            item.start()
+
+    def start(slots):
+        for slot in slots:
+            peer = flip(me, slot)
+            for number, (origin, place) in enumerate(pieces(peer, me)):
+                total = len(pieces(peer, me))
+                index = slot * total + number
+                if slot == 0:
+                    item = pltpu.make_async_copy(source.at[origin], target.at[place], send.at[index])
+                    local.append(item)
+                else:
+                    item = pltpu.make_async_remote_copy(
+                        source.at[origin],
+                        target.at[place],
+                        send.at[index],
+                        recv.at[index],
+                        device_id=(peer, group),
+                        device_id_type=MESH,
+                    )
+                    copies.append(item)
+                item.start()
 
     def finish():
         for item in local:
@@ -187,7 +189,11 @@
         for item in copies:
             item.wait_send()
 
-    return finish
+    return start, finish
+
+
+def all_slots(count):
+    return list(range(1, count)) + [0]
 
 
 def span(start, width):
@@ -247,40 +253,78 @@
     return [(flip(me, slot), group) for slot in range(1, count)]
 
 
-def spread_kernel(count, qkv, mlp, qkv_parts, mlp_parts, send, recv, mlp_send, mlp_recv):
+def spread_qkv_kernel(count, qkv, out, parts, send, recv, local):
+    me = lax.axis_index("ctx")
+    group = lax.axis_index("fsdp")
+    width = parts.shape[2]
+    greet(everyone(count, me, group))
+    start, finish = trade(count, me, group, outgoing(qkv_spans, count), qkv, parts, send, recv)
+    start(all_slots(count))
+    items = [
+        pltpu.make_async_copy(
+            out.at[:, pl.ds(index * width, width)], parts.at[count + index], local.at[index]
+        )
+        for index in range(parts.shape[0] - count)
+    ]
+    for item in items:
+        item.start()
+    finish()
+    for item in items:
+        item.wait()
+
+
+def spread_qkv(count, collective, qkv, out):
+    rows = qkv.shape[0]
+    width = qkv_width(count)
+    extra = out.shape[1] // width if merges(count, out.shape[1]) else 0
+    return pl.pallas_call(
+        functools.partial(spread_qkv_kernel, count),
+        out_shape=jax.ShapeDtypeStruct((count + extra, rows, width), BF16),
+        in_specs=[ANY, VMEM],
+        out_specs=ANY,
+        scratch_shapes=[DMA((3 * count,)), DMA((3 * count,)), DMA((max(1, extra),))],
+        compiler_params=pltpu.CompilerParams(collective_id=collective, has_side_effects=True),
+        cost_estimate=cost(12),
+    )(qkv, out)
+
+
+def qkv_width(count):
+    return QUERY_HEADS // count * HEAD + 2 * HEAD
+
+
+def merges(count, width):
+    return width % qkv_width(count) == 0
+
+
+def spread_mlp_kernel(count, weight, parts, send, recv):
     me = lax.axis_index("ctx")
     group = lax.axis_index("fsdp")
     greet(everyone(count, me, group))
-    finish = trade(count, me, group, outgoing(qkv_spans, count), qkv, qkv_parts, send, recv)
-    finish_mlp = trade(count, me, group, outgoing(mlp_spans, count), mlp, mlp_parts, mlp_send, mlp_recv)
+    start, finish = trade(count, me, group, outgoing(mlp_spans, count), weight, parts, send, recv)
+    start(all_slots(count))
     finish()
-    finish_mlp()
-
-
-def spread(count, collective, qkv, mlp):
-    rows = qkv.shape[0]
-    width = QUERY_HEADS // count * HEAD + 2 * HEAD
+
+
+def spread_mlp(count, collective, weight):
     return pl.pallas_call(
-        functools.partial(spread_kernel, count),
-        out_shape=[
-            jax.ShapeDtypeStruct((count, rows, width), BF16),
-            jax.ShapeDtypeStruct((count, rows, 2 * FF // count), BF16),
-        ],
-        in_specs=[ANY, ANY],
-        out_specs=[ANY, ANY],
-        scratch_shapes=[DMA((3 * count,)), DMA((3 * count,)), DMA((2 * count,)), DMA((2 * count,))],
+        functools.partial(spread_mlp_kernel, count),
+        out_shape=jax.ShapeDtypeStruct((count, weight.shape[0], 2 * FF // count), BF16),
+        in_specs=[ANY],
+        out_specs=ANY,
+        scratch_shapes=[DMA((2 * count,)), DMA((2 * count,))],
         compiler_params=pltpu.CompilerParams(collective_id=collective, has_side_effects=True),
-        cost_estimate=cost(28),
-    )(qkv, mlp)
+        cost_estimate=cost(22),
+    )(weight)
 
 
 def opening_kernel(count, normed, runs, rows, all_runs, send, recv, own, run_send, run_recv):
     me = lax.axis_index("ctx")
     group = lax.axis_index("fsdp")
     greet(everyone(count, me, group))
-    finish_runs = trade(
+    start, finish_runs = trade(
         count, me, group, lambda device, owner: [((0,), (owner,))], runs, all_runs, run_send, run_recv
     )
+    start(all_slots(count))
     start, finish = gather_rows(count, me, group, 2, normed, rows, send, recv, own)
     start(0)
     start(1)
@@ -308,12 +352,8 @@
     return lax.ppermute(values, "ctx", [(index, index ^ bit) for index in range(count)])
 
 
-def join_kernel(count, slots, *refs):
-    blocks, (target, send, recv) = refs[:-3], refs[-3:]
-    me = lax.axis_index("ctx")
-    group = lax.axis_index("fsdp")
+def join_rows(count, me, group, slots, blocks, target, send, recv, local):
     other = flip(me, 1)
-    greet([(other, group)])
     half = blocks[0].shape[1]
     items = []
     for block, (part, masks) in zip(blocks, slots):
@@ -334,15 +374,22 @@
             device_id_type=MESH,
         )
 
-    for number in range(len(items)):
-        copy(number, me).start()
-    for number in range(len(items)):
+    def keep(number):
         block, index = items[number][:2]
-        target[place(number, me), :] = block[index]
-    for number in range(len(items)):
-        copy(number, other).wait_recv()
-    for number in range(len(items)):
-        copy(number, me).wait_send()
+        return pltpu.make_async_copy(block.at[index], target.at[place(number, me)], local.at[number])
+
+    def start():
+        for number in range(len(items)):
+            copy(number, me).start()
+            keep(number).start()
+
+    def finish():
+        for number in range(len(items)):
+            keep(number).wait()
+            copy(number, other).wait_recv()
+            copy(number, me).wait_send()
+
+    return start, finish
 
 
 def gather_step(count, masks, blocks, step):
@@ -353,36 +400,23 @@
     return arrived, filled
 
 
-def gather_join(count, collective, masks, blocks, filled, arrived):
-    slots = []
-    for part in (0, 1):
-        slots += [(part, masks[part]), (part, filled[part])]
-    held = [block for pair in zip(blocks, arrived) for block in pair]
-    half, width = held[0].shape[1:]
-    return pl.pallas_call(
-        functools.partial(join_kernel, count, slots),
-        out_shape=jax.ShapeDtypeStruct((count * 2 * half, width), BF16),
-        in_specs=[VMEM] * len(held),
-        out_specs=VMEM,
-        scratch_shapes=[DMA((count,)), DMA((count,))],
-        compiler_params=pltpu.CompilerParams(
-            collective_id=collective, has_side_effects=True, vmem_limit_bytes=VMEM_LIMIT
-        ),
-        cost_estimate=cost(13),
-    )(*held)
-
-
 def last_kernel(
     count,
     groups,
-    values,
+    attn_part,
+    mlp_part,
+    q_part,
+    k_part,
     parts,
     attn_gain,
     mlp_gain,
     q_gain,
     k_gain,
     d_qkv,
+    d_out,
     columns,
+    out_parts,
+    values,
     near,
     far,
     send,
@@ -391,11 +425,20 @@
     far_recv,
     part_send,
     part_recv,
+    out_in,
 ):
     me = lax.axis_index("ctx")
     group = lax.axis_index("fsdp")
     others = [lax.rem(group + step, groups) for step in range(1, groups)]
     greet(everyone(count, me, group) + [(me, other) for other in others])
+    fetched = fetch([parts.at[pl.ds(count, out_parts.shape[0])]], [out_parts], out_in)
+    rows = attn_gain.shape[0]
+    for row in range(rows):
+        values[row : row + 1] = attn_part[:, row * 128 : (row + 1) * 128]
+        values[rows + row : rows + row + 1] = mlp_part[:, row * 128 : (row + 1) * 128]
+    values[2 * rows : 2 * rows + 1] = q_part[...]
+    values[2 * rows + 1 : 2 * rows + 2] = k_part[...]
+    values[2 * rows + 2 :] = jnp.zeros((6, 128), F32)
     copies = []
     for slot in range(1, count):
         item = pltpu.make_async_remote_copy(
@@ -408,7 +451,10 @@
         )
         item.start()
         copies.append(item)
-    finish = trade(count, me, group, incoming(qkv_spans, count), parts, columns, part_send, part_recv)
+    start, finish = trade(
+        count, me, group, incoming(qkv_spans, count), parts, columns, part_send, part_recv
+    )
+    start(all_slots(count))
     near[me] = values[...]
     for item in copies:
         item.wait()
@@ -433,29 +479,38 @@
     summed = far[0]
     for index in range(1, groups):
         summed = summed + far[index]
-    rows = attn_gain.shape[0]
     attn_gain[...] = summed[:rows]
     mlp_gain[...] = summed[rows : 2 * rows]
     q_gain[...] = summed[2 * rows : 2 * rows + 1]
     k_gain[...] = summed[2 * rows + 1 : 2 * rows + 2]
+    fetched()
+    width = out_parts.shape[2]
+    for index in range(out_parts.shape[0]):
+        d_out[:, index * width : (index + 1) * width] = out_parts[index].astype(F32)
     finish()
     d_qkv[...] = columns[...].astype(F32)
 
 
-def last(count, groups, collective, values, parts, width, columns):
-    shape = values.shape
-    long, short = (width // 128, 128), (1, 128)
+def last(count, groups, collective, gains, parts, columns):
+    width = gains[0].shape[1]
+    rows = width // 128
+    shape = (2 * rows + 8, 128)
+    long, short = (rows, 128), (1, 128)
     pieces = len(qkv_spans(count, 0, True))
+    out_shape = (parts.shape[0] - count,) + parts.shape[1:]
     return pl.pallas_call(
         functools.partial(last_kernel, count, groups),
-        out_shape=[
-            jax.ShapeDtypeStruct(size, F32)
-            for size in (long, long, short, short, (parts.shape[1], columns))
+        out_shape=[jax.ShapeDtypeStruct(size, F32) for size in (long, long, short, short)]
+        + [
+            jax.ShapeDtypeStruct((parts.shape[1], columns), F32),
+            jax.ShapeDtypeStruct((parts.shape[1], out_shape[0] * out_shape[2]), F32),
         ],
-        in_specs=[VMEM, ANY],
-        out_specs=[VMEM] * 5,
+        in_specs=[VMEM] * 4 + [ANY],
+        out_specs=[VMEM] * 6,
         scratch_shapes=[
             pltpu.VMEM((parts.shape[1], columns), BF16),
+            pltpu.VMEM(out_shape, BF16),
+            pltpu.VMEM(shape, F32),
             pltpu.VMEM((count,) + shape, F32),
             pltpu.VMEM((groups,) + shape, F32),
             DMA((count,)),
@@ -464,10 +519,11 @@
             DMA((groups,)),
             DMA((pieces * count,)),
             DMA((pieces * count,)),
+            DMA((1,)),
         ],
         compiler_params=pltpu.CompilerParams(collective_id=collective, has_side_effects=True),
         cost_estimate=cost(14),
-    )(values, parts)
+    )(*gains, parts)
 
 
 def product_slots(count):
@@ -730,12 +786,18 @@
     return values * lax.rsqrt(jnp.mean(values * values, axis=-1, keepdims=True) + EPS) * gain
 
 
-def middle_kernel(count, left, right, hidden, gain, middle, gathered, own_rows, sums, *scratch):
+def middle_kernel(count, slots, left, right, hidden, gain, *refs):
+    held, refs = refs[: len(slots)], refs[len(slots) :]
+    (middle, gathered, joined, own_rows, sums), refs = refs[:5], refs[5:]
+    blocks, refs = refs[: len(slots)], refs[len(slots) :]
+    (held_in, send, recv, local), scratch = refs[:4], refs[4:]
     me = lax.axis_index("ctx")
     group = lax.axis_index("fsdp")
     piece = middle.shape[0] // PARTS
+    fetched = fetch(held, blocks, held_in)
     greet([(flip(me, bit), group) for bit in bits_of(count)])
     start, finish = gather_rows(count, me, group, PARTS, own_rows, gathered, *scratch[SCATTER:])
+    start_join, finish_join = join_rows(count, me, group, slots, blocks, joined, send, recv, local)
 
     def done(part, value):
         sums[...] = value
@@ -748,16 +810,19 @@
         row_blocks(part * piece, piece, step)
         start(part)
 
-    begin, send, pass_on, end, close = product_scatter(
+    begin, send_batch, pass_on, end, close = product_scatter(
         count, me, group, PARTS, False, left, right, done, *scratch[:SCATTER]
     )
     begin()
+    fetched()
+    start_join()
     pass_on(0)
-    send(1)
+    send_batch(1)
     end(0)
     pass_on(1)
     end(1)
     finish()
+    finish_join()
     close()
 
 
@@ -765,22 +830,29 @@
     return [DMA((parts * count,)), DMA((parts * count,)), DMA((parts,))]
 
 
-def middle_and_second(count, collective, left, right, hidden, gain):
+def middle_and_second(count, collective, left, right, hidden, gain, masks, blocks, filled, arrived):
     rows, width = hidden.shape
+    slots, held = [], []
+    for part in (0, 1):
+        slots += [(part, masks[part]), (part, filled[part])]
+        held += [blocks[part], arrived[part]]
     return pl.pallas_call(
-        functools.partial(middle_kernel, count),
+        functools.partial(middle_kernel, count, slots),
         out_shape=[
             jax.ShapeDtypeStruct((rows, width), F32),
             jax.ShapeDtypeStruct((count * rows, width), BF16),
+            jax.ShapeDtypeStruct((count * rows, width), BF16),
         ],
-        in_specs=[VMEM] * 4,
-        out_specs=[VMEM, ANY],
+        in_specs=[VMEM] * 4 + [ANY] * len(held),
+        out_specs=[VMEM, ANY, ANY],
         scratch_shapes=[pltpu.VMEM((rows, width), BF16), pltpu.VMEM((rows // PARTS, width), F32)]
+        + [pltpu.VMEM(block.shape, BF16) for block in held]
+        + [DMA((len(held),)), DMA((count,)), DMA((count,)), DMA((count,))]
         + scatter_scratch(count, rows, width, PARTS)
         + gather_scratch(count, PARTS),
         compiler_params=comm_params(collective),
         cost_estimate=cost(80),
-    )(left, right, hidden, gain)
+    )(left, right, hidden, gain, *held)
 
 
 def back_kernel(
@@ -904,13 +976,15 @@
 
 
 def input_kernel(
-    count, left, right, hidden, d_middle, gain, parts, d_hidden, d_gain, d_gate_up, columns, sums, send, recv, *scratch
+    count, left, right, hidden, d_middle, gain, parts, d_hidden, d_gain, columns, sums, send, recv, *scratch
 ):
     me = lax.axis_index("ctx")
     group = lax.axis_index("fsdp")
     half = hidden.shape[0] // 2
     greet(everyone(count, me, group))
-    finish = trade(count, me, group, incoming(mlp_spans, count), parts, columns, send, recv)
+    start, finish = trade(count, me, group, incoming(mlp_spans, count), parts, columns, send, recv)
+    early = [0, 1, 2, 4]
+    start(early)
     d_gain[...] = jnp.zeros_like(d_gain)
 
     def done(part, value):
@@ -930,10 +1004,10 @@
     )
     begin()
     pass_on(0)
+    start([slot for slot in range(count) if slot not in early])
     end(0)
     finish()
     close()
-    d_gate_up[...] = columns[...].astype(F32)
 
 
 def back_to_input(count, collective, left, right, hidden, d_middle, gain, parts):
@@ -944,12 +1018,11 @@
         out_shape=[
             shape((rows, width), F32),
             shape((1, width), F32),
-            shape((parts.shape[1], 2 * FF), F32),
+            shape((parts.shape[1], 2 * FF), BF16),
         ],
         in_specs=[VMEM] * 5 + [ANY],
-        out_specs=[VMEM] * 3,
+        out_specs=[VMEM, VMEM, ANY],
         scratch_shapes=[
-            pltpu.VMEM((parts.shape[1], 2 * FF), BF16),
             pltpu.VMEM((rows // 2, width), F32),
             DMA((2 * count,)),
             DMA((2 * count,)),
@@ -1572,14 +1645,20 @@
     def scatter_groups(values):
         return lax.psum_scatter(values, "fsdp", scatter_dimension=0, tiled=True)
 
-    w_out = gather_groups(out_weight, 0)
-    qkv_parts, mlp_parts = spread(count, 1, qkv_weight, gate_up)
-    qkv_parts, w_out = lax.optimization_barrier((qkv_parts, w_out))
-    w_qkv = gather_groups(qkv_parts, 1).reshape(width, -1)
+    qkv_parts = spread_qkv(count, 1, qkv_weight, out_weight)
+    gate_up, qkv_parts = lax.optimization_barrier((gate_up, qkv_parts))
+    w_qkv = gather_groups(qkv_parts, 1)
+    if merges(count, width):
+        w_out = w_qkv[count:].transpose(1, 0, 2).reshape(-1, width)
+        w_qkv = w_qkv[:count]
+    else:
+        w_out = gather_groups(out_weight, 0)
+    w_qkv = w_qkv.reshape(width, -1)
+    mlp_parts = spread_mlp(count, 5, gate_up)
     normed_local = norm_rows(hidden, attn_gain).astype(BF16)
-    normed_local, qkv_parts = lax.optimization_barrier((normed_local, qkv_parts))
+    normed_local, mlp_parts = lax.optimization_barrier((normed_local, mlp_parts))
     normed, all_runs = opening(count, 2, normed_local, runs)
-    mlp_parts, w_qkv, normed, upstream = lax.optimization_barrier((mlp_parts, w_qkv, normed, cotangent[0]))
+    w_qkv, normed, upstream = lax.optimization_barrier((w_qkv, normed, cotangent[0]))
     w_gu = gather_groups(mlp_parts, 1).reshape(width, -1)
     w_down = gather_groups(down_weight, 0)
     run_order = all_runs[:, 0, : rows // RUN].reshape(-1)
@@ -1601,14 +1680,14 @@
         heads, run_order, joined, cosine, sine, q_gain_row, k_gain_row
     )
     attended, arrived = lax.optimization_barrier((attended, arrived))
-    middle, second = middle_and_second(count, 3, attended, w_out, hidden_in[0], mlp_gain[None, :])
+    middle, second, upstream = middle_and_second(
+        count, 3, attended, w_out, hidden_in[0], mlp_gain[None, :], masks, blocks, filled, arrived
+    )
     both = jnp.dot(second, w_gu, preferred_element_type=F32)
     own = both.shape[1] // 2
     gate, up = both[:, :own], both[:, own:]
     activated = (gate * jax.nn.sigmoid(gate) * up).astype(BF16)
 
-    activated, arrived = lax.optimization_barrier((activated, arrived))
-    upstream = gather_join(count, 5, masks, blocks, filled, arrived)
     d_down = jnp.dot(activated.T, upstream, preferred_element_type=F32).astype(BF16)
     d_down, upstream = lax.optimization_barrier((d_down, upstream))
     d_down = scatter_groups(d_down)
@@ -1649,7 +1728,6 @@
         )
         parts, gu_parts, d_joined = lax.optimization_barrier((parts, gu_parts, d_joined))
         qkv_grad_parts = scatter_groups(parts.reshape((-1,) + parts.shape[2:]))
-        d_out = qkv_grad_parts[count:].transpose(1, 0, 2).reshape(-1, width)
     else:
         d_queries, d_keys, d_values = attention_back(
             heads, run_order, d_attended, queries, keys, values, mixed, lse
@@ -1668,21 +1746,23 @@
     )
     d_hidden, qkv_grad_parts = lax.optimization_barrier((d_hidden, qkv_grad_parts))
 
-    small = jnp.concatenate([attn_gain_grad[0], mlp_gain_grad[0], q_gain_grad[0], k_gain_grad[0]])
-    padded = -(-small.shape[0] // 1024) * 1024
-    small = jnp.pad(small, (0, padded - small.shape[0])).reshape(-1, 128)
-    gains = last(count, groups, 11, small, qkv_grad_parts, width, qkv_weight.shape[1])
-    attn_gain_sum, mlp_gain_sum, q_gain_sum, k_gain_sum, d_qkv = gains
+    gains = (attn_gain_grad, mlp_gain_grad, q_gain_grad, k_gain_grad)
+    if repeat > 1:
+        extra = jnp.zeros((1,) + qkv_grad_parts.shape[1:], BF16)
+        qkv_grad_parts = jnp.concatenate([qkv_grad_parts, extra])
+    *gains, d_qkv, out_rows = last(count, groups, 11, gains, qkv_grad_parts, qkv_weight.shape[1])
+    if repeat == 1:
+        d_out = out_rows
     return (
         output[None],
         d_hidden[None],
-        attn_gain_sum.reshape(-1),
+        gains[0].reshape(-1),
         d_qkv,
-        q_gain_sum.reshape(-1),
-        k_gain_sum.reshape(-1),
+        gains[2].reshape(-1),
+        gains[3].reshape(-1),
         d_out.astype(F32),
-        mlp_gain_sum.reshape(-1),
-        d_gate_up,
+        gains[1].reshape(-1),
+        d_gate_up.astype(F32),
         d_down.astype(F32),
     )
 

time: 544 us -> 536 us (0.985)
  Pallas kernels: 441 us -> 430 us
    pallas_call x3, Pallas kernels: 126 us -> 117 us  [the longest x1 83.4 us: middle_and_second(): pl.pallas_call(functools.partial(middle_kernel, count, slots), out_shape=...]
    unnamed x46 -> x51, local copies, waits for them, and re-layouts: 11.7 us -> 15.7 us
    all_gather x4 -> x3, waiting for transfers between devices: 8.62 us -> 12.4 us  [gather_groups(): return lax.all_gather(values, 'fsdp', axis=axis, tiled=True)]
  transfers between devices with their start and end apart: 11 -> 10, of which waited for: 5 -> 3; matrix products, arithmetic and copies ran while one was open for 10% -> 10% of each run, Pallas kernels for 79% -> 76%
where the time goes in v5:
time: 536 us; the launch traced here: 532 us
  Pallas kernels  430 us (80%)
  matrix products  36.5 us (7%)
  local copies, waits for them, and re-layouts  21.4 us (4%)
  waiting for transfers between devices  14.8 us (3%)
  between operations  14.7 us (3%)
  other arithmetic  8.6 us (2%)
  starting transfers between devices  5.69 us (1%)
    pallas_call x1, Pallas kernels, back_through_middle(): pl.pallas_call(functools.partial(back_kernel, count), out_shape=[shape((r...  92.3 us
    pallas_call x1, Pallas kernels, middle_and_second(): pl.pallas_call(functools.partial(middle_kernel, count, slots), out_shape=...  83.4 us
    pallas_call x1, Pallas kernels, back_to_input(): pl.pallas_call(functools.partial(input_kernel, count), out_shape=[shape((...  60.2 us
    pallas_call x1, Pallas kernels, back_through_mlp(): pl.pallas_call(functools.partial(mlp_kernel, count, groups), out_shape=[s...  49.6 us
    pallas_call x1, Pallas kernels, opening(): pl.pallas_call(functools.partial(opening_kernel, count), out_shape=[jax.S...  43.4 us
    pallas_call x1, Pallas kernels, attention_and_joined_back(): pl.pallas_call(functools.partial(attention_and_joined_back_kernel, heads,...  33.7 us
    pallas_call x1, Pallas kernels, spread_mlp(): pl.pallas_call(functools.partial(spread_mlp_kernel, count), out_shape=jax...  21 us
    pallas_call x1, Pallas kernels, attention(): pl.pallas_call(functools.partial(attention_kernel, heads), out_shape=[sha...  20.5 us
  transfers between devices with their start and end apart: 10, of which 3 were waited for; matrix products, arithmetic and copies ran while one was open for 10% of the time, Pallas kernels for 76%

profile of v5, /device:TPU:0, one launch (start us, length us, event | category | flops | bytes accessed | tf_op | source)
XLA Modules:
  0.0 531.6 jit_solution(2533813239040911142)
XLA Ops:
  7.2 12.5 %shard_map.213 = bf16[12,64,512]{2,1,0:T(8,128)(2,1)} custom-call(bf16[64,4096]{1,0:T(8,128)(2,1)} %qkv.1, bf16[64,2048]{1,0:T(8,128)(2,1)} %out.1), custom_call_target="tpu_custom_call" | custom-call | bytes 12000000 | tf_op jit(solution)/shard_map/pallas_call | solution.py:280
  19.8 21.0 %shard_map.214 = bf16[8,64,1536]{2,1,0:T(8,128)(2,1)} custom-call(bf16[64,12288]{1,0:T(8,128)(2,1)} %weight), custom_call_target="tpu_custom_call" | custom-call | bytes 22000000 | tf_op jit(solution)/shard_map/pallas_call | solution.py:309
  43.3 43.4 %shard_map.215 = (bf16[2048,2048]{1,0:T(8,128)(2,1)}, s32[8,8,128]{2,1,0:T(8,128)}) custom-call(bf16[256,2048]{1,0:T(8,128)(2,1)} %fusion.3.normed, s32[1,8,128]{2,1,0:T(8,128)} %scatter.4.runs), custom_call_target="tpu_custom_call" | custom-call | bytes 45000000 | tf_op jit(solution)/shard_map/pallas_call | solution.py:337
  86.8 1.8 slice.57
  88.7 1.6 collective-permute-start
  90.3 1.5 collective-permute-start.1
  91.8 10.3 %fusion.4.joined = f32[2048,512]{1,0:T(8,128)} fusion(bf16[2048,2048]{1,0:T(8,128)(2,1)} %get-tuple-element.83.normed, bf16[2048,512]{1,0:T(8,128)(2,1)S(1)} %bitcast.48), kind=kOutput, calls=%fused_computation.20 | convolution fusion | flops 4294967296 | bytes 14680064 | tf_op jit(solution)/shard_map/dot_general | solution.py:1674
  105.1 1.5 collective-permute-start.2
  110.8 20.5 %shard_map.216 = (bf16[2048,256]{1,0:T(8,128)(2,1)}, f32[2048,512]{1,0:T(8,128)}, bf16[16,256,128]{2,1,0:T(8,128)(2,1)}, bf16[2048,128]{1,0:T(8,128)(2,1)}, bf16...) custom-call(s32[64]{0:T(128)} %reshape_squeeze.3.runs, f32[2048,512]{1,0:T(8,128)} %fusion.4.joined, ...), custom_call_target="tpu_custom_call" | custom-call | bytes 15000000 | tf_op jit(solution)/shard_map/pallas_call | solution.py:1292
  132.3 83.4 %shard_map.217 = (f32[256,2048]{1,0:T(8,128)}, bf16[2048,2048]{1,0:T(8,128)(2,1)}, bf16[2048,2048]{1,0:T(8,128)(2,1)}) custom-call(bf16[2048,256]{1,0:T(8,128)(2,1)} %get-tuple-element.90.left.attended_from, bf16[256,2048]{1,0:T(8,128)(2,1)} %bitcast.46, bf16[256,2048]{1,0:T(8,128)(2,1)} %bitcast.44, f32[1,2048]{1,0:T(1,128)} %bitcast.59, ...), custom_call_target="tpu_custom_call" | custom-call | bytes 80000000 | tf_op jit(solution)/shard_map/pallas_call | solution.py:839
  215.7 17.4 %fusion.5.both = f32[2048,1536]{1,0:T(8,128)S(1)} fusion(bf16[2048,2048]{1,0:T(8,128)(2,1)} %get-tuple-element.93.second, bf16[2048,1536]{1,0:T(8,128)(2,1)} %bitcast.51), kind=kOutput, calls=%fused_computation.21 | convolution fusion | flops 12884901888 | bytes 27262976 | tf_op jit(solution)/shard_map/dot_general | solution.py:1686
  233.2 2.1 fusion.activated_from
  235.3 4.3 copy-done
  239.5 2.7 copy-done.4
  242.3 8.8 %convolution_convert_fusion = bf16[768,2048]{1,0:T(8,128)(2,1)} fusion(bf16[2048,768]{1,0:T(8,128)(2,1)S(1)} %fusion.activated_from, bf16[2048,2048]{1,0:T(8,128)(2,1)S(1)} %copy-done.4), kind=kOutput, calls=%fused_computation.2 | convolution fusion | flops 6444023808 | bytes 14680064 | tf_op jit(solution)/shard_map/dot_general | solution.py:1691
  251.1 12.4 %all-gather.8.cloned.1.call-done.weight_from = bf16[768,2048]{1,0:T(8,128)(2,1)} async-done(((bf16[192,2048]{1,0:T(8,128)(2,1)}), bf16[768,2048]{1,0:T(8,128)(2,1)}) %all-gather.8.cloned.1.call-update) | async-done | bytes 3145744 | tf_op jit(solution)/shard_map/all_gather | solution.py:1643
  263.5 49.6 %shard_map.218 = (bf16[256,2048]{1,0:T(8,128)(2,1)}, bf16[2048,1536]{1,0:T(8,128)(2,1)}, bf16[4,8,64,1536]{3,2,1,0:T(8,128)(2,1)}) custom-call(bf16[2048,768]{1,0:T(8,128)(2,1)} %copy-done.2, bf16[768,2048]{1,0:T(8,128)(2,1)} %all-gather.8.cloned.1.call-done.weight_from, f32[256,2048]{1,0:T(8,128)} %get-tuple-element.95.middle_from, ...), custom_call_target="tpu_custom_call" | custom-call | bytes 48000000 | tf_op jit(solution)/shard_map/pallas_call | solution.py:1174
  313.2 92.3 %shard_map.219 = (f32[256,2048]{1,0:T(8,128)}, f32[1,2048]{1,0:T(1,128)}, bf16[2048,256]{1,0:T(8,128)(2,1)}, bf16[256,2048]{1,0:T(8,128)(2,1)}) custom-call(bf16[2048,1536]{1,0:T(8,128)(2,1)} %get-tuple-element.101.left_from, bf16[2048,1536]{1,0:T(8,128)(2,1)} %bitcast.52, f32[256,2048]{1,0:T(8,128)} %get-tuple-element.95.middle_from, ...), custom_call_target="tpu_custom_call" | custom-call | bytes 85000000 | tf_op jit(solution)/shard_map/pallas_call | solution.py:947
  406.1 33.7 %shard_map.220 = (bf16[2048,512]{1,0:T(8,128)(2,1)}, f32[1,128]{1,0:T(1,128)}, f32[1,128]{1,0:T(1,128)}, bf16[4,12,64,512]{3,2,1,0:T(8,128)(2,1)}) custom-call(s32[64]{0:T(128)} %reshape_squeeze.3.runs, bf16[2048,256]{1,0:T(8,128)(2,1)} %get-tuple-element.104.d_attended, bf16[16,256,128]{2,1,0:T(8,128)(2,1)} %get-tuple-element.105.queries, ...), custom_call_target="tpu_custom_call" | custom-call | bytes 30000000 | tf_op jit(solution)/shard_map/pallas_call | solution.py:1562
  439.9 1.3 convert_element_type.23
  441.2 60.2 %shard_map.221 = (f32[256,2048]{1,0:T(8,128)}, f32[1,2048]{1,0:T(1,128)}, bf16[64,12288]{1,0:T(8,128)(2,1)}) custom-call(bf16[2048,512]{1,0:T(8,128)(2,1)} %get-tuple-element.115.left, bf16[2048,512]{1,0:T(8,128)(2,1)} %bitcast.49, bf16[256,2048]{1,0:T(8,128)(2,1)} %bitcast.45, f32[256,2048]{1,0:T(8,128)} %get-tuple-element.116.d_middle, ...), custom_call_target="tpu_custom_call" | custom-call | bytes 60000000 | tf_op jit(solution)/shard_map/pallas_call | solution.py:1016
  501.5 3.4 convert_element_type.22
  504.9 13.3 %shard_map.222 = (f32[16,128]{1,0:T(8,128)}, f32[16,128]{1,0:T(8,128)}, f32[1,128]{1,0:T(1,128)}, f32[1,128]{1,0:T(1,128)}, f32[64,4096]{1,0:T(8,128)}, /*index=5*/f32[64,2048]{1,0:T(8,128)}) custom-call(f32[1,2048]{1,0:T(1,128)} %get-tuple-element.121.attn_part, f32[1,2048]{1,0:T(1,128)} %get-tuple-element.122.mlp_part, ...), custom_call_target="tpu_custom_call" | custom-call | bytes 14000000 | tf_op jit(solution)/shard_map/pallas_call | solution.py:501
  519.2 1.3 copy.35
  (84 shorter events, 16.5 us)
Async XLA Ops:
  7.2 33.6 %copy-start.1 = (bf16[1,256,2048]{2,1,0:T(8,128)(2,1)S(1)}, bf16[1,256,2048]{2,1,0:T(8,128)(2,1)}, u32[]{:S(2)}) copy-start(bf16[1,256,2048]{2,1,0:T(8,128)(2,1)} %param.16) | copy-start | bytes 3145732
  7.2 33.9 %copy-start.14 = (f32[2048]{0:T(1024)S(1)}, f32[2048]{0:T(1024)}, u32[]{:S(2)}) copy-start(f32[2048]{0:T(1024)} %param.19) | copy-start | bytes 24580
  7.2 79.6 %all-gather.4.cloned.1.call-start = ((), (), s32[]{:S(2)}) async-start(), calls=%async_computation.3 | async-start | bytes 3932160 | tf_op jit(solution)/shard_map/all_gather | solution.py:1643
  19.7 22.8 %copy-start.17 = (s32[1,256]{1,0:T(1,128)S(1)}, s32[1,256]{1,0:T(1,128)}, u32[]{:S(2)}) copy-start(s32[1,256]{1,0:T(1,128)} %param.17) | copy-start | bytes 3076
  19.7 22.9 %copy-start.18 = (s32[1,256]{1,0:T(1,128)S(1)}, s32[1,256]{1,0:T(1,128)}, u32[]{:S(2)}) copy-start(s32[1,256]{1,0:T(1,128)} %param.18) | copy-start | bytes 3076
  19.8 196.0 %all-gather.6.cloned.1.call-start = ((), (), s32[]{:S(2)}) async-start(), calls=%async_computation.4 | async-start | bytes 7864320 | tf_op jit(solution)/shard_map/all_gather | solution.py:1643
  41.1 47.5 %copy-start.5 = (bf16[1,256,2048]{2,1,0:T(8,128)(2,1)S(1)}, bf16[1,256,2048]{2,1,0:T(8,128)(2,1)}, u32[]{:S(2)}) copy-start(bf16[1,256,2048]{2,1,0:T(8,128)(2,1)} %param.27) | copy-start | bytes 3145732
  42.5 221.0 %all-gather.8.cloned.1.call-start = ((), (), s32[]{:S(2)}) async-start(), calls=%async_computation.5 | async-start | bytes 3932160 | tf_op jit(solution)/shard_map/all_gather | solution.py:1643
  88.6 13.5 %copy-start.3 = (bf16[8,256,512]{2,1,0:T(8,128)(2,1)}, bf16[8,256,512]{2,1,0:T(8,128)(2,1)S(1)}, u32[]{:S(2)}) copy-start(bf16[8,256,512]{2,1,0:T(8,128)(2,1)S(1)} %slice.57) | copy-start | bytes 6291460
  88.7 14.3 %collective-permute-start = (bf16[1,128,2048]{2,1,0:T(8,128)(2,1)S(1)}, bf16[1,128,2048]{2,1,0:T(8,128)(2,1)S(1)}, u32[]{:S(2)}, u32[]{:S(2)}) collective-permute-start(bf16[1,128,2048]{2,1,0:T(8,128)(2,1)S(1)} %get-tuple-element.135), channel_id=1, source_target_pairs={{0,8},{4,12},{8,0},{12,4},{16,24},{20,28},{24,16},{28,20},{1,9},{5... | collective-permute-start | bytes 1572872 | tf_op jit(solution)/shard_map/ppermute | solution.py:352
  90.3 14.0 %collective-permute-start.1 = (bf16[1,128,2048]{2,1,0:T(8,128)(2,1)S(1)}, bf16[1,128,2048]{2,1,0:T(8,128)(2,1)S(1)}, u32[]{:S(2)}, u32[]{:S(2)}) collective-permute-start(bf16[1,128,2048]{2,1,0:T(8,128)(2,1)S(1)} %get-tuple-element.134), channel_id=1, source_target_pairs={{0,16},{4,20},{8,24},{12,28},{16,0},{20,4},{24,8},{28,12},{1,17},{... | collective-permute-start | bytes 1572872 | tf_op jit(solution)/shard_map/ppermute | solution.py:352
  104.4 26.9 %copy-start.6 = (bf16[2,128,2048]{2,1,0:T(8,128)(2,1)}, bf16[2,128,2048]{2,1,0:T(8,128)(2,1)S(1)}, u32[]{:S(2)}) copy-start(bf16[2,128,2048]{2,1,0:T(8,128)(2,1)S(1)} %pad_maximum_fusion.1.refs_2_) | copy-start | bytes 3145732
  104.4 26.9 %collective-permute-start.3 = (bf16[2,128,2048]{2,1,0:T(8,128)(2,1)S(1)}, bf16[2,128,2048]{2,1,0:T(8,128)(2,1)S(1)}, u32[]{:S(2)}, u32[]{:S(2)}) collective-permute-start(bf16[2,128,2048]{2,1,0:T(8,128)(2,1)S(1)} %pad_maximum_fusion.1.refs_2_), channel_id=1, source_target_pairs={{0,8},{4,12},{8,0},{12,4},{16,24},{20,28},{24,16},{28,20},{1,9},{5... | collective-permute-start | bytes 3145736 | tf_op jit(solution)/shard_map/ppermute | solution.py:352
  105.1 26.2 %copy-start.7 = (bf16[2,128,2048]{2,1,0:T(8,128)(2,1)}, bf16[2,128,2048]{2,1,0:T(8,128)(2,1)S(1)}, u32[]{:S(2)}) copy-start(bf16[2,128,2048]{2,1,0:T(8,128)(2,1)S(1)} %pad_maximum_fusion.refs_0_) | copy-start | bytes 3145732
  105.1 26.3 %collective-permute-start.2 = (bf16[2,128,2048]{2,1,0:T(8,128)(2,1)S(1)}, bf16[2,128,2048]{2,1,0:T(8,128)(2,1)}, u32[]{:S(2)}, u32[]{:S(2)}) collective-permute-start(bf16[2,128,2048]{2,1,0:T(8,128)(2,1)S(1)} %pad_maximum_fusion.refs_0_), channel_id=1, source_target_pairs={{0,16},{4,20},{8,24},{12,28},{16,0},{20,4},{24,8},{28,12},{1,17},{... | collective-permute-start | bytes 3145736 | tf_op jit(solution)/shard_map/ppermute | solution.py:352
  106.6 298.9 %reduce-scatter.4.cloned.1.call-start = ((), (), s32[]{:S(2)}) async-start(), calls=%async_computation.6 | async-start | bytes 3932160 | tf_op jit(solution)/shard_map/reduce_scatter | solution.py:1646
  233.2 6.4 %copy-start = (f32[2048,1536]{1,0:T(8,128)}, f32[2048,1536]{1,0:T(8,128)S(1)}, u32[]{:S(2)}) copy-start(f32[2048,1536]{1,0:T(8,128)S(1)} %fusion.5.both) | copy-start | bytes 37748740
  233.2 9.1 %copy-start.4 = (bf16[2048,2048]{1,0:T(8,128)(2,1)S(1)}, bf16[2048,2048]{1,0:T(8,128)(2,1)}, u32[]{:S(2)}) copy-start(bf16[2048,2048]{1,0:T(8,128)(2,1)} %get-tuple-element.97.upstream) | copy-start | bytes 25165828
  239.5 11.5 %copy-start.2 = (bf16[2048,768]{1,0:T(8,128)(2,1)}, bf16[2048,768]{1,0:T(8,128)(2,1)S(1)}, u32[]{:S(2)}) copy-start(bf16[2048,768]{1,0:T(8,128)(2,1)S(1)} %fusion.activated_from) | copy-start | bytes 9437188
  251.0 188.8 %reduce-scatter.6.cloned.1.call-start = ((), (), s32[]{:S(2)}) async-start(), calls=%async_computation.7 | async-start | bytes 7864320 | tf_op jit(solution)/shard_map/reduce_scatter | solution.py:1646
  313.2 191.7 %reduce-scatter.8.cloned.1.call-start = ((), (), s32[]{:S(2)}) async-start(), calls=%async_computation.8 | async-start | bytes 3932160 | tf_op jit(solution)/shard_map/reduce_scatter | solution.py:1646
  406.1 33.8 %copy-start.12 = (bf16[192,2048]{1,0:T(8,128)(2,1)S(1)}, bf16[192,2048]{1,0:T(8,128)(2,1)}, u32[]{:S(2)}) copy-start(bf16[192,2048]{1,0:T(8,128)(2,1)} %reduce-scatter.4.cloned.1.call-done) | copy-start | bytes 2359300
  501.4 16.8 %copy-start.9 = (bf16[256,2048]{1,0:T(8,128)(2,1)S(1)}, bf16[256,2048]{1,0:T(8,128)(2,1)}, u32[]{:S(2)}) copy-start(bf16[256,2048]{1,0:T(8,128)(2,1)} %get-tuple-element.98) | copy-start | bytes 3145732
  501.4 17.8 %copy-start.8 = (f32[256,2048]{1,0:T(8,128)S(1)}, f32[256,2048]{1,0:T(8,128)}, u32[]{:S(2)}) copy-start(f32[256,2048]{1,0:T(8,128)} %get-tuple-element.120) | copy-start | bytes 6291460
  (7 other events, 24.3 us)
Sparse Core Ops, SparseCore 0:
  19.9 64.6 all-gather.3
  86.1 114.0 all-gather.5
  201.8 61.6 all-gather.7
  265.6 58.8 reduce-scatter.3
  326.7 110.7 reduce-scatter.5
  440.0 60.4 reduce-scatter.7

commit v6 on v5

--- a/solution.py
+++ b/solution.py
@@ -170,9 +170,11 @@
                     copies.append(item)
                 item.start()
 
-    def finish():
+    def finish(arrived=None):
         for item in local:
             item.wait()
+        if arrived:
+            arrived(me)
         for slot in range(1, count):
             peer = flip(me, slot)
             listed = pieces(me, peer)
@@ -186,6 +188,8 @@
                     device_id=(peer, group),
                     device_id_type=MESH,
                 ).wait_recv()
+            if arrived:
+                arrived(peer)
         for item in copies:
             item.wait_send()
 
@@ -239,14 +243,16 @@
     return pieces
 
 
-def incoming(spans, count):
-    def pieces(device, owner):
-        return [
-            ((device, slice(None), span(part, width)), (slice(None), span(whole, width)))
-            for whole, part, width in spans(count, owner, True)
-        ]
-
-    return pieces
+def incoming(device, owner):
+    return [((device,), (owner,))]
+
+
+def place_columns(count, spans, arrived, target):
+    def place(peer):
+        for whole, part, width in spans(count, peer, True):
+            target[:, span(whole, width)] = arrived[peer, :, span(part, width)].astype(F32)
+
+    return place
 
 
 def everyone(count, me, group):
@@ -451,9 +457,7 @@
         )
         item.start()
         copies.append(item)
-    start, finish = trade(
-        count, me, group, incoming(qkv_spans, count), parts, columns, part_send, part_recv
-    )
+    start, finish = trade(count, me, group, incoming, parts, columns, part_send, part_recv)
     start(all_slots(count))
     near[me] = values[...]
     for item in copies:
@@ -487,8 +491,7 @@
     width = out_parts.shape[2]
     for index in range(out_parts.shape[0]):
         d_out[:, index * width : (index + 1) * width] = out_parts[index].astype(F32)
-    finish()
-    d_qkv[...] = columns[...].astype(F32)
+    finish(place_columns(count, qkv_spans, columns, d_qkv))
 
 
 def last(count, groups, collective, gains, parts, columns):
@@ -496,7 +499,6 @@
     rows = width // 128
     shape = (2 * rows + 8, 128)
     long, short = (rows, 128), (1, 128)
-    pieces = len(qkv_spans(count, 0, True))
     out_shape = (parts.shape[0] - count,) + parts.shape[1:]
     return pl.pallas_call(
         functools.partial(last_kernel, count, groups),
@@ -508,7 +510,7 @@
         in_specs=[VMEM] * 4 + [ANY],
         out_specs=[VMEM] * 6,
         scratch_shapes=[
-            pltpu.VMEM((parts.shape[1], columns), BF16),
+            pltpu.VMEM((count,) + parts.shape[1:], BF16),
             pltpu.VMEM(out_shape, BF16),
             pltpu.VMEM(shape, F32),
             pltpu.VMEM((count,) + shape, F32),
@@ -517,8 +519,8 @@
             DMA((count,)),
             DMA((groups,)),
             DMA((groups,)),
-            DMA((pieces * count,)),
-            DMA((pieces * count,)),
+            DMA((count,)),
+            DMA((count,)),
             DMA((1,)),
         ],
         compiler_params=pltpu.CompilerParams(collective_id=collective, has_side_effects=True),
@@ -976,13 +978,36 @@
 
 
 def input_kernel(
-    count, left, right, hidden, d_middle, gain, parts, d_hidden, d_gain, columns, sums, send, recv, *scratch
+    count,
+    left_from,
+    right_from,
+    hidden_from,
+    d_middle_from,
+    gain,
+    parts,
+    d_hidden,
+    d_gain,
+    d_gate_up,
+    columns,
+    left,
+    right,
+    left_in,
+    right_in,
+    hidden,
+    d_middle,
+    others_in,
+    sums,
+    send,
+    recv,
+    *scratch,
 ):
     me = lax.axis_index("ctx")
     group = lax.axis_index("fsdp")
     half = hidden.shape[0] // 2
+    ready = load_operands(count, me, True, left_from, right_from, left, right, left_in, right_in)
+    fetched = fetch((hidden_from, d_middle_from), (hidden, d_middle), others_in)
     greet(everyone(count, me, group))
-    start, finish = trade(count, me, group, incoming(mlp_spans, count), parts, columns, send, recv)
+    start, finish = trade(count, me, group, incoming, parts, columns, send, recv)
     early = [0, 1, 2, 4]
     start(early)
     d_gain[...] = jnp.zeros_like(d_gain)
@@ -1000,13 +1025,14 @@
         row_blocks(part * half, half, step)
 
     begin, _, pass_on, end, close = product_scatter(
-        count, me, group, 2, True, left, right, done, *scratch
+        count, me, group, 2, True, left, right, done, *scratch, ready=ready
     )
     begin()
+    fetched()
     pass_on(0)
     start([slot for slot in range(count) if slot not in early])
     end(0)
-    finish()
+    finish(place_columns(count, mlp_spans, columns, d_gate_up))
     close()
 
 
@@ -1018,14 +1044,19 @@
         out_shape=[
             shape((rows, width), F32),
             shape((1, width), F32),
-            shape((parts.shape[1], 2 * FF), BF16),
+            shape((parts.shape[1], 2 * FF), F32),
         ],
-        in_specs=[VMEM] * 5 + [ANY],
-        out_specs=[VMEM, VMEM, ANY],
-        scratch_shapes=[
+        in_specs=[ANY] * 4 + [VMEM, ANY],
+        out_specs=[VMEM] * 3,
+        scratch_shapes=[pltpu.VMEM(parts.shape, BF16)]
+        + operand_scratch(count, left, right, True)
+        + [
+            pltpu.VMEM((rows, width), BF16),
+            pltpu.VMEM((rows, width), F32),
+            DMA((2,)),
             pltpu.VMEM((rows // 2, width), F32),
-            DMA((2 * count,)),
-            DMA((2 * count,)),
+            DMA((count,)),
+            DMA((count,)),
         ]
         + scatter_scratch(count, rows, width),
         compiler_params=comm_params(collective),
@@ -1309,7 +1340,20 @@
 
 
 def attention_back_kernel(
-    heads, runs, d_attended, queries, keys, values, mixed, lse, d_queries, d_keys, d_values, arrived, keys_turned
+    heads,
+    runs,
+    d_attended,
+    queries,
+    keys,
+    values,
+    mixed,
+    lse,
+    d_queries,
+    d_keys,
+    d_values,
+    arrived,
+    keys_turned,
+    ready=None,
 ):
     tokens = keys.shape[0]
     blocks = tokens // CONT
@@ -1331,6 +1375,9 @@
         return carry
 
     lax.fori_loop(0, blocks, turn, 0)
+
+    if ready:
+        ready()
 
     def back(block, own, before):
         query = queries[block]
@@ -1414,7 +1461,7 @@
             )
             placed[span_rows, columns] = grad.astype(BF16)
             d_q_gain[...] += gain_grad
-        key_part, value_part = share[:1, :], share[1:, :]
+        key_part, value_part = (1.0, 1.0) if share is None else (share[:1, :], share[1:, :])
         grad, gain_grad = pull(
             raw[span_rows, wide : wide + HEAD],
             (d_keys[span_rows, :] * SCALE).astype(BF16).astype(F32),
@@ -1445,20 +1492,19 @@
     queries,
     keys,
     values,
-    mixed,
+    mixed_from,
     lse,
     raw,
     cosine,
     sine,
     q_gain,
     k_gain,
-    share,
     normed,
-    d_out,
-    d_joined,
+    d_out_from,
+    d_joined_to,
     d_q_gain,
     d_k_gain,
-    parts,
+    parts_to,
     d_queries,
     d_keys,
     d_values,
@@ -1469,8 +1515,14 @@
     sine_here,
     placed,
     normed_slots,
+    mixed,
+    d_out,
+    d_joined,
+    parts,
     loaded,
     normed_in,
+    joined_out,
+    parts_out,
 ):
     columns = normed_slots.shape[2]
 
@@ -1482,16 +1534,36 @@
     loads = [
         pltpu.make_async_copy(source, target, loaded.at[index])
         for index, (source, target) in enumerate(
-            [(raw, raw_here), (cosine, cosine_here), (sine, sine_here)]
+            [
+                (raw, raw_here),
+                (cosine, cosine_here),
+                (sine, sine_here),
+                (mixed_from, mixed),
+                (d_out_from, d_out),
+            ]
         )
     ]
-    for item in loads:
+    ready = loads[3].wait
+    for item in [loads[3]] + loads[:3] + loads[4:]:
         item.start()
     normed_copy(0).start()
     attention_back_kernel(
-        heads, runs, d_attended, queries, keys, values, mixed, lse, d_queries, d_keys, d_values, arrived, keys_turned
+        heads,
+        runs,
+        d_attended,
+        queries,
+        keys,
+        values,
+        mixed,
+        lse,
+        d_queries,
+        d_keys,
+        d_values,
+        arrived,
+        keys_turned,
+        ready,
     )
-    for item in loads:
+    for item in loads[:3] + loads[4:]:
         item.wait()
     joined_back_kernel(
         heads,
@@ -1504,7 +1576,7 @@
         sine_here,
         q_gain,
         k_gain,
-        share,
+        None,
         d_joined,
         d_q_gain,
         d_k_gain,
@@ -1512,6 +1584,25 @@
     )
     rows = columns // groups
     width = d_joined.shape[1]
+    joined_copy = pltpu.make_async_copy(d_joined, d_joined_to, joined_out.at[0])
+    joined_copy.start()
+
+    def part_copies(index):
+        return [
+            pltpu.make_async_copy(
+                parts.at[owner, index], parts_to.at[owner, index], parts_out.at[owner, index]
+            )
+            for owner in range(groups)
+        ]
+
+    extras = range(d_out.shape[1] // width)
+    for extra in extras:
+        for owner in range(groups):
+            parts[owner, count + extra] = d_out[
+                owner * rows : (owner + 1) * rows, extra * width : (extra + 1) * width
+            ]
+        for item in part_copies(count + extra):
+            item.start()
 
     def weight_grad(index, carry):
         @pl.when(index + 1 < count)
@@ -1524,14 +1615,15 @@
         ).astype(BF16)
         for owner in range(groups):
             parts[owner, index] = value[owner * rows : (owner + 1) * rows]
+        for item in part_copies(index):
+            item.start()
         return carry
 
     lax.fori_loop(0, count, weight_grad, 0)
-    for owner in range(groups):
-        for extra in range(d_out.shape[1] // width):
-            parts[owner, count + extra] = d_out[
-                owner * rows : (owner + 1) * rows, extra * width : (extra + 1) * width
-            ]
+    for index in range(count + len(extras)):
+        for item in part_copies(index):
+            item.wait()
+    joined_copy.wait()
 
 
 def attention_and_joined_back(
@@ -1550,7 +1642,6 @@
     sine,
     q_gain,
     k_gain,
-    share,
     normed,
     d_out,
 ):
@@ -1567,8 +1658,8 @@
             shape((1, HEAD), F32),
             shape((groups, blocks, columns // groups, raw.shape[1]), BF16),
         ],
-        in_specs=[SMEM] + [VMEM] * 6 + [ANY] * 3 + [VMEM] * 3 + [ANY, VMEM],
-        out_specs=[VMEM] * 4,
+        in_specs=[SMEM] + [VMEM] * 4 + [ANY, VMEM] + [ANY] * 3 + [VMEM] * 2 + [ANY] * 2,
+        out_specs=[ANY, VMEM, VMEM, ANY],
         scratch_shapes=[
             pltpu.VMEM((tokens, wide), BF16),
             pltpu.VMEM((tokens, HEAD), F32),
@@ -1580,12 +1671,18 @@
             pltpu.VMEM(sine.shape, F32),
             pltpu.VMEM(raw.shape, BF16),
             pltpu.VMEM((2, tokens, columns), BF16),
-            DMA((3,)),
+            pltpu.VMEM(mixed.shape, F32),
+            pltpu.VMEM(d_out.shape, BF16),
+            pltpu.VMEM(raw.shape, BF16),
+            pltpu.VMEM((groups, blocks, columns // groups, raw.shape[1]), BF16),
+            DMA((5,)),
             DMA((2,)),
+            DMA((1,)),
+            DMA((groups, blocks)),
         ],
         compiler_params=pltpu.CompilerParams(vmem_limit_bytes=VMEM_LIMIT),
         cost_estimate=cost(30),
-    )(runs, d_attended, queries, keys, values, mixed, lse, raw, cosine, sine, q_gain, k_gain, share, normed, d_out)
+    )(runs, d_attended, queries, keys, values, mixed, lse, raw, cosine, sine, q_gain, k_gain, normed, d_out)
 
 
 def joined_back(heads, runs, raw, d_queries, d_keys, d_values, cosine, sine, q_gain, k_gain, share):
@@ -1706,7 +1803,6 @@
         count, 6, d_both, w_gu, middle, cotangent[0], mlp_gain[None, :], attended, w_out
     )
     d_attended, d_down = lax.optimization_barrier((d_attended, d_down))
-    share = jnp.ones((2, HEAD), F32)
     tables = (cosine, sine, q_gain_row, k_gain_row)
     if repeat == 1:
         d_joined, q_gain_grad, k_gain_grad, parts = attention_and_joined_back(
@@ -1722,7 +1818,6 @@
             lse,
             raw,
             *tables,
-            share,
             normed,
             d_out,
         )
@@ -1735,7 +1830,7 @@
         d_keys = d_keys + across(count, 1, d_keys)
         d_values = d_values + across(count, 1, d_values)
         mine = lax.rem(lax.axis_index("ctx"), 2) == jnp.arange(2)
-        share = share * mine[:, None].astype(F32)
+        share = jnp.broadcast_to(mine[:, None].astype(F32), (2, HEAD))
         d_joined, q_gain_grad, k_gain_grad = joined_back(
             heads, run_order, raw, d_queries, d_keys, d_values, *tables, share
         )
@@ -1762,7 +1857,7 @@
         gains[3].reshape(-1),
         d_out.astype(F32),
         gains[1].reshape(-1),
-        d_gate_up.astype(F32),
+        d_gate_up,
         d_down.astype(F32),
     )
 

time: 536 us -> 535 us (level)
    unnamed x51 -> x54, local copies, waits for them, and re-layouts: 15.7 us -> 17.3 us
  transfers between devices with their start and end apart: 10 -> 10, of which waited for: 3 -> 4; matrix products, arithmetic and copies ran while one was open for 10% -> 9% of each run, Pallas kernels for 76% -> 76%
where the time goes in v6:
time: 535 us; the launch traced here: 530 us
  Pallas kernels  429 us (80%)
  matrix products  36.5 us (7%)
  local copies, waits for them, and re-layouts  22.5 us (4%)
  waiting for transfers between devices  16.5 us (3%)
  between operations  14.7 us (3%)
  starting transfers between devices  5.79 us (1%)
    pallas_call x1, Pallas kernels, back_through_middle(): pl.pallas_call(functools.partial(back_kernel, count), out_shape=[shape((r...  92.3 us
    pallas_call x1, Pallas kernels, middle_and_second(): pl.pallas_call(functools.partial(middle_kernel, count, slots), out_shape=...  83.2 us
    pallas_call x1, Pallas kernels, back_to_input(): pl.pallas_call(functools.partial(input_kernel, count), out_shape=[shape((...  58.8 us
    pallas_call x1, Pallas kernels, back_through_mlp(): pl.pallas_call(functools.partial(mlp_kernel, count, groups), out_shape=[s...  49.6 us
    pallas_call x1, Pallas kernels, opening(): pl.pallas_call(functools.partial(opening_kernel, count), out_shape=[jax.S...  43.4 us
    pallas_call x1, Pallas kernels, attention_and_joined_back(): pl.pallas_call(functools.partial(attention_and_joined_back_kernel, heads,...  33.6 us
    pallas_call x1, Pallas kernels, spread_mlp(): pl.pallas_call(functools.partial(spread_mlp_kernel, count), out_shape=jax...  21 us
    pallas_call x1, Pallas kernels, attention(): pl.pallas_call(functools.partial(attention_kernel, heads), out_shape=[sha...  20.5 us
  transfers between devices with their start and end apart: 10, of which 4 were waited for; matrix products, arithmetic and copies ran while one was open for 9% of the time, Pallas kernels for 76%

profile of v6, /device:TPU:0, one launch (start us, length us, event | category | flops | bytes accessed | tf_op | source)
XLA Modules:
  0.0 530.4 jit_solution(1968386416982872201)
XLA Ops:
  7.2 12.5 %shard_map.213 = bf16[12,64,512]{2,1,0:T(8,128)(2,1)} custom-call(bf16[64,4096]{1,0:T(8,128)(2,1)} %qkv.1, bf16[64,2048]{1,0:T(8,128)(2,1)} %out.1), custom_call_target="tpu_custom_call" | custom-call | bytes 12000000 | tf_op jit(solution)/shard_map/pallas_call | solution.py:286
  19.8 21.0 %shard_map.214 = bf16[8,64,1536]{2,1,0:T(8,128)(2,1)} custom-call(bf16[64,12288]{1,0:T(8,128)(2,1)} %weight), custom_call_target="tpu_custom_call" | custom-call | bytes 22000000 | tf_op jit(solution)/shard_map/pallas_call | solution.py:315
  43.3 43.4 %shard_map.215 = (bf16[2048,2048]{1,0:T(8,128)(2,1)}, s32[8,8,128]{2,1,0:T(8,128)}) custom-call(bf16[256,2048]{1,0:T(8,128)(2,1)} %fusion.3.normed, s32[1,8,128]{2,1,0:T(8,128)} %scatter.4.runs), custom_call_target="tpu_custom_call" | custom-call | bytes 45000000 | tf_op jit(solution)/shard_map/pallas_call | solution.py:343
  86.8 1.8 slice.57
  88.7 1.5 collective-permute-start.1
  90.2 1.5 collective-permute-start
  91.8 10.3 %fusion.4.joined = f32[2048,512]{1,0:T(8,128)} fusion(bf16[2048,2048]{1,0:T(8,128)(2,1)} %get-tuple-element.83.normed, bf16[2048,512]{1,0:T(8,128)(2,1)S(1)} %bitcast.48), kind=kOutput, calls=%fused_computation.20 | convolution fusion | flops 4294967296 | bytes 14680064 | tf_op jit(solution)/shard_map/dot_general | solution.py:1771
  104.5 1.6 collective-permute-start.3
  110.8 20.5 %shard_map.216 = (bf16[2048,256]{1,0:T(8,128)(2,1)}, f32[2048,512]{1,0:T(8,128)}, bf16[16,256,128]{2,1,0:T(8,128)(2,1)}, bf16[2048,128]{1,0:T(8,128)(2,1)}, bf16...) custom-call(s32[64]{0:T(128)} %reshape_squeeze.3.runs, f32[2048,512]{1,0:T(8,128)} %fusion.4.joined, ...), custom_call_target="tpu_custom_call" | custom-call | bytes 15000000 | tf_op jit(solution)/shard_map/pallas_call | solution.py:1323
  132.4 83.2 %shard_map.217 = (f32[256,2048]{1,0:T(8,128)}, bf16[2048,2048]{1,0:T(8,128)(2,1)}, bf16[2048,2048]{1,0:T(8,128)(2,1)}) custom-call(bf16[2048,256]{1,0:T(8,128)(2,1)} %get-tuple-element.90.left.attended_from, bf16[256,2048]{1,0:T(8,128)(2,1)} %bitcast.46, bf16[256,2048]{1,0:T(8,128)(2,1)} %bitcast.44, f32[1,2048]{1,0:T(1,128)} %bitcast.59, ...), custom_call_target="tpu_custom_call" | custom-call | bytes 80000000 | tf_op jit(solution)/shard_map/pallas_call | solution.py:841
  215.6 17.4 %fusion.5.both = f32[2048,1536]{1,0:T(8,128)S(1)} fusion(bf16[2048,2048]{1,0:T(8,128)(2,1)} %get-tuple-element.93.second, bf16[2048,1536]{1,0:T(8,128)(2,1)} %bitcast.51), kind=kOutput, calls=%fused_computation.21 | convolution fusion | flops 12884901888 | bytes 27262976 | tf_op jit(solution)/shard_map/dot_general | solution.py:1783
  233.1 2.1 fusion.activated_from
  235.2 4.3 copy-done
  239.4 2.7 copy-done.4
  242.1 8.8 %convolution_convert_fusion = bf16[768,2048]{1,0:T(8,128)(2,1)} fusion(bf16[2048,768]{1,0:T(8,128)(2,1)S(1)} %fusion.activated_from, bf16[2048,2048]{1,0:T(8,128)(2,1)S(1)} %copy-done.4), kind=kOutput, calls=%fused_computation.2 | convolution fusion | flops 6444023808 | bytes 14680064 | tf_op jit(solution)/shard_map/dot_general | solution.py:1788
  251.0 12.5 %all-gather.8.cloned.1.call-done.weight_from = bf16[768,2048]{1,0:T(8,128)(2,1)} async-done(((bf16[192,2048]{1,0:T(8,128)(2,1)}), bf16[768,2048]{1,0:T(8,128)(2,1)}) %all-gather.8.cloned.1.call-update) | async-done | bytes 3145744 | tf_op jit(solution)/shard_map/all_gather | solution.py:1740
  263.5 49.6 %shard_map.218 = (bf16[256,2048]{1,0:T(8,128)(2,1)}, bf16[2048,1536]{1,0:T(8,128)(2,1)}, bf16[4,8,64,1536]{3,2,1,0:T(8,128)(2,1)}) custom-call(bf16[2048,768]{1,0:T(8,128)(2,1)} %copy-done.2, bf16[768,2048]{1,0:T(8,128)(2,1)} %all-gather.8.cloned.1.call-done.weight_from, f32[256,2048]{1,0:T(8,128)} %get-tuple-element.95.middle_from, ...), custom_call_target="tpu_custom_call" | custom-call | bytes 48000000 | tf_op jit(solution)/shard_map/pallas_call | solution.py:1205
  313.2 92.3 %shard_map.219 = (f32[256,2048]{1,0:T(8,128)}, f32[1,2048]{1,0:T(1,128)}, bf16[2048,256]{1,0:T(8,128)(2,1)}, bf16[256,2048]{1,0:T(8,128)(2,1)}) custom-call(bf16[2048,1536]{1,0:T(8,128)(2,1)} %get-tuple-element.101.left_from, bf16[2048,1536]{1,0:T(8,128)(2,1)} %bitcast.52, f32[256,2048]{1,0:T(8,128)} %get-tuple-element.95.middle_from, ...), custom_call_target="tpu_custom_call" | custom-call | bytes 85000000 | tf_op jit(solution)/shard_map/pallas_call | solution.py:949
  405.5 33.6 %shard_map.220 = (bf16[2048,512]{1,0:T(8,128)(2,1)}, f32[1,128]{1,0:T(1,128)}, f32[1,128]{1,0:T(1,128)}, bf16[4,12,64,512]{3,2,1,0:T(8,128)(2,1)}) custom-call(s32[64]{0:T(128)} %reshape_squeeze.3.runs, bf16[2048,256]{1,0:T(8,128)(2,1)} %get-tuple-element.104.d_attended, bf16[16,256,128]{2,1,0:T(8,128)(2,1)} %get-tuple-element.105.queries, ...), custom_call_target="tpu_custom_call" | custom-call | bytes 30000000 | tf_op jit(solution)/shard_map/pallas_call | solution.py:1653
  440.5 58.8 %shard_map.221 = (f32[256,2048]{1,0:T(8,128)}, f32[1,2048]{1,0:T(1,128)}, f32[64,12288]{1,0:T(8,128)}) custom-call(bf16[2048,512]{1,0:T(8,128)(2,1)} %get-tuple-element.115.left_from, bf16[2048,512]{1,0:T(8,128)(2,1)} %bitcast.49, bf16[256,2048]{1,0:T(8,128)(2,1)} %bitcast.45, f32[256,2048]{1,0:T(8,128)} %get-tuple-element.116.d_middle_from, ...), custom_call_target="tpu_custom_call" | custom-call | bytes 60000000 | tf_op jit(solution)/shard_map/pallas_call | solution.py:1042
  499.4 1.7 reduce-scatter.8.cloned.1.call-done.parts
  501.1 14.2 %shard_map.222 = (f32[16,128]{1,0:T(8,128)}, f32[16,128]{1,0:T(8,128)}, f32[1,128]{1,0:T(1,128)}, f32[1,128]{1,0:T(1,128)}, f32[64,4096]{1,0:T(8,128)}, /*index=5*/f32[64,2048]{1,0:T(8,128)}) custom-call(f32[1,2048]{1,0:T(1,128)} %get-tuple-element.121.attn_part, f32[1,2048]{1,0:T(1,128)} %get-tuple-element.122.mlp_part, ...), custom_call_target="tpu_custom_call" | custom-call | bytes 14000000 | tf_op jit(solution)/shard_map/pallas_call | solution.py:503
  516.4 1.3 copy.36
  521.7 1.7 copy.43
  (85 shorter events, 17.2 us)
Async XLA Ops:
  7.2 33.6 %copy-start.1 = (bf16[1,256,2048]{2,1,0:T(8,128)(2,1)S(1)}, bf16[1,256,2048]{2,1,0:T(8,128)(2,1)}, u32[]{:S(2)}) copy-start(bf16[1,256,2048]{2,1,0:T(8,128)(2,1)} %param.16) | copy-start | bytes 3145732
  7.2 33.9 %copy-start.15 = (f32[2048]{0:T(1024)S(1)}, f32[2048]{0:T(1024)}, u32[]{:S(2)}) copy-start(f32[2048]{0:T(1024)} %param.19) | copy-start | bytes 24580
  7.2 79.6 %all-gather.4.cloned.1.call-start = ((), (), s32[]{:S(2)}) async-start(), calls=%async_computation.3 | async-start | bytes 3932160 | tf_op jit(solution)/shard_map/all_gather | solution.py:1740
  19.7 22.8 %copy-start.18 = (s32[1,256]{1,0:T(1,128)S(1)}, s32[1,256]{1,0:T(1,128)}, u32[]{:S(2)}) copy-start(s32[1,256]{1,0:T(1,128)} %param.17) | copy-start | bytes 3076
  19.7 22.9 %copy-start.19 = (s32[1,256]{1,0:T(1,128)S(1)}, s32[1,256]{1,0:T(1,128)}, u32[]{:S(2)}) copy-start(s32[1,256]{1,0:T(1,128)} %param.18) | copy-start | bytes 3076
  19.8 195.8 %all-gather.6.cloned.1.call-start = ((), (), s32[]{:S(2)}) async-start(), calls=%async_computation.4 | async-start | bytes 7864320 | tf_op jit(solution)/shard_map/all_gather | solution.py:1740
  41.1 47.5 %copy-start.5 = (bf16[1,256,2048]{2,1,0:T(8,128)(2,1)S(1)}, bf16[1,256,2048]{2,1,0:T(8,128)(2,1)}, u32[]{:S(2)}) copy-start(bf16[1,256,2048]{2,1,0:T(8,128)(2,1)} %param.27) | copy-start | bytes 3145732
  42.5 221.0 %all-gather.8.cloned.1.call-start = ((), (), s32[]{:S(2)}) async-start(), calls=%async_computation.5 | async-start | bytes 3932160 | tf_op jit(solution)/shard_map/all_gather | solution.py:1740
  88.6 13.5 %copy-start.3 = (bf16[8,256,512]{2,1,0:T(8,128)(2,1)}, bf16[8,256,512]{2,1,0:T(8,128)(2,1)S(1)}, u32[]{:S(2)}) copy-start(bf16[8,256,512]{2,1,0:T(8,128)(2,1)S(1)} %slice.57) | copy-start | bytes 6291460
  88.7 14.3 %collective-permute-start.1 = (bf16[1,128,2048]{2,1,0:T(8,128)(2,1)S(1)}, bf16[1,128,2048]{2,1,0:T(8,128)(2,1)S(1)}, u32[]{:S(2)}, u32[]{:S(2)}) collective-permute-start(bf16[1,128,2048]{2,1,0:T(8,128)(2,1)S(1)} %get-tuple-element.134), channel_id=1, source_target_pairs={{0,16},{4,20},{8,24},{12,28},{16,0},{20,4},{24,8},{28,12},{1,17},{... | collective-permute-start | bytes 1572872 | tf_op jit(solution)/shard_map/ppermute | solution.py:358
  90.2 14.0 %collective-permute-start = (bf16[1,128,2048]{2,1,0:T(8,128)(2,1)S(1)}, bf16[1,128,2048]{2,1,0:T(8,128)(2,1)S(1)}, u32[]{:S(2)}, u32[]{:S(2)}) collective-permute-start(bf16[1,128,2048]{2,1,0:T(8,128)(2,1)S(1)} %get-tuple-element.135), channel_id=1, source_target_pairs={{0,8},{4,12},{8,0},{12,4},{16,24},{20,28},{24,16},{28,20},{1,9},{5... | collective-permute-start | bytes 1572872 | tf_op jit(solution)/shard_map/ppermute | solution.py:358
  104.3 27.0 %copy-start.6 = (bf16[2,128,2048]{2,1,0:T(8,128)(2,1)}, bf16[2,128,2048]{2,1,0:T(8,128)(2,1)S(1)}, u32[]{:S(2)}) copy-start(bf16[2,128,2048]{2,1,0:T(8,128)(2,1)S(1)} %pad_maximum_fusion.refs_0_) | copy-start | bytes 3145732
  104.4 26.9 %copy-start.7 = (bf16[2,128,2048]{2,1,0:T(8,128)(2,1)}, bf16[2,128,2048]{2,1,0:T(8,128)(2,1)S(1)}, u32[]{:S(2)}) copy-start(bf16[2,128,2048]{2,1,0:T(8,128)(2,1)S(1)} %pad_maximum_fusion.1.refs_2_) | copy-start | bytes 3145732
  104.5 26.9 %collective-permute-start.3 = (bf16[2,128,2048]{2,1,0:T(8,128)(2,1)S(1)}, bf16[2,128,2048]{2,1,0:T(8,128)(2,1)S(1)}, u32[]{:S(2)}, u32[]{:S(2)}) collective-permute-start(bf16[2,128,2048]{2,1,0:T(8,128)(2,1)S(1)} %pad_maximum_fusion.1.refs_2_), channel_id=1, source_target_pairs={{0,8},{4,12},{8,0},{12,4},{16,24},{20,28},{24,16},{28,20},{1,9},{5... | collective-permute-start | bytes 3145736 | tf_op jit(solution)/shard_map/ppermute | solution.py:358
  106.1 25.3 %collective-permute-start.2 = (bf16[2,128,2048]{2,1,0:T(8,128)(2,1)S(1)}, bf16[2,128,2048]{2,1,0:T(8,128)(2,1)}, u32[]{:S(2)}, u32[]{:S(2)}) collective-permute-start(bf16[2,128,2048]{2,1,0:T(8,128)(2,1)S(1)} %pad_maximum_fusion.refs_0_), channel_id=1, source_target_pairs={{0,16},{4,20},{8,24},{12,28},{16,0},{20,4},{24,8},{28,12},{1,17},{... | collective-permute-start | bytes 3145736 | tf_op jit(solution)/shard_map/ppermute | solution.py:358
  106.7 298.8 %reduce-scatter.4.cloned.1.call-start = ((), (), s32[]{:S(2)}) async-start(), calls=%async_computation.6 | async-start | bytes 3932160 | tf_op jit(solution)/shard_map/reduce_scatter | solution.py:1743
  233.0 6.4 %copy-start = (f32[2048,1536]{1,0:T(8,128)}, f32[2048,1536]{1,0:T(8,128)S(1)}, u32[]{:S(2)}) copy-start(f32[2048,1536]{1,0:T(8,128)S(1)} %fusion.5.both) | copy-start | bytes 37748740
  233.1 9.1 %copy-start.4 = (bf16[2048,2048]{1,0:T(8,128)(2,1)S(1)}, bf16[2048,2048]{1,0:T(8,128)(2,1)}, u32[]{:S(2)}) copy-start(bf16[2048,2048]{1,0:T(8,128)(2,1)} %get-tuple-element.97.upstream) | copy-start | bytes 25165828
  239.4 11.5 %copy-start.2 = (bf16[2048,768]{1,0:T(8,128)(2,1)}, bf16[2048,768]{1,0:T(8,128)(2,1)S(1)}, u32[]{:S(2)}) copy-start(bf16[2048,768]{1,0:T(8,128)(2,1)S(1)} %fusion.activated_from) | copy-start | bytes 9437188
  250.9 188.2 %reduce-scatter.6.cloned.1.call-start = ((), (), s32[]{:S(2)}) async-start(), calls=%async_computation.7 | async-start | bytes 7864320 | tf_op jit(solution)/shard_map/reduce_scatter | solution.py:1743
  313.2 187.9 %reduce-scatter.8.cloned.1.call-start = ((), (), s32[]{:S(2)}) async-start(), calls=%async_computation.8 | async-start | bytes 3932160 | tf_op jit(solution)/shard_map/reduce_scatter | solution.py:1743
  405.5 33.7 %copy-start.13 = (bf16[192,2048]{1,0:T(8,128)(2,1)S(1)}, bf16[192,2048]{1,0:T(8,128)(2,1)}, u32[]{:S(2)}) copy-start(bf16[192,2048]{1,0:T(8,128)(2,1)} %reduce-scatter.4.cloned.1.call-done) | copy-start | bytes 2359300
  440.5 74.8 %copy-start.10 = (bf16[256,2048]{1,0:T(8,128)(2,1)S(1)}, bf16[256,2048]{1,0:T(8,128)(2,1)}, u32[]{:S(2)}) copy-start(bf16[256,2048]{1,0:T(8,128)(2,1)} %get-tuple-element.98) | copy-start | bytes 3145732
  499.3 17.0 %copy-start.9 = (f32[256,2048]{1,0:T(8,128)S(1)}, f32[256,2048]{1,0:T(8,128)}, u32[]{:S(2)}) copy-start(f32[256,2048]{1,0:T(8,128)} %get-tuple-element.120) | copy-start | bytes 6291460
  (8 other events, 29.6 us)
Sparse Core Ops, SparseCore 0:
  19.9 64.6 all-gather.3
  86.1 114.0 all-gather.5
  201.8 61.6 all-gather.7
  265.6 58.8 reduce-scatter.3
  326.7 110.7 reduce-scatter.5
  440.3 60.7 reduce-scatter.7

commit v7 on v6

--- a/solution.py
+++ b/solution.py
@@ -436,7 +436,6 @@
     me = lax.axis_index("ctx")
     group = lax.axis_index("fsdp")
     others = [lax.rem(group + step, groups) for step in range(1, groups)]
-    greet(everyone(count, me, group) + [(me, other) for other in others])
     fetched = fetch([parts.at[pl.ds(count, out_parts.shape[0])]], [out_parts], out_in)
     rows = attn_gain.shape[0]
     for row in range(rows):
@@ -445,6 +444,10 @@
     values[2 * rows : 2 * rows + 1] = q_part[...]
     values[2 * rows + 1 : 2 * rows + 2] = k_part[...]
     values[2 * rows + 2 :] = jnp.zeros((6, 128), F32)
+    near[me] = values[...]
+    greet(everyone(count, me, group) + [(me, other) for other in others])
+    start, finish = trade(count, me, group, incoming, parts, columns, part_send, part_recv)
+    start(all_slots(count))
     copies = []
     for slot in range(1, count):
         item = pltpu.make_async_remote_copy(
@@ -457,9 +460,6 @@
         )
         item.start()
         copies.append(item)
-    start, finish = trade(count, me, group, incoming, parts, columns, part_send, part_recv)
-    start(all_slots(count))
-    near[me] = values[...]
     for item in copies:
         item.wait()
     summed = near[0]

time: 535 us -> 540 us (level)
  transfers between devices with their start and end apart: 10 -> 10, of which waited for: 4 -> 4; matrix products, arithmetic and copies ran while one was open for 9% -> 9% of each run, Pallas kernels for 76% -> 75%
where the time goes in v7:
time: 540 us; the launch traced here: 535 us
  Pallas kernels  434 us (80%)
  matrix products  36.5 us (7%)
  local copies, waits for them, and re-layouts  22.5 us (4%)
  waiting for transfers between devices  16.5 us (3%)
  between operations  14.7 us (3%)
  starting transfers between devices  5.79 us (1%)
    pallas_call x1, Pallas kernels, back_through_middle(): pl.pallas_call(functools.partial(back_kernel, count), out_shape=[shape((r...  92.3 us
    pallas_call x1, Pallas kernels, middle_and_second(): pl.pallas_call(functools.partial(middle_kernel, count, slots), out_shape=...  83.2 us
    pallas_call x1, Pallas kernels, back_to_input(): pl.pallas_call(functools.partial(input_kernel, count), out_shape=[shape((...  58.8 us
    pallas_call x1, Pallas kernels, back_through_mlp(): pl.pallas_call(functools.partial(mlp_kernel, count, groups), out_shape=[s...  49.6 us
    pallas_call x1, Pallas kernels, opening(): pl.pallas_call(functools.partial(opening_kernel, count), out_shape=[jax.S...  43.4 us
    pallas_call x1, Pallas kernels, attention_and_joined_back(): pl.pallas_call(functools.partial(attention_and_joined_back_kernel, heads,...  33.6 us
    pallas_call x1, Pallas kernels, spread_mlp(): pl.pallas_call(functools.partial(spread_mlp_kernel, count), out_shape=jax...  21 us
    pallas_call x1, Pallas kernels, attention(): pl.pallas_call(functools.partial(attention_kernel, heads), out_shape=[sha...  20.5 us
  transfers between devices with their start and end apart: 10, of which 4 were waited for; matrix products, arithmetic and copies ran while one was open for 9% of the time, Pallas kernels for 75%

profile of v7, /device:TPU:0, one launch (start us, length us, event | category | flops | bytes accessed | tf_op | source)
XLA Modules:
  0.0 535.0 jit_solution(13107905054196200754)
XLA Ops:
  7.2 12.5 %shard_map.213 = bf16[12,64,512]{2,1,0:T(8,128)(2,1)} custom-call(bf16[64,4096]{1,0:T(8,128)(2,1)} %qkv.1, bf16[64,2048]{1,0:T(8,128)(2,1)} %out.1), custom_call_target="tpu_custom_call" | custom-call | bytes 12000000 | tf_op jit(solution)/shard_map/pallas_call | solution.py:286
  19.8 21.0 %shard_map.214 = bf16[8,64,1536]{2,1,0:T(8,128)(2,1)} custom-call(bf16[64,12288]{1,0:T(8,128)(2,1)} %weight), custom_call_target="tpu_custom_call" | custom-call | bytes 22000000 | tf_op jit(solution)/shard_map/pallas_call | solution.py:315
  43.3 43.4 %shard_map.215 = (bf16[2048,2048]{1,0:T(8,128)(2,1)}, s32[8,8,128]{2,1,0:T(8,128)}) custom-call(bf16[256,2048]{1,0:T(8,128)(2,1)} %fusion.3.normed, s32[1,8,128]{2,1,0:T(8,128)} %scatter.4.runs), custom_call_target="tpu_custom_call" | custom-call | bytes 45000000 | tf_op jit(solution)/shard_map/pallas_call | solution.py:343
  86.8 1.8 slice.57
  88.7 1.5 collective-permute-start.1
  90.2 1.5 collective-permute-start
  91.8 10.3 %fusion.4.joined = f32[2048,512]{1,0:T(8,128)} fusion(bf16[2048,2048]{1,0:T(8,128)(2,1)} %get-tuple-element.83.normed, bf16[2048,512]{1,0:T(8,128)(2,1)S(1)} %bitcast.48), kind=kOutput, calls=%fused_computation.20 | convolution fusion | flops 4294967296 | bytes 14680064 | tf_op jit(solution)/shard_map/dot_general | solution.py:1771
  104.5 1.6 collective-permute-start.3
  110.8 20.5 %shard_map.216 = (bf16[2048,256]{1,0:T(8,128)(2,1)}, f32[2048,512]{1,0:T(8,128)}, bf16[16,256,128]{2,1,0:T(8,128)(2,1)}, bf16[2048,128]{1,0:T(8,128)(2,1)}, bf16...) custom-call(s32[64]{0:T(128)} %reshape_squeeze.3.runs, f32[2048,512]{1,0:T(8,128)} %fusion.4.joined, ...), custom_call_target="tpu_custom_call" | custom-call | bytes 15000000 | tf_op jit(solution)/shard_map/pallas_call | solution.py:1323
  132.4 83.2 %shard_map.217 = (f32[256,2048]{1,0:T(8,128)}, bf16[2048,2048]{1,0:T(8,128)(2,1)}, bf16[2048,2048]{1,0:T(8,128)(2,1)}) custom-call(bf16[2048,256]{1,0:T(8,128)(2,1)} %get-tuple-element.90.left.attended_from, bf16[256,2048]{1,0:T(8,128)(2,1)} %bitcast.46, bf16[256,2048]{1,0:T(8,128)(2,1)} %bitcast.44, f32[1,2048]{1,0:T(1,128)} %bitcast.59, ...), custom_call_target="tpu_custom_call" | custom-call | bytes 80000000 | tf_op jit(solution)/shard_map/pallas_call | solution.py:841
  215.6 17.4 %fusion.5.both = f32[2048,1536]{1,0:T(8,128)S(1)} fusion(bf16[2048,2048]{1,0:T(8,128)(2,1)} %get-tuple-element.93.second, bf16[2048,1536]{1,0:T(8,128)(2,1)} %bitcast.51), kind=kOutput, calls=%fused_computation.21 | convolution fusion | flops 12884901888 | bytes 27262976 | tf_op jit(solution)/shard_map/dot_general | solution.py:1783
  233.1 2.1 fusion.activated_from
  235.2 4.3 copy-done
  239.4 2.7 copy-done.4
  242.1 8.8 %convolution_convert_fusion = bf16[768,2048]{1,0:T(8,128)(2,1)} fusion(bf16[2048,768]{1,0:T(8,128)(2,1)S(1)} %fusion.activated_from, bf16[2048,2048]{1,0:T(8,128)(2,1)S(1)} %copy-done.4), kind=kOutput, calls=%fused_computation.2 | convolution fusion | flops 6444023808 | bytes 14680064 | tf_op jit(solution)/shard_map/dot_general | solution.py:1788
  251.0 12.5 %all-gather.8.cloned.1.call-done.weight_from = bf16[768,2048]{1,0:T(8,128)(2,1)} async-done(((bf16[192,2048]{1,0:T(8,128)(2,1)}), bf16[768,2048]{1,0:T(8,128)(2,1)}) %all-gather.8.cloned.1.call-update) | async-done | bytes 3145744 | tf_op jit(solution)/shard_map/all_gather | solution.py:1740
  263.5 49.6 %shard_map.218 = (bf16[256,2048]{1,0:T(8,128)(2,1)}, bf16[2048,1536]{1,0:T(8,128)(2,1)}, bf16[4,8,64,1536]{3,2,1,0:T(8,128)(2,1)}) custom-call(bf16[2048,768]{1,0:T(8,128)(2,1)} %copy-done.2, bf16[768,2048]{1,0:T(8,128)(2,1)} %all-gather.8.cloned.1.call-done.weight_from, f32[256,2048]{1,0:T(8,128)} %get-tuple-element.95.middle_from, ...), custom_call_target="tpu_custom_call" | custom-call | bytes 48000000 | tf_op jit(solution)/shard_map/pallas_call | solution.py:1205
  313.2 92.3 %shard_map.219 = (f32[256,2048]{1,0:T(8,128)}, f32[1,2048]{1,0:T(1,128)}, bf16[2048,256]{1,0:T(8,128)(2,1)}, bf16[256,2048]{1,0:T(8,128)(2,1)}) custom-call(bf16[2048,1536]{1,0:T(8,128)(2,1)} %get-tuple-element.101.left_from, bf16[2048,1536]{1,0:T(8,128)(2,1)} %bitcast.52, f32[256,2048]{1,0:T(8,128)} %get-tuple-element.95.middle_from, ...), custom_call_target="tpu_custom_call" | custom-call | bytes 85000000 | tf_op jit(solution)/shard_map/pallas_call | solution.py:949
  405.5 33.6 %shard_map.220 = (bf16[2048,512]{1,0:T(8,128)(2,1)}, f32[1,128]{1,0:T(1,128)}, f32[1,128]{1,0:T(1,128)}, bf16[4,12,64,512]{3,2,1,0:T(8,128)(2,1)}) custom-call(s32[64]{0:T(128)} %reshape_squeeze.3.runs, bf16[2048,256]{1,0:T(8,128)(2,1)} %get-tuple-element.104.d_attended, bf16[16,256,128]{2,1,0:T(8,128)(2,1)} %get-tuple-element.105.queries, ...), custom_call_target="tpu_custom_call" | custom-call | bytes 30000000 | tf_op jit(solution)/shard_map/pallas_call | solution.py:1653
  440.5 58.8 %shard_map.221 = (f32[256,2048]{1,0:T(8,128)}, f32[1,2048]{1,0:T(1,128)}, f32[64,12288]{1,0:T(8,128)}) custom-call(bf16[2048,512]{1,0:T(8,128)(2,1)} %get-tuple-element.115.left_from, bf16[2048,512]{1,0:T(8,128)(2,1)} %bitcast.49, bf16[256,2048]{1,0:T(8,128)(2,1)} %bitcast.45, f32[256,2048]{1,0:T(8,128)} %get-tuple-element.116.d_middle_from, ...), custom_call_target="tpu_custom_call" | custom-call | bytes 60000000 | tf_op jit(solution)/shard_map/pallas_call | solution.py:1042
  499.4 1.7 reduce-scatter.8.cloned.1.call-done.parts
  501.1 18.8 %shard_map.222 = (f32[16,128]{1,0:T(8,128)}, f32[16,128]{1,0:T(8,128)}, f32[1,128]{1,0:T(1,128)}, f32[1,128]{1,0:T(1,128)}, f32[64,4096]{1,0:T(8,128)}, /*index=5*/f32[64,2048]{1,0:T(8,128)}) custom-call(f32[1,2048]{1,0:T(1,128)} %get-tuple-element.121.attn_part, f32[1,2048]{1,0:T(1,128)} %get-tuple-element.122.mlp_part, ...), custom_call_target="tpu_custom_call" | custom-call | bytes 14000000 | tf_op jit(solution)/shard_map/pallas_call | solution.py:503
  520.9 1.3 copy.36
  526.2 1.7 copy.43
  (85 shorter events, 17.2 us)
Async XLA Ops:
  7.2 33.6 %copy-start.1 = (bf16[1,256,2048]{2,1,0:T(8,128)(2,1)S(1)}, bf16[1,256,2048]{2,1,0:T(8,128)(2,1)}, u32[]{:S(2)}) copy-start(bf16[1,256,2048]{2,1,0:T(8,128)(2,1)} %param.16) | copy-start | bytes 3145732
  7.2 33.9 %copy-start.15 = (f32[2048]{0:T(1024)S(1)}, f32[2048]{0:T(1024)}, u32[]{:S(2)}) copy-start(f32[2048]{0:T(1024)} %param.19) | copy-start | bytes 24580
  7.2 79.6 %all-gather.4.cloned.1.call-start = ((), (), s32[]{:S(2)}) async-start(), calls=%async_computation.3 | async-start | bytes 3932160 | tf_op jit(solution)/shard_map/all_gather | solution.py:1740
  19.7 22.8 %copy-start.18 = (s32[1,256]{1,0:T(1,128)S(1)}, s32[1,256]{1,0:T(1,128)}, u32[]{:S(2)}) copy-start(s32[1,256]{1,0:T(1,128)} %param.17) | copy-start | bytes 3076
  19.7 22.9 %copy-start.19 = (s32[1,256]{1,0:T(1,128)S(1)}, s32[1,256]{1,0:T(1,128)}, u32[]{:S(2)}) copy-start(s32[1,256]{1,0:T(1,128)} %param.18) | copy-start | bytes 3076
  19.8 195.8 %all-gather.6.cloned.1.call-start = ((), (), s32[]{:S(2)}) async-start(), calls=%async_computation.4 | async-start | bytes 7864320 | tf_op jit(solution)/shard_map/all_gather | solution.py:1740
  41.1 47.5 %copy-start.5 = (bf16[1,256,2048]{2,1,0:T(8,128)(2,1)S(1)}, bf16[1,256,2048]{2,1,0:T(8,128)(2,1)}, u32[]{:S(2)}) copy-start(bf16[1,256,2048]{2,1,0:T(8,128)(2,1)} %param.27) | copy-start | bytes 3145732
  42.5 221.0 %all-gather.8.cloned.1.call-start = ((), (), s32[]{:S(2)}) async-start(), calls=%async_computation.5 | async-start | bytes 3932160 | tf_op jit(solution)/shard_map/all_gather | solution.py:1740
  88.6 13.5 %copy-start.3 = (bf16[8,256,512]{2,1,0:T(8,128)(2,1)}, bf16[8,256,512]{2,1,0:T(8,128)(2,1)S(1)}, u32[]{:S(2)}) copy-start(bf16[8,256,512]{2,1,0:T(8,128)(2,1)S(1)} %slice.57) | copy-start | bytes 6291460
  88.7 14.3 %collective-permute-start.1 = (bf16[1,128,2048]{2,1,0:T(8,128)(2,1)S(1)}, bf16[1,128,2048]{2,1,0:T(8,128)(2,1)S(1)}, u32[]{:S(2)}, u32[]{:S(2)}) collective-permute-start(bf16[1,128,2048]{2,1,0:T(8,128)(2,1)S(1)} %get-tuple-element.134), channel_id=1, source_target_pairs={{0,16},{4,20},{8,24},{12,28},{16,0},{20,4},{24,8},{28,12},{1,17},{... | collective-permute-start | bytes 1572872 | tf_op jit(solution)/shard_map/ppermute | solution.py:358
  90.2 14.0 %collective-permute-start = (bf16[1,128,2048]{2,1,0:T(8,128)(2,1)S(1)}, bf16[1,128,2048]{2,1,0:T(8,128)(2,1)S(1)}, u32[]{:S(2)}, u32[]{:S(2)}) collective-permute-start(bf16[1,128,2048]{2,1,0:T(8,128)(2,1)S(1)} %get-tuple-element.135), channel_id=1, source_target_pairs={{0,8},{4,12},{8,0},{12,4},{16,24},{20,28},{24,16},{28,20},{1,9},{5... | collective-permute-start | bytes 1572872 | tf_op jit(solution)/shard_map/ppermute | solution.py:358
  104.3 27.0 %copy-start.6 = (bf16[2,128,2048]{2,1,0:T(8,128)(2,1)}, bf16[2,128,2048]{2,1,0:T(8,128)(2,1)S(1)}, u32[]{:S(2)}) copy-start(bf16[2,128,2048]{2,1,0:T(8,128)(2,1)S(1)} %pad_maximum_fusion.refs_0_) | copy-start | bytes 3145732
  104.4 26.9 %copy-start.7 = (bf16[2,128,2048]{2,1,0:T(8,128)(2,1)}, bf16[2,128,2048]{2,1,0:T(8,128)(2,1)S(1)}, u32[]{:S(2)}) copy-start(bf16[2,128,2048]{2,1,0:T(8,128)(2,1)S(1)} %pad_maximum_fusion.1.refs_2_) | copy-start | bytes 3145732
  104.5 26.9 %collective-permute-start.3 = (bf16[2,128,2048]{2,1,0:T(8,128)(2,1)S(1)}, bf16[2,128,2048]{2,1,0:T(8,128)(2,1)S(1)}, u32[]{:S(2)}, u32[]{:S(2)}) collective-permute-start(bf16[2,128,2048]{2,1,0:T(8,128)(2,1)S(1)} %pad_maximum_fusion.1.refs_2_), channel_id=1, source_target_pairs={{0,8},{4,12},{8,0},{12,4},{16,24},{20,28},{24,16},{28,20},{1,9},{5... | collective-permute-start | bytes 3145736 | tf_op jit(solution)/shard_map/ppermute | solution.py:358
  106.1 25.3 %collective-permute-start.2 = (bf16[2,128,2048]{2,1,0:T(8,128)(2,1)S(1)}, bf16[2,128,2048]{2,1,0:T(8,128)(2,1)}, u32[]{:S(2)}, u32[]{:S(2)}) collective-permute-start(bf16[2,128,2048]{2,1,0:T(8,128)(2,1)S(1)} %pad_maximum_fusion.refs_0_), channel_id=1, source_target_pairs={{0,16},{4,20},{8,24},{12,28},{16,0},{20,4},{24,8},{28,12},{1,17},{... | collective-permute-start | bytes 3145736 | tf_op jit(solution)/shard_map/ppermute | solution.py:358
  106.7 298.8 %reduce-scatter.4.cloned.1.call-start = ((), (), s32[]{:S(2)}) async-start(), calls=%async_computation.6 | async-start | bytes 3932160 | tf_op jit(solution)/shard_map/reduce_scatter | solution.py:1743
  233.0 6.4 %copy-start = (f32[2048,1536]{1,0:T(8,128)}, f32[2048,1536]{1,0:T(8,128)S(1)}, u32[]{:S(2)}) copy-start(f32[2048,1536]{1,0:T(8,128)S(1)} %fusion.5.both) | copy-start | bytes 37748740
  233.1 9.1 %copy-start.4 = (bf16[2048,2048]{1,0:T(8,128)(2,1)S(1)}, bf16[2048,2048]{1,0:T(8,128)(2,1)}, u32[]{:S(2)}) copy-start(bf16[2048,2048]{1,0:T(8,128)(2,1)} %get-tuple-element.97.upstream) | copy-start | bytes 25165828
  239.4 11.5 %copy-start.2 = (bf16[2048,768]{1,0:T(8,128)(2,1)}, bf16[2048,768]{1,0:T(8,128)(2,1)S(1)}, u32[]{:S(2)}) copy-start(bf16[2048,768]{1,0:T(8,128)(2,1)S(1)} %fusion.activated_from) | copy-start | bytes 9437188
  250.9 188.2 %reduce-scatter.6.cloned.1.call-start = ((), (), s32[]{:S(2)}) async-start(), calls=%async_computation.7 | async-start | bytes 7864320 | tf_op jit(solution)/shard_map/reduce_scatter | solution.py:1743
  313.2 187.9 %reduce-scatter.8.cloned.1.call-start = ((), (), s32[]{:S(2)}) async-start(), calls=%async_computation.8 | async-start | bytes 3932160 | tf_op jit(solution)/shard_map/reduce_scatter | solution.py:1743
  405.5 33.7 %copy-start.13 = (bf16[192,2048]{1,0:T(8,128)(2,1)S(1)}, bf16[192,2048]{1,0:T(8,128)(2,1)}, u32[]{:S(2)}) copy-start(bf16[192,2048]{1,0:T(8,128)(2,1)} %reduce-scatter.4.cloned.1.call-done) | copy-start | bytes 2359300
  440.5 79.4 %copy-start.10 = (bf16[256,2048]{1,0:T(8,128)(2,1)S(1)}, bf16[256,2048]{1,0:T(8,128)(2,1)}, u32[]{:S(2)}) copy-start(bf16[256,2048]{1,0:T(8,128)(2,1)} %get-tuple-element.98) | copy-start | bytes 3145732
  499.3 21.6 %copy-start.9 = (f32[256,2048]{1,0:T(8,128)S(1)}, f32[256,2048]{1,0:T(8,128)}, u32[]{:S(2)}) copy-start(f32[256,2048]{1,0:T(8,128)} %get-tuple-element.120) | copy-start | bytes 6291460
  (8 other events, 29.6 us)
Sparse Core Ops, SparseCore 0:
  19.9 64.6 all-gather.3
  86.1 114.0 all-gather.5
  201.8 61.6 all-gather.7
  265.6 58.8 reduce-scatter.3
  326.7 110.7 reduce-scatter.5
  440.3 60.7 reduce-scatter.7
